TPU v7x, 128 devices: a whole 4x4x4 slice. The times are simulated.
128 devices in a mesh: section: 2 (over core), ctx: 16 (over y, x), wsh: 4 (over z).
Axes of the slice: x: 4, y: 4, z: 4, core: 2. Of those that a mesh axis runs over, the one named last changes fastest.
Arguments:
- tokens: float32 [2, 4, 2048, 960], P(None, 'wsh', 'ctx'), may hold values from -6 to 6
- cotangent: float32 [2, 4, 2048, 960], P(None, 'wsh', 'ctx'), may hold values from -6 to 6
- block_order: int32 [32], replicated, may hold values from 0 to 31, as said below
- norm_one: bfloat16 [2, 960], P('section', 'wsh'), may hold values from 0.5 to 1.5
- w_query: bfloat16 [2, 960, 960], P('section', 'wsh'), may hold values from -0.1875 to 0.1875
- w_key: bfloat16 [2, 960, 320], P('section', 'wsh'), may hold values from -0.1875 to 0.1875
- w_value: bfloat16 [2, 960, 320], P('section', 'wsh'), may hold values from -0.1875 to 0.1875
- w_out: bfloat16 [2, 960, 960], P('section', 'wsh'), may hold values from -1.5 to 1.5
- norm_two: bfloat16 [2, 960], P('section', 'wsh'), may hold values from 0.5 to 1.5
- w_gate: bfloat16 [2, 960, 2560], P('section', 'wsh'), may hold values from -0.1875 to 0.1875
- w_up: bfloat16 [2, 960, 2560], P('section', 'wsh'), may hold values from -0.1875 to 0.1875
- w_down: bfloat16 [2, 2560, 960], P('section', 'wsh'), may hold values from -0.125 to 0.125
Outputs:
- section_outputs: float32 [2, 2, 4, 2048, 960], P('section', None, 'wsh', 'ctx')
- input_grads: float32 [2, 2, 4, 2048, 960], P('section', None, 'wsh', 'ctx')
- grad_norm_one: float32 [2, 960], P('section', ('ctx', 'wsh'))
- grad_query: float32 [2, 960, 960], P('section', ('ctx', 'wsh'))
- grad_key: float32 [2, 960, 320], P('section', ('ctx', 'wsh'))
- grad_value: float32 [2, 960, 320], P('section', ('ctx', 'wsh'))
- grad_out: float32 [2, 960, 960], P('section', ('ctx', 'wsh'))
- grad_norm_two: float32 [2, 960], P('section', ('ctx', 'wsh'))
- grad_gate: float32 [2, 960, 2560], P('section', ('ctx', 'wsh'))
- grad_up: float32 [2, 960, 2560], P('section', ('ctx', 'wsh'))
- grad_down: float32 [2, 2560, 960], P('section', ('ctx', 'wsh'))
Inputs may be any that keep to these rules, and one draw needn't show every extreme that they name: block_order is a permutation of the 32 blocks of a sequence, and entries 2 r and 2 r + 1 sum to 31.
All inputs are finite; a program needn't handle non-finite values.
Results may differ from a plain program's by a relative error of at most 0.028.
Values may be sent and summed in bfloat16 or wider, within the bound.
No kernel may reach another device: no remote copies, remote signals or barrier semaphores. Data moves between devices by JAX's collectives and lax.ppermute only.
A program may use at most 256 MiB of HBM per device.

v0:
```python
import math

import jax
import jax.numpy as jnp
from jax import lax
from jax.sharding import PartitionSpec as P

HEADS = 15
KV_HEADS = 5
HEAD = 64


EPS = 1e-05
ROPE_BASE = 10000.0


def passed_along(value, axis, steps):
    count = lax.axis_size(axis)
    initial, last = (max(0, -steps), min(count, count - steps))
    return lax.ppermute(value, axis, [(source, source + steps) for source in range(initial, last)])


def norm_gain(source, gain_vec):
    return source * lax.rsqrt(jnp.mean(source * source, axis=-1, keepdims=True) + EPS) * gain_vec


def silu_product(gate, up_proj):
    return jax.nn.silu(gate) * up_proj


def angles(positions, head_size):
    half_size = head_size // 2
    frequency = jnp.exp(
        jnp.arange(half_size).astype(jnp.float32) * (-2.0 * math.log(ROPE_BASE) / head_size)
    )
    return positions.astype(jnp.float32)[:, None] * frequency[None, :]


def rotate(source, cosine, sine):
    half_size = source.shape[-1] // 2
    first_half = source[..., :half_size]
    second_half = source[..., half_size:]
    return jnp.concatenate(
        [first_half * cosine - second_half * sine, second_half * cosine + first_half * sine],
        axis=-1,
    )


def product(left, right):
    return jnp.dot(left, right, preferred_element_type=jnp.float32)


def product_back(left, right):
    return jnp.einsum("re,de->rd", left, right, preferred_element_type=jnp.float32)


def outer_sum(left, right):
    left_rows = left.reshape(-1, left.shape[-1])
    right_rows = right.reshape(-1, right.shape[-1])
    return jnp.einsum("rd,re->de", left_rows, right_rows, preferred_element_type=jnp.float32)


def weight_terms(saved, parts):
    (
        gain_one_part,
        gain_two_part,
        d_query,
        d_key,
        d_value,
        d_resid_low,
        d_gate_low,
        d_up_low,
        grad_low,
    ) = parts
    return (
        jnp.sum(gain_one_part, axis=0),
        outer_sum(saved["normed"], d_query),
        outer_sum(saved["normed"], d_key),
        outer_sum(saved["normed"], d_value),
        outer_sum(saved["mixed"], d_resid_low),
        jnp.sum(gain_two_part, axis=0),
        outer_sum(saved["second"], d_gate_low),
        outer_sum(saved["second"], d_up_low),
        outer_sum(saved["hidden"], grad_low),
    )


def shards(
    tokens,
    cotangent,
    block_order,
    norm_one,
    w_query,
    w_key,
    w_value,
    w_out,
    norm_two,
    w_gate,
    w_up,
    w_down,
):
    section_index = lax.axis_index("section")
    section_count = lax.axis_size("section")
    context_rank = lax.axis_index("ctx")
    context_size = lax.axis_size("ctx")
    micro_count = tokens.shape[0]
    local_rows = tokens.shape[2]
    model_width = tokens.shape[3]
    half_rows = local_rows // 2
    seq_len = local_rows * context_size
    head_size = HEAD
    head_count = HEADS
    kv_count = KV_HEADS
    group_size = head_count // kv_count
    query_width = head_count * head_size
    key_width = kv_count * head_size
    score_scale = head_size ** (-0.5)
    gathered = (
        lax.all_gather(norm_one[0], "wsh", axis=0, tiled=True),
        lax.all_gather(w_query[0], "wsh", axis=0, tiled=True),
        lax.all_gather(w_key[0], "wsh", axis=0, tiled=True),
        lax.all_gather(w_value[0], "wsh", axis=0, tiled=True),
        lax.all_gather(w_out[0], "wsh", axis=0, tiled=True),
        lax.all_gather(norm_two[0], "wsh", axis=0, tiled=True),
        lax.all_gather(w_gate[0], "wsh", axis=0, tiled=True),
        lax.all_gather(w_up[0], "wsh", axis=0, tiled=True),
        lax.all_gather(w_down[0], "wsh", axis=0, tiled=True),
    )
    gain_one = gathered[0].astype(jnp.float32)
    wq_full, wk_full, wv_full, wo_full = (gathered[1], gathered[2], gathered[3], gathered[4])
    gain_two = gathered[5].astype(jnp.float32)
    wg_full, wu_full, wd_full = (gathered[6], gathered[7], gathered[8])
    own_blocks = lax.dynamic_slice_in_dim(block_order, 2 * context_rank, 2, 0)
    offsets = jnp.arange(half_rows, dtype=jnp.int32)
    local_pos = jnp.concatenate(
        [own_blocks[0] * half_rows + offsets, own_blocks[1] * half_rows + offsets]
    )
    all_rows = jnp.arange(seq_len, dtype=jnp.int32)
    owner_block = all_rows // half_rows
    table_index = jnp.arange(2 * context_size, dtype=jnp.int32)
    key_pos = (
        jnp.sum(
            jnp.where(owner_block[:, None] == table_index[None, :], block_order[None, :], 0), axis=1
        )
        * half_rows
        + all_rows % half_rows
    )
    causal = local_pos[:, None] >= key_pos[None, :]
    local_angle = angles(local_pos, head_size)
    cosine = jnp.cos(local_angle)[:, None, :]
    sine = jnp.sin(local_angle)[:, None, :]

    def score_block(query_rot, key_all):
        grouped = query_rot.reshape(local_rows, kv_count, group_size, head_size)
        raw_scores = (
            jnp.einsum("qkgd,tkd->kgqt", grouped, key_all, preferred_element_type=jnp.float32)
            * score_scale
        )
        return jnp.where(causal, raw_scores, -1e30)

    step_count = micro_count + section_count - 1
    incoming = jnp.zeros((local_rows, model_width), jnp.float32)
    results = []
    saved_list = []
    for turn_index in range(step_count):
        first_in = tokens[min(turn_index, micro_count - 1), 0]
        layer_in = jnp.where(section_index == 0, first_in, incoming)
        normed = norm_gain(layer_in, gain_one).astype(jnp.bfloat16)
        forward_query_rot = rotate(
            product(normed, wq_full).reshape(local_rows, head_count, head_size), cosine, sine
        ).astype(jnp.bfloat16)
        key_local = rotate(
            product(normed, wk_full).reshape(local_rows, kv_count, head_size), cosine, sine
        ).astype(jnp.bfloat16)
        value_local = (
            product(normed, wv_full).astype(jnp.bfloat16).reshape(local_rows, kv_count, head_size)
        )
        forward_key_all = lax.all_gather(key_local, "ctx", axis=0, tiled=True)
        forward_value_all = lax.all_gather(value_local, "ctx", axis=0, tiled=True)
        forward_scores = score_block(forward_query_rot, forward_key_all)
        row_top = jnp.max(forward_scores, axis=-1, keepdims=True)
        exponent = jnp.exp(forward_scores - row_top)
        row_total = jnp.sum(exponent, axis=-1, keepdims=True)
        forward_probabilities = exponent / row_total
        log_total = row_top[..., 0] + jnp.log(row_total[..., 0])
        mixed = jnp.einsum(
            "kgqt,tkd->qkgd",
            forward_probabilities.astype(jnp.bfloat16),
            forward_value_all,
            preferred_element_type=jnp.float32,
        )
        mixed = mixed.reshape(local_rows, query_width).astype(jnp.bfloat16)
        resid = layer_in + product(mixed, wo_full)
        second = norm_gain(resid, gain_two).astype(jnp.bfloat16)
        gate = product(second, wg_full)
        up_proj = product(second, wu_full)
        hidden = silu_product(gate, up_proj).astype(jnp.bfloat16)
        result = resid + product(hidden, wd_full)
        forward_saved = {
            "layer_in": layer_in,
            "normed": normed,
            "query_rot": forward_query_rot,
            "log_total": log_total,
            "mixed": mixed,
            "resid": resid,
            "second": second,
            "gate": gate,
            "up_proj": up_proj,
            "hidden": hidden,
        }
        forward_saved["key_all"] = forward_key_all
        forward_saved["value_all"] = forward_value_all
        result, saved = (result, forward_saved)
        results.append(result)
        saved_list.append(saved)
        if turn_index + 1 < step_count:
            incoming = passed_along(result.astype(jnp.bfloat16), "section", 1).astype(result.dtype)
    saved_stack = jax.tree.map(lambda *items: jnp.stack(items), *saved_list)
    section_out = lax.dynamic_slice_in_dim(jnp.stack(results), section_index, micro_count, 0)
    grad_incoming = jnp.zeros((local_rows, model_width), jnp.float32)
    grad_list = []
    parts_list = []
    for turn_index in range(step_count):
        forward_turn = jnp.clip(
            turn_index - section_count + 1 + 2 * section_index, 0, step_count - 1
        )
        saved = jax.tree.map(
            lambda stacked: lax.dynamic_index_in_dim(stacked, forward_turn, 0, keepdims=False),
            saved_stack,
        )
        last_grad = cotangent[min(turn_index, micro_count - 1), 0]
        grad_out = jnp.where(section_index == section_count - 1, last_grad, grad_incoming)
        grad_low = grad_out.astype(jnp.bfloat16)
        d_hidden = product_back(grad_low, wd_full)
        _, silu_back = jax.vjp(silu_product, saved["gate"], saved["up_proj"])
        d_gate, d_up = silu_back(d_hidden)
        d_gate_low = d_gate.astype(jnp.bfloat16)
        d_up_low = d_up.astype(jnp.bfloat16)
        d_second = product_back(d_gate_low, wg_full) + product_back(d_up_low, wu_full)
        _, norm_back_two = jax.vjp(norm_gain, saved["resid"], gain_two)
        d_resid_norm, gain_two_part = norm_back_two(d_second)
        d_resid = grad_out + d_resid_norm
        d_resid_low = d_resid.astype(jnp.bfloat16)
        d_mixed = (
            product_back(d_resid_low, wo_full)
            .astype(jnp.bfloat16)
            .reshape(local_rows, kv_count, group_size, head_size)
        )
        backward_key_all = saved["key_all"]
        value_all = saved["value_all"]
        backward_query_rot = saved["query_rot"]
        scores = score_block(backward_query_rot, backward_key_all)
        probabilities = jnp.exp(scores - saved["log_total"][..., None])
        d_probs = jnp.einsum(
            "qkgd,tkd->kgqt", d_mixed, value_all, preferred_element_type=jnp.float32
        )
        d_value_all = jnp.einsum(
            "kgqt,qkgd->tkd",
            probabilities.astype(jnp.bfloat16),
            d_mixed,
            preferred_element_type=jnp.float32,
        )
        row_delta = jnp.sum(probabilities * d_probs, axis=-1, keepdims=True)
        d_scores = (probabilities * (d_probs - row_delta)).astype(jnp.bfloat16)
        query_grouped = backward_query_rot.reshape(local_rows, kv_count, group_size, head_size)
        d_query_rot = (
            jnp.einsum(
                "kgqt,tkd->qkgd", d_scores, backward_key_all, preferred_element_type=jnp.float32
            )
            * score_scale
        )
        d_key_all = (
            jnp.einsum(
                "kgqt,qkgd->tkd", d_scores, query_grouped, preferred_element_type=jnp.float32
            )
            * score_scale
        )
        d_key_sum = lax.psum_scatter(
            d_key_all.astype(jnp.bfloat16), "ctx", scatter_dimension=0, tiled=True
        ).astype(jnp.float32)
        d_value_sum = lax.psum_scatter(
            d_value_all.astype(jnp.bfloat16), "ctx", scatter_dimension=0, tiled=True
        ).astype(jnp.float32)
        d_query = (
            rotate(d_query_rot.reshape(local_rows, head_count, head_size), cosine, -sine)
            .reshape(local_rows, query_width)
            .astype(jnp.bfloat16)
        )
        d_key = rotate(d_key_sum, cosine, -sine).reshape(local_rows, key_width).astype(jnp.bfloat16)
        d_value = d_value_sum.reshape(local_rows, key_width).astype(jnp.bfloat16)
        d_normed = (
            product_back(d_query, wq_full)
            + product_back(d_key, wk_full)
            + product_back(d_value, wv_full)
        )
        _, norm_back_one = jax.vjp(norm_gain, saved["layer_in"], gain_one)
        d_in_norm, gain_one_part = norm_back_one(d_normed)
        grad_in = d_resid + d_in_norm
        parts = (
            gain_one_part,
            gain_two_part,
            d_query,
            d_key,
            d_value,
            d_resid_low,
            d_gate_low,
            d_up_low,
            grad_low,
        )
        grad_in, parts = (grad_in, parts)
        grad_list.append(grad_in)
        parts_list.append(parts)
        if turn_index + 1 < step_count:
            grad_incoming = passed_along(grad_in.astype(jnp.bfloat16), "section", -1).astype(
                grad_in.dtype
            )
    parts_stack = jax.tree.map(lambda *items: jnp.stack(items), *parts_list)
    input_grads = lax.dynamic_slice_in_dim(
        jnp.stack(grad_list), section_count - 1 - section_index, micro_count, 0
    )
    saved_valid = jax.tree.map(
        lambda stacked: lax.dynamic_slice_in_dim(stacked, section_index, micro_count, 0),
        saved_stack,
    )
    parts_valid = jax.tree.map(
        lambda stacked: lax.dynamic_slice_in_dim(
            stacked, section_count - 1 - section_index, micro_count, 0
        ),
        parts_stack,
    )
    terms = weight_terms(saved_valid, parts_valid)
    summed = (
        lax.psum_scatter(terms[0], ("ctx", "wsh"), scatter_dimension=0, tiled=True),
        lax.psum_scatter(terms[1], ("ctx", "wsh"), scatter_dimension=0, tiled=True),
        lax.psum_scatter(terms[2], ("ctx", "wsh"), scatter_dimension=0, tiled=True),
        lax.psum_scatter(terms[3], ("ctx", "wsh"), scatter_dimension=0, tiled=True),
        lax.psum_scatter(terms[4], ("ctx", "wsh"), scatter_dimension=0, tiled=True),
        lax.psum_scatter(terms[5], ("ctx", "wsh"), scatter_dimension=0, tiled=True),
        lax.psum_scatter(terms[6], ("ctx", "wsh"), scatter_dimension=0, tiled=True),
        lax.psum_scatter(terms[7], ("ctx", "wsh"), scatter_dimension=0, tiled=True),
        lax.psum_scatter(terms[8], ("ctx", "wsh"), scatter_dimension=0, tiled=True),
    )
    return (
        section_out[None, :, None],
        input_grads[None, :, None],
        summed[0][None],
        summed[1][None],
        summed[2][None],
        summed[3][None],
        summed[4][None],
        summed[5][None],
        summed[6][None],
        summed[7][None],
        summed[8][None],
    )


def solution(mesh):
    in_specs = (
        P(None, "wsh", "ctx", None),
        P(None, "wsh", "ctx", None),
        P(),
        P("section", "wsh"),
        P("section", "wsh", None),
        P("section", "wsh", None),
        P("section", "wsh", None),
        P("section", "wsh", None),
        P("section", "wsh"),
        P("section", "wsh", None),
        P("section", "wsh", None),
        P("section", "wsh", None),
    )
    out_specs = (
        P("section", None, "wsh", "ctx", None),
        P("section", None, "wsh", "ctx", None),
        P("section", ("ctx", "wsh")),
        P("section", ("ctx", "wsh"), None),
        P("section", ("ctx", "wsh"), None),
        P("section", ("ctx", "wsh"), None),
        P("section", ("ctx", "wsh"), None),
        P("section", ("ctx", "wsh")),
        P("section", ("ctx", "wsh"), None),
        P("section", ("ctx", "wsh"), None),
        P("section", ("ctx", "wsh"), None),
    )
    return jax.shard_map(shards, mesh=mesh, in_specs=in_specs, out_specs=out_specs, check_vma=False)
```

profile of v0, /device:TPU:16, one launch (start us, length us, event | category | flops | bytes accessed | tf_op | source)
XLA Modules:
  0.0 1949.5 jit_solution(12686872662532860846)
XLA Ops:
  14.4 11.7 all-reduce.17
  27.7 25.8 %all-gather.2 = bf16[1,960,320]{2,0,1:T(2,128)(2,1)} all-gather(bf16[1,240,320]{2,0,1:T(2,128)(2,1)S(1)} %copy.92), channel_id=4, replica_groups=mesh['section'=2,'ctx'=16,'wsh'=4] {'wsh'}, dimensions={1}, use_global_device_ids=true | all-gather | bytes 768000 | tf_op jit(solution)/shard_map/all_gather | solution.py:121
  60.1 17.5 all-gather.1
  119.9 28.4 %all-gather.21.cloned.1.call-done = bf16[2048,5,64]{0,2,1:T(8,128)(2,1)} async-done(((bf16[128,5,64]{0,2,1:T(8,128)(2,1)}), bf16[2048,5,64]{0,2,1:T(8,128)(2,1)}) %all-gather.21.cloned.1.call-update) | async-done | bytes 1310736 | tf_op jit(solution)/shard_map/all_gather | solution.py:179
  158.4 22.4 %all-gather.35.cloned.1.call-done = bf16[1,960,960]{2,1,0:T(8,128)(2,1)} async-done(((bf16[1,240,960]{2,1,0:T(8,128)(2,1)}), bf16[1,960,960]{2,1,0:T(8,128)(2,1)}) %all-gather.35.cloned.1.call-update) | async-done | bytes 1843216 | tf_op jit(solution)/shard_map/all_gather | solution.py:123
  183.2 53.4 %all-gather.37.cloned.1.call-done = bf16[1,960,2560]{2,1,0:T(8,128)(2,1)} async-done(((bf16[1,240,2560]{2,1,0:T(8,128)(2,1)}), bf16[1,960,2560]{2,1,0:T(8,128)(2,1)}) %all-gather.37.cloned.1.call-update) | async-done | bytes 4915216 | tf_op jit(solution)/shard_map/all_gather | solution.py:125
  241.5 51.4 %all-gather.39.cloned.1.call-done = bf16[1,960,2560]{2,1,0:T(8,128)(2,1)} async-done(((bf16[1,240,2560]{2,1,0:T(8,128)(2,1)}), bf16[1,960,2560]{2,1,0:T(8,128)(2,1)}) %all-gather.39.cloned.1.call-update) | async-done | bytes 4915216 | tf_op jit(solution)/shard_map/all_gather | solution.py:126
  297.8 51.6 %all-gather.41.cloned.1.call-done = bf16[1,2560,960]{1,2,0:T(8,128)(2,1)} async-done(((bf16[1,640,960]{1,2,0:T(8,128)(2,1)}), bf16[1,2560,960]{1,2,0:T(8,128)(2,1)}) %all-gather.41.cloned.1.call-update) | async-done | bytes 4915216 | tf_op jit(solution)/shard_map/all_gather | solution.py:127
  365.4 37.8 %all-gather.27.cloned.1.call-done = bf16[2048,5,64]{0,2,1:T(8,128)(2,1)} async-done(((bf16[128,5,64]{0,2,1:T(8,128)(2,1)}), bf16[2048,5,64]{0,2,1:T(8,128)(2,1)}) %all-gather.27.cloned.1.call-update) | async-done | bytes 1310736 | tf_op jit(solution)/shard_map/all_gather | solution.py:178
  422.4 26.6 %all-gather.25.cloned.1.call-done = bf16[2048,5,64]{0,2,1:T(8,128)(2,1)} async-done(((bf16[128,5,64]{0,2,1:T(8,128)(2,1)}), bf16[2048,5,64]{0,2,1:T(8,128)(2,1)}) %all-gather.25.cloned.1.call-update) | async-done | bytes 1310736 | tf_op jit(solution)/shard_map/all_gather | solution.py:179
  486.6 33.7 %all-gather.31.cloned.1.call-done = bf16[2048,5,64]{0,2,1:T(8,128)(2,1)} async-done(((bf16[128,5,64]{0,2,1:T(8,128)(2,1)}), bf16[2048,5,64]{0,2,1:T(8,128)(2,1)}) %all-gather.31.cloned.1.call-update) | async-done | bytes 1310736 | tf_op jit(solution)/shard_map/all_gather | solution.py:178
  539.4 26.6 %all-gather.29.cloned.1.call-done = bf16[2048,5,64]{0,2,1:T(8,128)(2,1)} async-done(((bf16[128,5,64]{0,2,1:T(8,128)(2,1)}), bf16[2048,5,64]{0,2,1:T(8,128)(2,1)}) %all-gather.29.cloned.1.call-update) | async-done | bytes 1310736 | tf_op jit(solution)/shard_map/all_gather | solution.py:179
  608.1 10.9 fusion.16
  657.9 49.6 %reduce-scatter.34.cloned.1.call-done = bf16[128,320]{1,0:T(8,128)(2,1)} async-done(((bf16[2048,320]{1,0:T(8,128)(2,1)}), bf16[128,320]{1,0:T(8,128)(2,1)}) %reduce-scatter.34.cloned.1.call-update) | async-done | bytes 81936
  712.6 71.0 %reduce-scatter.36.cloned.1.call-done = bf16[128,320]{1,0:T(8,128)(2,1)} async-done(((bf16[2048,320]{1,0:T(8,128)(2,1)}), bf16[128,320]{1,0:T(8,128)(2,1)}) %reduce-scatter.36.cloned.1.call-update) | async-done | bytes 81936 | tf_op jit(solution)/shard_map/convert_element_type | solution.py:290
  835.0 10.4 fusion.93
  855.0 53.4 %reduce-scatter.38.cloned.1.call-done = bf16[128,320]{1,0:T(8,128)(2,1)} async-done(((bf16[2048,320]{1,0:T(8,128)(2,1)}), bf16[128,320]{1,0:T(8,128)(2,1)}) %reduce-scatter.38.cloned.1.call-update) | async-done | bytes 81936
  913.6 70.8 %reduce-scatter.40.cloned.1.call-done = bf16[128,320]{1,0:T(8,128)(2,1)} async-done(((bf16[2048,320]{1,0:T(8,128)(2,1)}), bf16[128,320]{1,0:T(8,128)(2,1)}) %reduce-scatter.40.cloned.1.call-update) | async-done | bytes 81936 | tf_op jit(solution)/shard_map/convert_element_type | solution.py:290
  1035.5 10.4 fusion.90
  1097.3 12.0 reduce-scatter.42.cloned.1.call-done
  1112.5 72.8 %reduce-scatter.44.cloned.1.call-done = bf16[128,320]{1,0:T(8,128)(2,1)} async-done(((bf16[2048,320]{1,0:T(8,128)(2,1)}), bf16[128,320]{1,0:T(8,128)(2,1)}) %reduce-scatter.44.cloned.1.call-update) | async-done | bytes 81936 | tf_op jit(solution)/shard_map/convert_element_type | solution.py:290
  1193.9 466.7 %fusion.444 = (f32[16,960]{1,0:T(8,128)}, f32[16,320]{1,0:T(8,128)}, f32[16,320]{1,0:T(8,128)}, f32[16,960]{1,0:T(8,128)}, f32[16,2560]{1,0:T(8,128)}, /*index=5*/f32[16,2560]{1,0:T(8,128)}) fusion(f32[960,960]{1,0:T(8,128)} %convolution_bitcast_fusion.7, f32[960,320]{1,0:T(8,128)} %convolution_bitcast_fusion.9, f32[960,320]{1,0:T(8,128)} %convolution_bitcast_fusion.8, ...), kind=kCustom, calls=%all-reduce-scatter.6 | all-reduce-scatter fusion | flops 7864321 | bytes 29983232
  1681.9 160.7 %all-reduce.16 = (f32[960]{0:T(1024)S(1)}, f32[960]{0:T(1024)S(1)}) all-reduce(f32[960]{0:T(1024)S(1)} %fusion.404, f32[960]{0:T(1024)S(1)} %copy-done.145), channel_id=17, replica_groups=mesh['section'=2,'ctx'=16,'wsh'=4] {'ctx','wsh'}, use_global_device_ids=true, to_apply=%region_38.39.clone | all-reduce | flops 1920 | bytes 15360
  1902.1 10.5 collective-permute-start.21
  (689 shorter events, 542.6 us)
Async XLA Ops:
  7.2 78.1 %all-gather.33.cloned.1.call-start = ((), (), s32[]{:S(2)}) async-start(), calls=%async_computation.14 | async-start | bytes 2457600 | tf_op jit(solution)/shard_map/all_gather | solution.py:120
  7.9 94.0 %all-gather.23.cloned.1.call-start = ((), (), s32[]{:S(2)}) async-start(), calls=%async_computation.8 | async-start | bytes 1392640 | tf_op jit(solution)/shard_map/all_gather | solution.py:178
  59.3 89.0 %all-gather.21.cloned.1.call-start = ((), (), s32[]{:S(2)}) async-start(), calls=%async_computation.7 | async-start | bytes 1392640 | tf_op jit(solution)/shard_map/all_gather | solution.py:179
  82.2 98.5 %all-gather.35.cloned.1.call-start = ((), (), s32[]{:S(2)}) async-start(), calls=%async_computation.15 | async-start | bytes 2457600 | tf_op jit(solution)/shard_map/all_gather | solution.py:123
  82.8 153.8 %all-gather.37.cloned.1.call-start = ((), (), s32[]{:S(2)}) async-start(), calls=%async_computation.16 | async-start | bytes 6144000 | tf_op jit(solution)/shard_map/all_gather | solution.py:125
  83.4 209.5 %all-gather.39.cloned.1.call-start = ((), (), s32[]{:S(2)}) async-start(), calls=%async_computation.17 | async-start | bytes 6144000 | tf_op jit(solution)/shard_map/all_gather | solution.py:126
  84.0 265.4 %all-gather.41.cloned.1.call-start = ((), (), s32[]{:S(2)}) async-start(), calls=%async_computation.18 | async-start | bytes 6144000 | tf_op jit(solution)/shard_map/all_gather | solution.py:127
  84.7 318.5 %all-gather.27.cloned.1.call-start = ((), (), s32[]{:S(2)}) async-start(), calls=%async_computation.10 | async-start | bytes 1392640 | tf_op jit(solution)/shard_map/all_gather | solution.py:178
  360.0 89.0 %all-gather.25.cloned.1.call-start = ((), (), s32[]{:S(2)}) async-start(), calls=%async_computation.9 | async-start | bytes 1392640 | tf_op jit(solution)/shard_map/all_gather | solution.py:179
  362.0 158.2 %all-gather.31.cloned.1.call-start = ((), (), s32[]{:S(2)}) async-start(), calls=%async_computation.12 | async-start | bytes 1392640 | tf_op jit(solution)/shard_map/all_gather | solution.py:178
  476.4 89.6 %all-gather.29.cloned.1.call-start = ((), (), s32[]{:S(2)}) async-start(), calls=%async_computation.11 | async-start | bytes 1392640 | tf_op jit(solution)/shard_map/all_gather | solution.py:179
  481.1 226.4 %reduce-scatter.34.cloned.1.call-start = ((), (), s32[]{:S(2)}) async-start(), calls=%async_computation.19 | async-start | bytes 1671168
  633.2 150.4 %reduce-scatter.36.cloned.1.call-start = ((), (), s32[]{:S(2)}) async-start(), calls=%async_computation.20 | async-start | bytes 1671168 | tf_op jit(solution)/shard_map/convert_element_type | solution.py:290
  646.2 262.2 %reduce-scatter.38.cloned.1.call-start = ((), (), s32[]{:S(2)}) async-start(), calls=%async_computation.21 | async-start | bytes 1671168
  834.6 149.8 %reduce-scatter.40.cloned.1.call-start = ((), (), s32[]{:S(2)}) async-start(), calls=%async_computation.22 | async-start | bytes 1671168 | tf_op jit(solution)/shard_map/convert_element_type | solution.py:290
  848.0 261.3 %reduce-scatter.42.cloned.1.call-start = ((), (), s32[]{:S(2)}) async-start(), calls=%async_computation.23 | async-start | bytes 1671168
  1035.5 149.8 %reduce-scatter.44.cloned.1.call-start = ((), (), s32[]{:S(2)}) async-start(), calls=%async_computation.24 | async-start | bytes 1671168 | tf_op jit(solution)/shard_map/convert_element_type | solution.py:290
  1048.6 893.7 %reduce-scatter.32.cloned.1.call-start = ((), (), s32[]{:S(2)}) async-start(), calls=%async_computation.13 | async-start | bytes 10649600 | tf_op jit(solution)/shard_map/reduce_scatter | solution.py:341
  1662.0 187.4 %collective-permute-start.10 = (f32[16,320]{1,0:T(8,128)}, f32[16,320]{1,0:T(8,128)}, u32[]{:S(2)}, u32[]{:S(2)}) collective-permute-start(f32[16,320]{1,0:T(8,128)} %get-tuple-element.82), channel_id=1, source_target_pairs={{0,3},{1,4},{2,5},{3,6},{4,7},{5,8},{6,9},{7,10},{8,11},{9,12},{10... | collective-permute-start | bytes 61448
  1663.9 187.4 %collective-permute-start.9 = (f32[16,320]{1,0:T(8,128)}, f32[16,320]{1,0:T(8,128)}, u32[]{:S(2)}, u32[]{:S(2)}) collective-permute-start(f32[16,320]{1,0:T(8,128)} %get-tuple-element.82), channel_id=1, source_target_pairs={{0,2},{1,3},{2,4},{3,5},{4,6},{5,7},{6,8},{7,9},{8,10},{9,11},{10,... | collective-permute-start | bytes 61448
  1666.8 186.5 %collective-permute-start.8 = (f32[16,320]{1,0:T(8,128)}, f32[16,320]{1,0:T(8,128)}, u32[]{:S(2)}, u32[]{:S(2)}) collective-permute-start(f32[16,320]{1,0:T(8,128)} %get-tuple-element.82), channel_id=1, source_target_pairs={{0,1},{1,2},{2,3},{3,4},{4,5},{5,6},{6,7},{7,8},{8,9},{9,10},{10,1... | collective-permute-start | bytes 61448
  1668.7 178.7 %collective-permute-start.11 = (f32[15,320]{1,0:T(8,128)}, f32[15,320]{1,0:T(8,128)}, u32[]{:S(2)}, u32[]{:S(2)}) collective-permute-start(f32[15,320]{1,0:T(8,128)} %slice.147), channel_id=1, source_target_pairs={{0,4},{1,5},{2,6},{3,7},{4,8},{5,9},{6,10},{7,11},{8,12},{9,13},{1... | collective-permute-start | bytes 57608
  1673.4 185.1 %collective-permute-start.15 = (f32[15,320]{1,0:T(8,128)}, f32[15,320]{1,0:T(8,128)}, u32[]{:S(2)}, u32[]{:S(2)}) collective-permute-start(f32[15,320]{1,0:T(8,128)} %slice.148), channel_id=1, source_target_pairs={{0,4},{1,5},{2,6},{3,7},{4,8},{5,9},{6,10},{7,11},{8,12},{9,13},{1... | collective-permute-start | bytes 57608
  1891.7 36.1 %collective-permute-start.22 = (f32[16,2560]{1,0:T(8,128)S(1)}, f32[16,2560]{1,0:T(8,128)S(1)}, u32[]{:S(2)}, u32[]{:S(2)}) collective-permute-start(f32[16,2560]{1,0:T(8,128)S(1)} %copy-done.84), channel_id=1, source_target_pairs={{0,3},{1,4},{2,5},{3,6},{4,7},{5,8},{6,9},{7,10},{8,11},{9,12},{10... | collective-permute-start | bytes 491528
  (206 other events, 4874.6 us)
Sparse Core Ops, SparseCore 0:
  9.7 42.9 all-gather.32
  59.4 42.4 all-gather.22
  104.6 43.6 all-gather.20
  149.8 30.9 all-gather.34
  182.3 54.3 all-gather.36
  238.1 54.7 all-gather.38
  294.6 54.7 all-gather.40
  360.1 43.0 all-gather.26
  405.3 43.6 all-gather.24
  476.5 43.6 all-gather.30
  522.3 43.6 all-gather.28
  633.3 74.0 reduce-scatter.33
  710.7 72.8 reduce-scatter.35
  834.7 73.6 reduce-scatter.37
  911.5 72.8 reduce-scatter.39
  1035.6 73.5 reduce-scatter.41
  1112.3 72.8 reduce-scatter.43
  1188.1 365.9 reduce-scatter.31
where the time goes:
time: 1960 us; the launch traced here: 1950 us
  waiting for transfers between devices  683 us (35%)
  blocking collectives  682 us (35%)
  matrix products  279 us (14%)
  other arithmetic  104 us (5%)
  starting transfers between devices  96.7 us (5%)
  local copies, waits for them, and re-layouts  82.7 us (4%)
  between operations  20.8 us (1%)
    unnamed x3, blocking collectives  639 us
    convert_element_type x3, waiting for transfers between devices, shards(): d_value = d_value_sum.reshape(local_rows, key_width).astype(jnp.bfloat16)  215 us
    unnamed x45, waiting for transfers between devices  125 us
    unnamed x27, starting transfers between devices  89.6 us
    all_gather x3, waiting for transfers between devices, shards(): forward_value_all = lax.all_gather(value_local, 'ctx', axis=0, tiled=True)  81.6 us
    all_gather x3, waiting for transfers between devices, shards(): forward_key_all = lax.all_gather(key_local, 'ctx', axis=0, tiled=True)  81.5 us
    unnamed x403, local copies, waits for them, and re-layouts  64.3 us
    dot_general x21, matrix products, product(): return jnp.dot(left, right, preferred_element_type=jnp.float32)  54 us
  transfers between devices with their start and end apart: 46, of which 20 were waited for; matrix products, arithmetic and copies ran while one was open for 38% of the time, Pallas kernels for 0%

commit v1 on v0

v1 whole, which is shorter than its diff:
```python
import math

import jax
import jax.numpy as jnp
from jax import lax
from jax.experimental import pallas as pl
from jax.experimental.pallas import tpu as pltpu
from jax.sharding import PartitionSpec as P

HEADS = 15
KV_HEADS = 5
HEAD = 64
GROUP = HEADS // KV_HEADS
D = 960
FF = 2560
KW = KV_HEADS * HEAD
ROWS = 128
BLK = 64
SEQ = 2048
CHUNK = 256
STEPS = 9
EPS = 1e-05
ROPE_BASE = 10000.0
BF = jnp.bfloat16
F32 = jnp.float32
QP = 1024
NEG = -1e30
VMEM_BYTES = 48 * 1024 * 1024

NN = (((1,), (0,)), ((), ()))
NT = (((1,), (1,)), ((), ()))
TN = (((0,), (0,)), ((), ()))


def dot(left, right, dims=NN):
    return lax.dot_general(left, right, dims, preferred_element_type=F32)


def call(body, outs, scratch=(), smem=0):
    def run(*args):
        in_specs = [
            pl.BlockSpec(memory_space=pltpu.SMEM if i < smem else pltpu.VMEM)
            for i in range(len(args))
        ]
        out = pl.pallas_call(
            body,
            in_specs=in_specs,
            out_specs=[pl.BlockSpec(memory_space=pltpu.VMEM) for _ in outs],
            out_shape=[jax.ShapeDtypeStruct(s, t) for s, t in outs],
            scratch_shapes=list(scratch),
            compiler_params=pltpu.CompilerParams(vmem_limit_bytes=VMEM_BYTES),
        )(*args)
        return out

    return run


def lane(shape):
    return lax.broadcasted_iota(jnp.int32, shape, 1)


def normalise(x, gain):
    return x * lax.rsqrt(jnp.mean(x * x, axis=-1, keepdims=True) + EPS) * gain


def norm_back(x, gain, dy):
    r = lax.rsqrt(jnp.mean(x * x, axis=-1, keepdims=True) + EPS)
    cdy = gain * dy
    dx = r * cdy - x * (r * r * r) * jnp.mean(x * cdy, axis=-1, keepdims=True)
    dc = jnp.sum(dy * x * r, axis=0, keepdims=True)
    return dx, dc


def spin(tile, cosine, sine):
    first = (lane(tile.shape) % HEAD) < HEAD // 2
    swapped = jnp.where(first, pltpu.roll(tile, 96, 1), pltpu.roll(tile, 32, 1))
    return tile * cosine + swapped * sine


def project_body(count):
    def body(*refs):
        base = refs[0]
        parts = refs[1 : 1 + count]
        gain, weight, cosine, sine, x_out, normed_out, q_out, kv_out = refs[1 + count :]
        x = base[...]
        for part in parts:
            x = x + part[...].astype(F32)
        x_out[...] = x
        normed = normalise(x, gain[...]).astype(BF)
        normed_out[...] = normed
        cos, sin = cosine[...], sine[...]
        qkv = dot(normed, weight[...])
        for j in range(8):
            tile = spin(qkv[:, j * 128 : (j + 1) * 128], cos, sin)
            q_out[:, j * 128 : (j + 1) * 128] = (tile * (HEAD**-0.5)).astype(BF)
        for g in range(KV_HEADS):
            tile = qkv[:, QP + g * 128 : QP + (g + 1) * 128]
            tile = jnp.where(lane(tile.shape) < HEAD, spin(tile, cos, sin), tile)
            kv_out[:, g * 128 : (g + 1) * 128] = tile.astype(BF)

    return body


def project(base, parts, gain, weight, cosine, sine):
    outs = [((ROWS, D), F32), ((ROWS, D), BF), ((ROWS, QP), BF), ((ROWS, 2 * KW), BF)]
    return call(project_body(len(parts)), outs)(base, *parts, gain, weight, cosine, sine)


def step_place(info, t):
    first, second = info[0], info[1]
    count = first // 4 + 1
    early = t < count
    block = jnp.where(early, 0, 1)
    chunk = jnp.where(early, t, t - count)
    place = jnp.where(early, first, second)
    return block, chunk, place


def causal(place, chunk):
    rows = lax.broadcasted_iota(jnp.int32, (BLK, CHUNK), 0) + place * BLK
    cols = lax.broadcasted_iota(jnp.int32, (BLK, CHUNK), 1) + chunk * CHUNK
    one = rows >= cols
    return jnp.concatenate([one] * GROUP, axis=0)


def head_tile(ref, block, head, upper):
    j = head // 2
    tile = ref[block * BLK : (block + 1) * BLK, j * 128 : (j + 1) * 128].astype(F32)
    if (head % 2 == 1) != upper:
        tile = pltpu.roll(tile, 64, 1)
    keep = (lane(tile.shape) >= HEAD) if upper else (lane(tile.shape) < HEAD)
    return jnp.where(keep, tile, 0.0)


def attend_body(count):
    def body(*refs):
        info, q_ref = refs[0], refs[1]
        pieces = refs[2 : 2 + count]
        (wo, x_ref, gain, mixed_out, lse_out, kvs, resid_out, second_out) = refs[2 + count : 10 + count]
        qh, top, total, acc = refs[10 + count :]
        number = 0
        for piece in pieces:
            for b in range(piece.shape[0] // BLK):
                at = pl.multiple_of(info[2 + number] * BLK, BLK)
                kvs[pl.ds(at, BLK), :] = piece[b * BLK : (b + 1) * BLK, :]
                number += 1
        for i in range(2):
            for g in range(KV_HEADS):
                for r in range(GROUP):
                    qh[i, g, r * BLK : (r + 1) * BLK, :] = head_tile(
                        q_ref, i, g * GROUP + r, False
                    ).astype(BF)
        top[...] = jnp.full(top.shape, NEG, F32)
        total[...] = jnp.zeros(total.shape, F32)
        acc[...] = jnp.zeros(acc.shape, F32)

        def step(t, carry):
            block, chunk, place = step_place(info, t)
            allowed = causal(place, chunk)
            at = pl.multiple_of(chunk * CHUNK, CHUNK)
            for g in range(KV_HEADS):
                keys = kvs[pl.ds(at, CHUNK), g * 128 : (g + 1) * 128]
                scores = dot(qh[block, g], keys, NT)
                scores = jnp.where(allowed, scores, NEG)
                old = top[block, g]
                new = jnp.maximum(old, jnp.max(scores, axis=1, keepdims=True))
                probs = jnp.exp(scores - jnp.concatenate([new, new], axis=1))
                shrink = jnp.exp(old - new)
                top[block, g] = new
                total[block, g] = shrink * total[block, g] + jnp.sum(probs, axis=1, keepdims=True)
                acc[block, g] = shrink * acc[block, g] + dot(probs.astype(BF), keys)
            return carry

        lax.fori_loop(0, STEPS, step, 0)
        for i in range(2):
            heads = []
            for g in range(KV_HEADS):
                sums = total[i, g]
                result = acc[i, g] / sums
                lse_out[i, g] = top[i, g] + jnp.log(sums)
                for r in range(GROUP):
                    heads.append(result[r * BLK : (r + 1) * BLK, :])
            for j in range(8):
                low = pltpu.roll(heads[2 * j], 64, 1)
                rows = slice(i * BLK, (i + 1) * BLK)
                if j < 7:
                    tile = jnp.where(lane(low.shape) < HEAD, low, heads[2 * j + 1])
                    mixed_out[rows, j * 128 : (j + 1) * 128] = tile.astype(BF)
                else:
                    mixed_out[rows, 896:960] = low[:, :64].astype(BF)
        resid = x_ref[...] + dot(mixed_out[...], wo[...])
        resid_out[...] = resid
        second_out[...] = normalise(resid, gain[...]).astype(BF)

    return body


def attend(info, q, pieces, wo, x, gain):
    outs = [
        ((ROWS, D), BF),
        ((2, KV_HEADS, GROUP * BLK, 128), F32),
        ((SEQ, 2 * KW), BF),
        ((ROWS, D), F32),
        ((ROWS, D), BF),
    ]
    shape = (2, KV_HEADS, GROUP * BLK, 128)
    scratch = [pltpu.VMEM(shape, BF)] + [pltpu.VMEM(shape, F32)] * 3
    return call(attend_body(len(pieces)), outs, scratch, smem=1)(info, q, *pieces, wo, x, gain)


def feed_body(second, wgu, wd, gu_out, hidden_out, part_out):
    gu = dot(second[...], wgu[...])
    gu_out[...] = gu
    gate, up = gu[:, : FF // 4], gu[:, FF // 4 :]
    hidden = (gate / (1.0 + jnp.exp(-gate)) * up).astype(BF)
    hidden_out[...] = hidden
    part_out[...] = dot(hidden, wd[...]).astype(BF)


def feed(second, wgu, wd):
    outs = [((ROWS, FF // 2), F32), ((ROWS, FF // 4), BF), ((ROWS, D), BF)]
    return call(feed_body, outs)(second, wgu, wd)


def feed_back_body(grad_low, gu, wgu, wd, dgu_out, part_out):
    d_hidden = dot(grad_low[...], wd[...], NT)
    gate, up = gu[:, : FF // 4], gu[:, FF // 4 :]
    sig = 1.0 / (1.0 + jnp.exp(-gate))
    d_gate = d_hidden * up * sig * (1.0 + gate * (1.0 - sig))
    d_up = d_hidden * gate * sig
    dgu_out[:, : FF // 4] = d_gate.astype(BF)
    dgu_out[:, FF // 4 :] = d_up.astype(BF)
    part_out[...] = dot(dgu_out[...], wgu[...], NT).astype(BF)


def feed_back(grad_low, gu, wgu, wd):
    outs = [((ROWS, FF // 2), BF), ((ROWS, D), BF)]
    return call(feed_back_body, outs)(grad_low, gu, wgu, wd)


def attend_back_body(
    info, p0, p1, p2, p3, grad, resid, gain, wo, mixed, q_ref, lse, kvs, cosine, sine,
    d_resid_out, d_low_out, dc_out, dq_out, o0, o1, o2, o3,
    qd, delta, dq, dkv, dm, mx,
):
    d_second = p0[...].astype(F32) + p1[...].astype(F32) + p2[...].astype(F32) + p3[...].astype(F32)
    dx, dc = norm_back(resid[...], gain[...], d_second)
    dc_out[...] = dc
    d_resid = grad[...] + dx
    d_resid_out[...] = d_resid
    low = d_resid.astype(BF)
    d_low_out[...] = low
    dm[:, :D] = dot(low, wo[...], NT).astype(BF)
    dm[:, D:] = jnp.zeros((ROWS, QP - D), BF)
    mx[:, :D] = mixed[...]
    mx[:, D:] = jnp.zeros((ROWS, QP - D), BF)
    span = GROUP * BLK
    for i in range(2):
        for g in range(KV_HEADS):
            for r in range(GROUP):
                head = g * GROUP + r
                there = slice(r * BLK, (r + 1) * BLK)
                qd[i, g, there, :] = head_tile(q_ref, i, head, False).astype(BF)
                do = head_tile(dm, i, head, True)
                qd[i, g, span + r * BLK : span + (r + 1) * BLK, :] = do.astype(BF)
                dots = jnp.sum(do * head_tile(mx, i, head, True), axis=1, keepdims=True)
                delta[i, g, there, :] = jnp.broadcast_to(dots, (BLK, 128))
    dq[...] = jnp.zeros(dq.shape, F32)
    dkv[...] = jnp.zeros(dkv.shape, F32)

    def step(t, carry):
        block, chunk, place = step_place(info, t)
        allowed = causal(place, chunk)
        at = pl.multiple_of(chunk * CHUNK, CHUNK)
        for g in range(KV_HEADS):
            keys = kvs[pl.ds(at, CHUNK), g * 128 : (g + 1) * 128]
            both = dot(qd[block, g], keys, NT)
            scores, d_probs = both[:span], both[span:]
            total = lse[block, g]
            probs = jnp.exp(
                jnp.where(allowed, scores, NEG) - jnp.concatenate([total, total], axis=1)
            )
            shift = delta[block, g]
            d_scores = probs * (d_probs - jnp.concatenate([shift, shift], axis=1))
            d_low = d_scores.astype(BF)
            dq[block, g] += dot(d_low, keys)
            stacked = jnp.concatenate([d_low, probs.astype(BF)], axis=0)
            dkv[pl.ds(at, CHUNK), g * 128 : (g + 1) * 128] += dot(stacked, qd[block, g], TN)
        return carry

    lax.fori_loop(0, STEPS, step, 0)
    for i in range(2):
        rows = slice(i * BLK, (i + 1) * BLK)
        cos, sin = cosine[rows, :], sine[rows, :]
        heads = []
        for g in range(KV_HEADS):
            for r in range(GROUP):
                heads.append(dq[i, g, r * BLK : (r + 1) * BLK, :] * (HEAD**-0.5))
        for j in range(8):
            if j < 7:
                high = pltpu.roll(heads[2 * j + 1], 64, 1)
                tile = jnp.where(lane(high.shape) < HEAD, heads[2 * j], high)
                dq_out[rows, j * 128 : (j + 1) * 128] = spin(tile, cos, -sin).astype(BF)
            else:
                dq_out[rows, 896:960] = spin(heads[14], cos, -sin)[:, :64].astype(BF)
    number = 0
    for out in (o0, o1, o2, o3):
        for b in range(out.shape[0] // BLK):
            at = pl.multiple_of(info[34 + number] * BLK, BLK)
            out[b * BLK : (b + 1) * BLK, :] = dkv[pl.ds(at, BLK), :].astype(BF)
            number += 1


def attend_back(info, parts, grad, resid, gain, wo, mixed, q, lse, kvs, cosine, sine):
    outs = [
        ((ROWS, D), F32),
        ((ROWS, D), BF),
        ((1, D), F32),
        ((ROWS, D), BF),
    ] + [((4 * ROWS, 2 * KW), BF)] * 4
    shape = (2, KV_HEADS, GROUP * BLK, 128)
    scratch = [
        pltpu.VMEM((2, KV_HEADS, 2 * GROUP * BLK, 128), BF),
        pltpu.VMEM(shape, F32),
        pltpu.VMEM(shape, F32),
        pltpu.VMEM((SEQ, 2 * KW), F32),
        pltpu.VMEM((ROWS, QP), BF),
        pltpu.VMEM((ROWS, QP), BF),
    ]
    return call(attend_back_body, outs, scratch, smem=1)(
        info, *parts, grad, resid, gain, wo, mixed, q, lse, kvs, cosine, sine
    )


def project_back_body(
    k0, k1, k2, k3, dq, d_resid, x_ref, gain, weight, cosine, sine, dkv_out, grad_out, dc_out
):
    sums = k0[...].astype(F32) + k1[...].astype(F32) + k2[...].astype(F32) + k3[...].astype(F32)
    cos, sin = cosine[...], -sine[...]
    for g in range(KV_HEADS):
        tile = sums[:, g * 128 : (g + 1) * 128]
        tile = jnp.where(lane(tile.shape) < HEAD, spin(tile, cos, sin), tile)
        dkv_out[:, g * 128 : (g + 1) * 128] = tile.astype(BF)
    d_normed = dot(dq[...], weight[:, :D], NT) + dot(dkv_out[...], weight[:, QP:], NT)
    dx, dc = norm_back(x_ref[...], gain[...], d_normed)
    dc_out[...] = dc
    grad_out[...] = d_resid[...] + dx


def project_back(pieces, dq, d_resid, x, gain, weight, cosine, sine):
    outs = [((ROWS, 2 * KW), BF), ((ROWS, D), F32), ((1, D), F32)]
    return call(project_back_body, outs)(*pieces, dq, d_resid, x, gain, weight, cosine, sine)


def z_shift(value, steps):
    return lax.ppermute(value, "wsh", [(i, (i + steps) % 4) for i in range(4)])


def x_shift(value, steps):
    pairs = [(y * 4 + x, y * 4 + (x + steps) % 4) for y in range(4) for x in range(4)]
    return lax.ppermute(value, "ctx", pairs)


def y_shift(value, steps):
    pairs = [(y * 4 + x, ((y + steps) % 4) * 4 + x) for y in range(4) for x in range(4)]
    return lax.ppermute(value, "ctx", pairs)


def swap(value):
    return lax.ppermute(value, "section", [(0, 1), (1, 0)])


def reduce_ctx(value):
    rank = lax.axis_index("ctx")
    y, x = rank // 4, rank % 4
    cut = value.reshape((4, 4) + value.shape[1:])
    total = lax.dynamic_index_in_dim(cut, y, 0, False).astype(F32)
    for k in (1, 3, 2):
        total = total + y_shift(lax.dynamic_index_in_dim(cut, (y + k) % 4, 0, False), k).astype(F32)
    low = total.astype(BF)
    out = lax.dynamic_index_in_dim(total, x, 0, False)
    for k in (1, 3, 2):
        out = out + x_shift(lax.dynamic_index_in_dim(low, (x + k) % 4, 0, False), k).astype(F32)
    return out


def in_order(pieces, rank):
    stacked = jnp.stack(pieces)
    return [lax.dynamic_index_in_dim(stacked, (rank - z) % 4, 0, False) for z in range(4)]


def shards(
    tokens, cotangent, block_order, norm_one, w_query, w_key, w_value, w_out, norm_two, w_gate, w_up, w_down
):
    section = lax.axis_index("section")
    rank = lax.axis_index("ctx")
    z_rank = lax.axis_index("wsh")
    first_core = section == 0
    quarter = FF // 4

    key_value = jnp.concatenate(
        [w_key[0].reshape(-1, KV_HEADS, HEAD), w_value[0].reshape(-1, KV_HEADS, HEAD)], axis=2
    ).reshape(-1, 2 * KW)
    shard_qkv = jnp.concatenate(
        [w_query[0], jnp.zeros((w_query.shape[1], QP - D), BF), key_value], axis=1
    )
    gains = jnp.stack([norm_one[0], norm_two[0]])
    gain_parts = [gains] + [z_shift(gains, k) for k in (1, 2, 3)]
    gains = jnp.concatenate(in_order(gain_parts, z_rank), axis=1)

    def both(value):
        other = swap(value)
        return jnp.where(first_core, value, other), jnp.where(first_core, other, value)

    gain_pair = [g.astype(F32) for g in both(gains)]
    wqkv = both(lax.all_gather(shard_qkv, "wsh", axis=0, tiled=True))
    wo = both(lax.all_gather(w_out[0], "wsh", axis=0, tiled=True))
    def columns(z):
        start = z * quarter
        return jnp.concatenate(
            [
                lax.dynamic_slice_in_dim(w_gate[0], start, quarter, 1),
                lax.dynamic_slice_in_dim(w_up[0], start, quarter, 1),
            ],
            axis=1,
        )

    wgu_parts = [columns(z_rank)] + [z_shift(columns((z_rank + k) % 4), k) for k in (1, 2, 3)]
    wgu = both(jnp.concatenate(in_order(wgu_parts, z_rank), axis=0))
    wd = both(w_down[0])

    own = lax.dynamic_slice_in_dim(block_order, 2 * rank, 2, 0)
    pairs = block_order.reshape(4, 4, 2)
    y, x = rank // 4, rank % 4
    step = jnp.arange(4, dtype=jnp.int32)
    came = pairs[(y - step) % 4][:, (x - step) % 4].reshape(32)
    goes = pairs[(y + step) % 4][:, (x + step) % 4].reshape(32)
    info = jnp.concatenate([own, came, goes]).astype(jnp.int32)
    offsets = jnp.arange(BLK, dtype=jnp.int32)
    local_pos = (own[:, None] * BLK + offsets[None, :]).reshape(ROWS)
    frequency = jnp.exp(
        jnp.arange(HEAD // 2).astype(F32) * (-2.0 * math.log(ROPE_BASE) / HEAD)
    )
    angle = local_pos.astype(F32)[:, None] * frequency[None, :]
    cos32, sin32 = jnp.cos(angle), jnp.sin(angle)
    cosine = jnp.concatenate([cos32] * 4, axis=1)
    sine = jnp.concatenate([-sin32, sin32, -sin32, sin32], axis=1)

    micro = section
    own_tokens = lax.dynamic_index_in_dim(tokens, micro, 0, False)[0]
    own_cotangent = lax.dynamic_index_in_dim(cotangent, micro, 0, False)[0]

    saved = []
    base, parts = own_tokens, []
    for layer in range(2):
        gain_one = gain_pair[layer][0:1]
        gain_two = gain_pair[layer][1:2]
        x_in, normed, q, kv = project(base, parts, gain_one, wqkv[layer], cosine, sine)
        row = jnp.concatenate([kv] + [x_shift(kv, k) for k in (1, 2, 3)], axis=0)
        pieces = [row] + [y_shift(row, k) for k in (1, 2, 3)]
        mixed, lse, kvs, resid, second = attend(info, q, pieces, wo[layer], x_in, gain_two)
        seconds = [second] + [z_shift(second, k) for k in (1, 2, 3)]
        fed = [feed(s, wgu[layer], wd[layer]) for s in seconds]
        parts = [fed[0][2]] + [z_shift(fed[k][2], -k) for k in (1, 2, 3)]
        base = resid
        saved.append(
            dict(
                x=x_in, normed=normed, q=q, mixed=mixed, lse=lse, kvs=kvs, resid=resid,
                seconds=jnp.concatenate(seconds), gu=[f[0] for f in fed],
                hidden=jnp.concatenate([f[1] for f in fed]),
            )
        )
    final = base
    for part in parts:
        final = final + part.astype(F32)
    outputs = [saved[1]["x"], final]

    grad = own_cotangent
    input_grads = [None, None]
    sums = [None, None]
    for layer in (1, 0):
        s = saved[layer]
        gain_one = gain_pair[layer][0:1]
        gain_two = gain_pair[layer][1:2]
        low = grad.astype(BF)
        lows = [low] + [z_shift(low, k) for k in (1, 2, 3)]
        back = [feed_back(lows[k], s["gu"][k], wgu[layer], wd[layer]) for k in range(4)]
        parts = [back[0][1]] + [z_shift(back[k][1], -k) for k in (1, 2, 3)]
        dgu = jnp.concatenate([b[0] for b in back])
        grad_gu = dot(s["seconds"], dgu, TN)
        grad_down = dot(s["hidden"], jnp.concatenate(lows), TN)
        d_resid, d_low, dc_two, dq, k0, k1, k2, k3 = attend_back(
            info, parts, grad, s["resid"], gain_two, wo[layer], s["mixed"], s["q"], s["lse"], s["kvs"], cosine, sine
        )
        row = k0.astype(F32)
        for k, piece in ((1, k1), (3, k3), (2, k2)):
            row = row + y_shift(piece, k).astype(F32)
        row = row.astype(BF).reshape(4, ROWS, 2 * KW)
        own_pieces = [row[0]] + [x_shift(row[k], k) for k in (1, 2, 3)]
        dkv, grad, dc_one = project_back(
            own_pieces, dq, d_resid, s["x"], gain_one, wqkv[layer], cosine, sine
        )
        input_grads[layer] = grad
        dkv_heads = dkv.reshape(ROWS, KV_HEADS, 2 * HEAD)
        dk = dkv_heads[:, :, :HEAD].reshape(ROWS, KW)
        dv = dkv_heads[:, :, HEAD:].reshape(ROWS, KW)
        cut = jnp.concatenate(
            [
                jnp.concatenate(
                    [
                        dq[:, z * 240 : (z + 1) * 240],
                        dk[:, z * 80 : (z + 1) * 80],
                        dv[:, z * 80 : (z + 1) * 80],
                        d_low[:, z * 240 : (z + 1) * 240],
                    ],
                    axis=1,
                )[None]
                for z in range(4)
            ]
        )
        mine = [lax.dynamic_index_in_dim(cut, z_rank, 0, False)] + [
            z_shift(lax.dynamic_index_in_dim(cut, (z_rank + k) % 4, 0, False), k) for k in (1, 2, 3)
        ]
        mine = jnp.concatenate(mine)
        ahead = jnp.concatenate([s["normed"], s["mixed"]], axis=1)
        ahead = jnp.concatenate([ahead] + [z_shift(ahead, k) for k in (1, 2, 3)])
        grad_qkv = dot(ahead[:, :D], mine[:, :400], TN)
        grad_out = dot(ahead[:, D:], mine[:, 400:], TN)
        halves = (
            jnp.concatenate([grad_gu[:, :quarter], grad_qkv[:, :320], dc_one.T], axis=1),
            jnp.concatenate([grad_gu[:, quarter:], grad_qkv[:, 320:], grad_out, dc_two.T], axis=1),
        )
        downs = (grad_down[:, :480], grad_down[:, 480:])

        def shared(pair):
            keep = jnp.where(first_core, pair[0], pair[1])
            give = jnp.where(first_core, pair[1], pair[0])
            return (keep + swap(give.astype(BF)).astype(F32)).astype(BF)

        part_a = reduce_ctx(shared(halves).reshape(16, 60, 961))
        part_b = reduce_ctx(shared(downs).reshape(16, 40, 480))
        sums[layer] = (part_a, part_b)

    def meet(index):
        mine = jnp.where(first_core, sums[0][index], sums[1][index])
        other = swap(jnp.where(first_core, sums[1][index], sums[0][index]))
        return mine, other

    own_a, other_a = meet(0)
    own_b, other_b = meet(1)
    half_a = (jnp.where(first_core, own_a, other_a), jnp.where(first_core, other_a, own_a))
    half_b = (jnp.where(first_core, own_b, other_b), jnp.where(first_core, other_b, own_b))
    joined = jnp.concatenate(half_a, axis=1).reshape(4, 15, 1922)
    pieces = [lax.dynamic_index_in_dim(joined, z_rank, 0, False)] + [
        z_shift(lax.dynamic_index_in_dim(joined, (z_rank + k) % 4, 0, False), k) for k in (1, 2, 3)
    ]
    pieces = in_order(pieces, z_rank)

    def spread(start, width):
        return jnp.concatenate([p[:, start : start + width] for p in pieces], axis=1)[None]

    grad_gate = spread(0, 640)
    grad_query = spread(640, 240)
    grad_key = spread(880, 80)
    gain_one_sum = sum(p[:, 960] for p in pieces)[None]
    grad_up = spread(961, 640)
    grad_value = spread(1601, 80)
    grad_out = spread(1681, 240)
    gain_two_sum = sum(p[:, 1921] for p in pieces)[None]
    down = jnp.concatenate(half_b, axis=1)
    moves = [(c * 4 + z, (4 * z + c // 4) * 4 + c % 4) for c in range(16) for z in range(4)]
    grad_down = lax.ppermute(down, ("ctx", "wsh"), moves)[None]
    def arranged(pair):
        mine = jnp.where(first_core, pair[0], pair[1])
        other = swap(jnp.where(first_core, pair[1], pair[0]))
        first = jnp.where(first_core, mine, other)
        last = jnp.where(first_core, other, mine)
        return jnp.stack([first, last])[None, :, None]

    return (
        arranged(outputs),
        arranged(input_grads),
        gain_one_sum,
        grad_query,
        grad_key,
        grad_value,
        grad_out,
        gain_two_sum,
        grad_gate,
        grad_up,
        grad_down,
    )


def solution(mesh):
    rows = P(None, "wsh", "ctx", None)
    gain = P("section", "wsh")
    weight = P("section", "wsh", None)
    in_specs = (rows, rows, P(), gain, weight, weight, weight, weight, gain, weight, weight, weight)
    result = P("section", None, "wsh", "ctx", None)
    gain_out = P("section", ("ctx", "wsh"))
    weight_out = P("section", ("ctx", "wsh"), None)
    out_specs = (
        result, result, gain_out, weight_out, weight_out, weight_out, weight_out, gain_out,
        weight_out, weight_out, weight_out,
    )
    return jax.shard_map(shards, mesh=mesh, in_specs=in_specs, out_specs=out_specs, check_vma=False)
```

time: 1960 us -> 735 us (0.38)
  blocking collectives: 682 us -> 0 us
  waiting for transfers between devices: 683 us -> 256 us
  matrix products: 279 us -> 19.8 us
  Pallas kernels: 0 us -> 98.2 us
  starting transfers between devices: 96.7 us -> 148 us
  other arithmetic: 104 us -> 81 us
  local copies, waits for them, and re-layouts: 82.7 us -> 103 us
    unnamed x3 -> x0, blocking collectives: 639 us -> none
    all_gather x11 -> x2, waiting for transfers between devices: 342 us -> 67.8 us  [the longest x1 53.2 us: shards(): wqkv = both(lax.all_gather(shard_qkv, 'wsh', axis=0, tiled=True))]
    dot_general x70 -> x8, matrix products: 279 us -> 19.8 us  [dot(): return lax.dot_general(left, right, dims, preferred_element_type=F32)]
    convert_element_type x3 -> x0, waiting for transfers between devices: 215 us -> none  [shards(): d_value = d_value_sum.reshape(local_rows, key_width).astype(jnp.bfloat16)]
    ppermute x4 -> x107, waiting for transfers between devices: 2.22 us -> 188 us  [the longest x24 99.4 us: y_shift(): return lax.ppermute(value, 'ctx', pairs)]
    ppermute x4 -> x107, starting transfers between devices: 5.86 us -> 148 us  [the longest x45 63.6 us: z_shift(): return lax.ppermute(value, 'wsh', [(i, (i + steps) % 4) for i in range(4)])]
    unnamed x45 -> x2, waiting for transfers between devices: 125 us -> 0.03 us
    pallas_call x0 -> x24, Pallas kernels: none -> 98.2 us  [run(): pl.pallas_call(body, in_specs=in_specs, out_specs=[pl.BlockSpec(memory_sp...]
  transfers between devices with their start and end apart: 46 -> 109, of which waited for: 20 -> 48; matrix products, arithmetic and copies ran while one was open for 38% -> 23% of each run, Pallas kernels for 0% -> 13%
where the time goes in v1:
time: 735 us; the launch traced here: 723 us
  waiting for transfers between devices  256 us (35%)
  starting transfers between devices  148 us (20%)
  local copies, waits for them, and re-layouts  103 us (14%)
  Pallas kernels  98.2 us (13%)
  other arithmetic  81 us (11%)
  matrix products  19.8 us (3%)
  between operations  16.7 us (2%)
    ppermute x24, waiting for transfers between devices, y_shift(): return lax.ppermute(value, 'ctx', pairs)  99.4 us
    pallas_call x24, Pallas kernels, run(): pl.pallas_call(body, in_specs=in_specs, out_specs=[pl.BlockSpec(memory_sp...  98.2 us
    ppermute x45, starting transfers between devices, z_shift(): return lax.ppermute(value, 'wsh', [(i, (i + steps) % 4) for i in range(4)])  63.6 us
    all_gather x1, waiting for transfers between devices, shards(): wqkv = both(lax.all_gather(shard_qkv, 'wsh', axis=0, tiled=True))  53.2 us
    ppermute x45, waiting for transfers between devices, z_shift(): return lax.ppermute(value, 'wsh', [(i, (i + steps) % 4) for i in range(4)])  46.3 us
    unnamed x314, local copies, waits for them, and re-layouts  45.6 us
    ppermute x24, starting transfers between devices, x_shift(): return lax.ppermute(value, 'ctx', pairs)  42.7 us
    ppermute x24, starting transfers between devices, y_shift(): return lax.ppermute(value, 'ctx', pairs)  35.3 us
  transfers between devices with their start and end apart: 109, of which 48 were waited for; matrix products, arithmetic and copies ran while one was open for 23% of the time, Pallas kernels for 13%

profile of v1, /device:TPU:16, one launch (start us, length us, event | category | flops | bytes accessed | tf_op | source)
XLA Modules:
  0.0 722.7 jit_solution(17033255945378151708)
XLA Ops:
  22.0 53.2 %all-gather.4.cloned.1.call-done = bf16[960,1664]{1,0:T(8,128)(2,1)} async-done(((bf16[240,1664]{1,0:T(8,128)(2,1)}), bf16[960,1664]{1,0:T(8,128)(2,1)}) %all-gather.4.cloned.1.call-update) | async-done | bytes 3194896 | tf_op jit(solution)/shard_map/all_gather | solution.py:416
  91.1 14.6 %all-gather.6.cloned.1.call-done = bf16[1,960,960]{2,1,0:T(8,128)(2,1)} async-done(((bf16[1,240,960]{2,1,0:T(8,128)(2,1)}), bf16[1,960,960]{2,1,0:T(8,128)(2,1)}) %all-gather.6.cloned.1.call-update) | async-done | bytes 1843216 | tf_op jit(solution)/shard_map/all_gather | solution.py:417
  105.7 5.2 broadcast_select_fusion
  139.8 7.6 %collective-permute-done.8.refs_3_ = bf16[512,640]{1,0:T(8,128)(2,1)S(1)} collective-permute-done((bf16[512,640]{1,0:T(8,128)(2,1)S(1)}, bf16[512,640]{1,0:T(8,128)(2,1)S(1)}, u32[]{:S(2)}, u32[]{:S(2)}) %collective-permute-start.8) | collective-permute-done | bytes 655392 | tf_op jit(solution)/shard_map/ppermute | solution.py:366
  147.5 12.4 %collective-permute-done.9.refs_4_ = bf16[512,640]{1,0:T(8,128)(2,1)S(1)} collective-permute-done((bf16[512,640]{1,0:T(8,128)(2,1)S(1)}, bf16[512,640]{1,0:T(8,128)(2,1)S(1)}, u32[]{:S(2)}, u32[]{:S(2)}) %collective-permute-start.9) | collective-permute-done | bytes 655392 | tf_op jit(solution)/shard_map/ppermute | solution.py:366
  161.7 10.9 %shard_map.204 = (bf16[128,960]{1,0:T(8,128)(2,1)S(1)}, f32[2,5,192,128]{3,2,1,0:T(8,128)S(1)}, bf16[2048,640]{1,0:T(8,128)(2,1)}, f32[128,960]{1,0:T(8,128)S(1)}, bf16[128,960]{1,0:T(8,128)(2,1)S(1)}) custom-call(s32[66]{0:T(128)S(1)} %pad_add_fusion.refs_0_.info, bf16[128,1024]{1,0:T(8,128)(2,1)S(1)} %get-tuple-element.91.refs_1_.q_ref, ...), custom_call_target="tpu_custom_call" | custom-call | tf_op jit(solution)/shard_map/pallas_call | solution.py:45
  180.5 5.5 collective-permute-done.17.second
  221.9 11.3 %collective-permute-done.26.refs_3_ = bf16[512,640]{1,0:T(8,128)(2,1)S(1)} collective-permute-done((bf16[512,640]{1,0:T(8,128)(2,1)}, bf16[512,640]{1,0:T(8,128)(2,1)S(1)}, u32[]{:S(2)}, u32[]{:S(2)}) %collective-permute-start.26) | collective-permute-done | bytes 655392 | tf_op jit(solution)/shard_map/ppermute | solution.py:366
  244.0 11.7 %shard_map.210 = (bf16[128,960]{1,0:T(8,128)(2,1)S(1)}, f32[2,5,192,128]{3,2,1,0:T(8,128)S(1)}, bf16[2048,640]{1,0:T(8,128)(2,1)}, f32[128,960]{1,0:T(8,128)S(1)}, bf16[128,960]{1,0:T(8,128)(2,1)}) custom-call(s32[66]{0:T(128)S(1)} %pad_add_fusion.refs_0_.info, bf16[128,1024]{1,0:T(8,128)(2,1)S(1)} %copy-done.28, ...), custom_call_target="tpu_custom_call" | custom-call | tf_op jit(solution)/shard_map/pallas_call | solution.py:45
  267.0 5.2 collective-permute-done.33.second
  315.0 8.5 %collective-permute-start.41 = (bf16[128,960]{1,0:T(8,128)(2,1)S(1)}, bf16[128,960]{1,0:T(8,128)(2,1)S(1)}, u32[]{:S(2)}, u32[]{:S(2)}) collective-permute-start(bf16[128,960]{1,0:T(8,128)(2,1)S(1)} %get-tuple-element.116), channel_id=1, source_target_pairs={{0,1},{1,2},{2,3},{3,0},{4,5},{5,6},{6,7},{7,4},{8,9},{9,10},{10,1... | collective-permute-start | bytes 737288 | tf_op jit(solution)/shard_map/ppermute | solution.py:356
  332.4 23.5 %shard_map.219 = (f32[128,960]{1,0:T(8,128)S(1)}, bf16[128,960]{1,0:T(8,128)(2,1)S(1)}, f32[1,960]{1,0:T(1,128)S(1)}, bf16[128,960]{1,0:T(8,128)(2,1)S(1)}, bf16...) custom-call(s32[66]{0:T(128)S(1)} %pad_add_fusion.refs_0_.info, ...), custom_call_target="tpu_custom_call" | custom-call | tf_op jit(solution)/shard_map/pallas_call | solution.py:45
  367.1 8.3 %collective-permute-done.44 = bf16[512,640]{1,0:T(8,128)(2,1)} collective-permute-done((bf16[512,640]{1,0:T(8,128)(2,1)}, bf16[512,640]{1,0:T(8,128)(2,1)}, u32[]{:S(2)}, u32[]{:S(2)}) %collective-permute-start.44) | collective-permute-done | bytes 655392 | tf_op jit(solution)/shard_map/ppermute | solution.py:366
  375.4 15.2 %collective-permute-done.43 = bf16[512,640]{1,0:T(8,128)(2,1)} collective-permute-done((bf16[512,640]{1,0:T(8,128)(2,1)}, bf16[512,640]{1,0:T(8,128)(2,1)}, u32[]{:S(2)}, u32[]{:S(2)}) %collective-permute-start.43) | collective-permute-done | bytes 655392 | tf_op jit(solution)/shard_map/ppermute | solution.py:366
  483.9 5.2 collective-permute-done.53.p3
  489.1 23.5 %shard_map.225 = (f32[128,960]{1,0:T(8,128)S(1)}, bf16[128,960]{1,0:T(8,128)(2,1)S(1)}, f32[1,960]{1,0:T(1,128)S(1)}, bf16[128,960]{1,0:T(8,128)(2,1)S(1)}, bf16...) custom-call(s32[66]{0:T(128)S(1)} %pad_add_fusion.refs_0_.info, ...), custom_call_target="tpu_custom_call" | custom-call | tf_op jit(solution)/shard_map/pallas_call | solution.py:45
  524.6 7.4 %collective-permute-done.56 = bf16[512,640]{1,0:T(8,128)(2,1)} collective-permute-done((bf16[512,640]{1,0:T(8,128)(2,1)}, bf16[512,640]{1,0:T(8,128)(2,1)}, u32[]{:S(2)}, u32[]{:S(2)}) %collective-permute-start.56) | collective-permute-done | bytes 655392 | tf_op jit(solution)/shard_map/ppermute | solution.py:366
  532.0 13.7 %collective-permute-done.55 = bf16[512,640]{1,0:T(8,128)(2,1)} collective-permute-done((bf16[512,640]{1,0:T(8,128)(2,1)}, bf16[512,640]{1,0:T(8,128)(2,1)}, u32[]{:S(2)}, u32[]{:S(2)}) %collective-permute-start.55) | collective-permute-done | bytes 655392 | tf_op jit(solution)/shard_map/ppermute | solution.py:366
  552.4 5.6 collective-permute-done.57.k1
  608.6 5.1 add_convert_fusion
  638.8 7.4 %collective-permute-done.82 = bf16[4,60,961]{2,1,0:T(8,128)(2,1)} collective-permute-done((bf16[4,60,961]{2,1,0:T(8,128)(2,1)}, bf16[4,60,961]{2,1,0:T(8,128)(2,1)}, u32[]{:S(2)}, u32[]{:S(2)}) %collective-permute-start.82) | collective-permute-done | bytes 461312 | tf_op jit(solution)/shard_map/ppermute | solution.py:366
  646.2 5.2 collective-permute-start.106
  659.5 8.8 %collective-permute-start.86 = (bf16[60,961]{1,0:T(8,128)(2,1)S(1)}, bf16[60,961]{1,0:T(8,128)(2,1)S(1)}, u32[]{:S(2)}, u32[]{:S(2)}) collective-permute-start(bf16[60,961]{1,0:T(8,128)(2,1)S(1)} %get-tuple-element.313), channel_id=1, source_target_pairs={{0,8},{4,12},{8,0},{12,4},{16,24},{20,28},{24,16},{28,20},{32,40},... | collective-permute-start | bytes 345968 | tf_op jit(solution)/shard_map/ppermute | solution.py:361
  671.8 13.3 %collective-permute-done.106 = f32[40,960]{1,0:T(8,128)S(1)} collective-permute-done((f32[40,960]{1,0:T(8,128)S(1)}, f32[40,960]{1,0:T(8,128)S(1)}, u32[]{:S(2)}, u32[]{:S(2)}) %collective-permute-start.106) | collective-permute-done | bytes 153632 | tf_op jit(solution)/shard_map/ppermute | solution.py:572
  (709 shorter events, 417.9 us)
Async XLA Ops:
  7.2 67.9 %all-gather.4.cloned.1.call-start = ((), (), s32[]{:S(2)}) async-start(), calls=%async_computation | async-start | bytes 3993600 | tf_op jit(solution)/shard_map/all_gather | solution.py:416
  10.6 95.1 %all-gather.6.cloned.1.call-start = ((), (), s32[]{:S(2)}) async-start(), calls=%async_computation.1 | async-start | bytes 2457600 | tf_op jit(solution)/shard_map/all_gather | solution.py:417
  10.7 65.5 %collective-permute-start.2 = (bf16[2,240]{1,0:T(2,128)(2,1)S(1)}, bf16[2,240]{1,0:T(2,128)(2,1)S(1)}, u32[]{:S(2)}, u32[]{:S(2)}) collective-permute-start(bf16[2,240]{1,0:T(2,128)(2,1)S(1)} %pad_maximum_fusion.31), channel_id=1, source_target_pairs={{0,3},{1,0},{2,1},{3,2},{4,7},{5,4},{6,5},{7,6},{8,11},{9,8},{10,9... | collective-permute-start | bytes 2888 | tf_op jit(solution)/shard_map/ppermute | solution.py:356
  17.9 68.3 %collective-permute-start.14 = (bf16[240,1280]{1,0:T(8,128)(2,1)}, bf16[240,1280]{1,0:T(8,128)(2,1)}, u32[]{:S(2)}, u32[]{:S(2)}) collective-permute-start(bf16[240,1280]{1,0:T(8,128)(2,1)} %pad_maximum_fusion.14), channel_id=1, source_target_pairs={{0,3},{1,0},{2,1},{3,2},{4,7},{5,4},{6,5},{7,6},{8,11},{9,8},{10,9... | collective-permute-start | bytes 1843208 | tf_op jit(solution)/shard_map/ppermute | solution.py:356
  19.2 67.6 %collective-permute-start.13 = (bf16[240,1280]{1,0:T(8,128)(2,1)}, bf16[240,1280]{1,0:T(8,128)(2,1)}, u32[]{:S(2)}, u32[]{:S(2)}) collective-permute-start(bf16[240,1280]{1,0:T(8,128)(2,1)} %pad_maximum_fusion.13), channel_id=1, source_target_pairs={{0,2},{1,3},{2,0},{3,1},{4,6},{5,7},{6,4},{7,5},{8,10},{9,11},{10,... | collective-permute-start | bytes 1843208 | tf_op jit(solution)/shard_map/ppermute | solution.py:356
  20.1 66.7 %collective-permute-start.12 = (bf16[240,1280]{1,0:T(8,128)(2,1)}, bf16[240,1280]{1,0:T(8,128)(2,1)}, u32[]{:S(2)}, u32[]{:S(2)}) collective-permute-start(bf16[240,1280]{1,0:T(8,128)(2,1)} %pad_maximum_fusion.12), channel_id=1, source_target_pairs={{0,1},{1,2},{2,3},{3,0},{4,5},{5,6},{6,7},{7,4},{8,9},{9,10},{10,1... | collective-permute-start | bytes 1843208 | tf_op jit(solution)/shard_map/ppermute | solution.py:356
  91.0 86.1 %collective-permute-start.15 = (bf16[960,1280]{1,0:T(8,128)(2,1)}, bf16[960,1280]{1,0:T(8,128)(2,1)}, u32[]{:S(2)}, u32[]{:S(2)}) collective-permute-start(bf16[960,1280]{1,0:T(8,128)(2,1)} %pad_maximum_fusion.5), channel_id=1, source_target_pairs={{0,64},{64,0},{1,65},{65,1},{2,66},{66,2},{3,67},{67,3},{4,68},{68... | collective-permute-start | bytes 7372808 | tf_op jit(solution)/shard_map/ppermute | solution.py:370
  220.3 40.6 %collective-permute-start.63 = (bf16[128,1920]{1,0:T(8,128)(2,1)}, bf16[128,1920]{1,0:T(8,128)(2,1)}, u32[]{:S(2)}, u32[]{:S(2)}) collective-permute-start(bf16[128,1920]{1,0:T(8,128)(2,1)} %pad_maximum_fusion.17), channel_id=1, source_target_pairs={{0,3},{1,0},{2,1},{3,2},{4,7},{5,4},{6,5},{7,6},{8,11},{9,8},{10,9... | collective-permute-start | bytes 1474568 | tf_op jit(solution)/shard_map/ppermute | solution.py:356
  221.4 42.7 %collective-permute-start.62 = (bf16[128,1920]{1,0:T(8,128)(2,1)}, bf16[128,1920]{1,0:T(8,128)(2,1)}, u32[]{:S(2)}, u32[]{:S(2)}) collective-permute-start(bf16[128,1920]{1,0:T(8,128)(2,1)} %pad_maximum_fusion.17), channel_id=1, source_target_pairs={{0,2},{1,3},{2,0},{3,1},{4,6},{5,7},{6,4},{7,5},{8,10},{9,11},{10,... | collective-permute-start | bytes 1474568 | tf_op jit(solution)/shard_map/ppermute | solution.py:356
  292.7 64.8 %collective-permute-start.34 = (bf16[128,960]{1,0:T(8,128)(2,1)S(1)}, bf16[128,960]{1,0:T(8,128)(2,1)}, u32[]{:S(2)}, u32[]{:S(2)}) collective-permute-start(bf16[128,960]{1,0:T(8,128)(2,1)S(1)} %get-tuple-element.108), channel_id=1, source_target_pairs={{0,1},{1,2},{2,3},{3,0},{4,5},{5,6},{6,7},{7,4},{8,9},{9,10},{10,1... | collective-permute-start | bytes 737288 | tf_op jit(solution)/shard_map/ppermute | solution.py:356
  307.0 55.0 %collective-permute-start.32 = (bf16[128,960]{1,0:T(8,128)(2,1)S(1)}, bf16[128,960]{1,0:T(8,128)(2,1)S(1)}, u32[]{:S(2)}, u32[]{:S(2)}) collective-permute-start(bf16[128,960]{1,0:T(8,128)(2,1)S(1)} %get-tuple-element.107), channel_id=1, source_target_pairs={{0,2},{1,3},{2,0},{3,1},{4,6},{5,7},{6,4},{7,5},{8,10},{9,11},{10,... | collective-permute-start | bytes 737288 | tf_op jit(solution)/shard_map/ppermute | solution.py:356
  310.7 51.3 %collective-permute-start.30 = (bf16[128,960]{1,0:T(8,128)(2,1)S(1)}, bf16[128,960]{1,0:T(8,128)(2,1)S(1)}, u32[]{:S(2)}, u32[]{:S(2)}) collective-permute-start(bf16[128,960]{1,0:T(8,128)(2,1)S(1)} %get-tuple-element.106), channel_id=1, source_target_pairs={{0,3},{1,0},{2,1},{3,2},{4,7},{5,4},{6,5},{7,6},{8,11},{9,8},{10,9... | collective-permute-start | bytes 737288 | tf_op jit(solution)/shard_map/ppermute | solution.py:356
  329.6 68.1 %collective-permute-start.98 = (bf16[640,480]{0,1:T(8,128)(2,1)}, bf16[640,480]{0,1:T(8,128)(2,1)}, u32[]{:S(2)}, u32[]{:S(2)}) collective-permute-start(bf16[640,480]{0,1:T(8,128)(2,1)} %select_convert_fusion.2), channel_id=1, source_target_pairs={{0,64},{64,0},{1,65},{65,1},{2,66},{66,2},{3,67},{67,3},{4,68},{68... | collective-permute-start | bytes 1843208 | tf_op jit(solution)/shard_map/ppermute | solution.py:370
  357.5 33.1 %collective-permute-start.43 = (bf16[512,640]{1,0:T(8,128)(2,1)}, bf16[512,640]{1,0:T(8,128)(2,1)}, u32[]{:S(2)}, u32[]{:S(2)}) collective-permute-start(bf16[512,640]{1,0:T(8,128)(2,1)} %get-tuple-element.122), channel_id=1, source_target_pairs={{0,48},{4,52},{8,56},{12,60},{16,0},{20,4},{24,8},{28,12},{32,16},... | collective-permute-start | bytes 1966088 | tf_op jit(solution)/shard_map/ppermute | solution.py:366
  364.3 241.4 %collective-permute-start.35 = (f32[128,960]{1,0:T(8,128)}, f32[128,960]{1,0:T(8,128)}, u32[]{:S(2)}, u32[]{:S(2)}) collective-permute-start(f32[128,960]{1,0:T(8,128)} %get-tuple-element.242), channel_id=1, source_target_pairs={{0,64},{64,0},{1,65},{65,1},{2,66},{66,2},{3,67},{67,3},{4,68},{68... | collective-permute-start | bytes 1474568 | tf_op jit(solution)/shard_map/ppermute | solution.py:370
  403.9 38.5 %collective-permute-start.101 = (bf16[4,40,480]{2,1,0:T(8,128)(2,1)}, bf16[4,40,480]{2,1,0:T(8,128)(2,1)}, u32[]{:S(2)}, u32[]{:S(2)}) collective-permute-start(bf16[4,40,480]{2,1,0:T(8,128)(2,1)} %get-tuple-element.283), channel_id=1, source_target_pairs={{0,32},{4,36},{8,40},{12,44},{16,48},{20,52},{24,56},{28,60},{32,0... | collective-permute-start | bytes 460808 | tf_op jit(solution)/shard_map/ppermute | solution.py:366
  406.6 37.6 %collective-permute-start.100 = (bf16[4,40,480]{2,1,0:T(8,128)(2,1)}, bf16[4,40,480]{2,1,0:T(8,128)(2,1)}, u32[]{:S(2)}, u32[]{:S(2)}) collective-permute-start(bf16[4,40,480]{2,1,0:T(8,128)(2,1)} %get-tuple-element.284), channel_id=1, source_target_pairs={{0,48},{4,52},{8,56},{12,60},{16,0},{20,4},{24,8},{28,12},{32,16},... | collective-permute-start | bytes 460808 | tf_op jit(solution)/shard_map/ppermute | solution.py:366
  409.3 36.2 %collective-permute-start.99 = (bf16[4,40,480]{2,1,0:T(8,128)(2,1)}, bf16[4,40,480]{2,1,0:T(8,128)(2,1)}, u32[]{:S(2)}, u32[]{:S(2)}) collective-permute-start(bf16[4,40,480]{2,1,0:T(8,128)(2,1)} %get-tuple-element.282), channel_id=1, source_target_pairs={{0,16},{4,20},{8,24},{12,28},{16,32},{20,36},{24,40},{28,44},{32,4... | collective-permute-start | bytes 460808 | tf_op jit(solution)/shard_map/ppermute | solution.py:366
  469.0 139.6 %collective-permute-start.80 = (bf16[960,961]{1,0:T(8,128)(2,1)}, bf16[960,961]{1,0:T(8,128)(2,1)}, u32[]{:S(2)}, u32[]{:S(2)}) collective-permute-start(bf16[960,961]{1,0:T(8,128)(2,1)} %select_convert_fusion), channel_id=1, source_target_pairs={{0,64},{64,0},{1,65},{65,1},{2,66},{66,2},{3,67},{67,3},{4,68},{68... | collective-permute-start | bytes 5535368 | tf_op jit(solution)/shard_map/ppermute | solution.py:370
  590.5 32.6 %collective-permute-start.67 = (bf16[960,961]{1,0:T(8,128)(2,1)}, bf16[960,961]{1,0:T(8,128)(2,1)}, u32[]{:S(2)}, u32[]{:S(2)}) collective-permute-start(bf16[960,961]{1,0:T(8,128)(2,1)} %select_convert_fusion.1), channel_id=1, source_target_pairs={{0,64},{64,0},{1,65},{65,1},{2,66},{66,2},{3,67},{67,3},{4,68},{68... | collective-permute-start | bytes 5535368 | tf_op jit(solution)/shard_map/ppermute | solution.py:370
  634.0 34.4 %collective-permute-start.69 = (bf16[4,60,961]{2,1,0:T(8,128)(2,1)S(1)}, bf16[4,60,961]{2,1,0:T(8,128)(2,1)S(1)}, u32[]{:S(2)}, u32[]{:S(2)}) collective-permute-start(bf16[4,60,961]{2,1,0:T(8,128)(2,1)S(1)} %get-tuple-element.267), channel_id=1, source_target_pairs={{0,48},{4,52},{8,56},{12,60},{16,0},{20,4},{24,8},{28,12},{32,16},... | collective-permute-start | bytes 1383848 | tf_op jit(solution)/shard_map/ppermute | solution.py:366
  637.1 33.2 %collective-permute-start.68 = (bf16[4,60,961]{2,1,0:T(8,128)(2,1)S(1)}, bf16[4,60,961]{2,1,0:T(8,128)(2,1)S(1)}, u32[]{:S(2)}, u32[]{:S(2)}) collective-permute-start(bf16[4,60,961]{2,1,0:T(8,128)(2,1)S(1)} %get-tuple-element.265), channel_id=1, source_target_pairs={{0,16},{4,20},{8,24},{12,28},{16,32},{20,36},{24,40},{28,44},{32,4... | collective-permute-start | bytes 1383848 | tf_op jit(solution)/shard_map/ppermute | solution.py:366
  646.2 38.9 %collective-permute-start.106 = (f32[40,960]{1,0:T(8,128)S(1)}, f32[40,960]{1,0:T(8,128)S(1)}, u32[]{:S(2)}, u32[]{:S(2)}) collective-permute-start(f32[40,960]{1,0:T(8,128)S(1)} %copy-done.130), channel_id=1, source_target_pairs={{0,0},{1,16},{2,32},{3,48},{4,1},{5,17},{6,33},{7,49},{8,2},{9,18}... | collective-permute-start | bytes 460808 | tf_op jit(solution)/shard_map/ppermute | solution.py:572
  651.4 45.3 %collective-permute-start.60 = (f32[128,960]{1,0:T(8,128)}, f32[128,960]{1,0:T(8,128)}, u32[]{:S(2)}, u32[]{:S(2)}) collective-permute-start(f32[128,960]{1,0:T(8,128)} %broadcast_select_fusion.6), channel_id=1, source_target_pairs={{0,64},{64,0},{1,65},{65,1},{2,66},{66,2},{3,67},{67,3},{4,68},{68... | collective-permute-start | bytes 1474568 | tf_op jit(solution)/shard_map/ppermute | solution.py:370
  (229 other events, 2796.5 us)
Sparse Core Ops, SparseCore 0:
  10.7 64.3 all-gather.3
  76.8 28.8 all-gather.5

commit v2 on v1

v2 whole, which is shorter than its diff:
```python
import math
from functools import partial

import jax
import jax.numpy as jnp
from jax import lax
from jax.experimental import pallas as pl
from jax.experimental.pallas import tpu as pltpu
from jax.sharding import PartitionSpec as P

HEADS = 15
KV_HEADS = 5
HEAD = 64
GROUP = HEADS // KV_HEADS
D = 960
FF = 2560
KW = KV_HEADS * HEAD
ROWS = 128
BLK = 64
SEQ = 2048
CHUNK = 256
STEPS = 9
EPS = 1e-05
ROPE_BASE = 10000.0
BF = jnp.bfloat16
F32 = jnp.float32
QP = 1024
HALF = 896
NEG = -1e30
VMEM_BYTES = 48 * 1024 * 1024

NN = (((1,), (0,)), ((), ()))
NT = (((1,), (1,)), ((), ()))
TN = (((0,), (0,)), ((), ()))


def dot(left, right, dims=NN):
    return lax.dot_general(left, right, dims, preferred_element_type=F32)


def call(body, outs, micros, scratch=(), smem=0):
    def run(*args, after=()):
        count = len(args)
        in_specs = [
            pl.BlockSpec(memory_space=pltpu.SMEM if i < smem else pltpu.VMEM) for i in range(count)
        ] + [pl.BlockSpec(memory_space=pl.ANY) for _ in after]

        def inner(*refs):
            body(*refs[:count], *refs[count + len(after) :])

        out = pl.pallas_call(
            inner,
            in_specs=in_specs,
            out_specs=[pl.BlockSpec(memory_space=pltpu.VMEM) for _ in outs],
            out_shape=[jax.ShapeDtypeStruct(s, t) for s, t in outs],
            scratch_shapes=list(scratch),
            cost_estimate=pl.CostEstimate(
                flops=int(micros * 1.1e9), bytes_accessed=int(micros * 3.6e6), transcendentals=0
            ),
            compiler_params=pltpu.CompilerParams(vmem_limit_bytes=VMEM_BYTES),
        )(*args, *after)
        return out

    return run


def lane(shape):
    return lax.broadcasted_iota(jnp.int32, shape, 1)


def normalise(x, gain):
    return x * lax.rsqrt(jnp.mean(x * x, axis=-1, keepdims=True) + EPS) * gain


def norm_back(x, gain, dy):
    r = lax.rsqrt(jnp.mean(x * x, axis=-1, keepdims=True) + EPS)
    cdy = gain * dy
    dx = r * cdy - x * (r * r * r) * jnp.mean(x * cdy, axis=-1, keepdims=True)
    dc = jnp.sum(dy * x * r, axis=0, keepdims=True)
    return dx, dc


def spin(tile, cosine, sine):
    first = (lane(tile.shape) % HEAD) < HEAD // 2
    swapped = jnp.where(first, pltpu.roll(tile, 96, 1), pltpu.roll(tile, 32, 1))
    return tile * cosine + swapped * sine


def project_body(count):
    def body(*refs):
        info, base = refs[:2]
        parts = refs[2 : 2 + count]
        (gain, own, other, cosine, sine, x_out, normed_out, q_out, kv_out, halves) = refs[2 + count :]
        side = info[0]
        x = base[...]
        for part in parts:
            x = x + part[...].astype(F32)
        x_out[...] = x
        normed = normalise(x, gain[...]).astype(BF)
        normed_out[...] = normed
        cos, sin = cosine[...], sine[...]
        halves[side] = dot(normed, own[:, :HALF])
        halves[1 - side] = dot(normed, other[:, :HALF])
        for j in range(8):
            tile = halves[0, :, j * 128 : (j + 1) * 128] if j < 7 else halves[1, :, 0:128]
            q_out[:, j * 128 : (j + 1) * 128] = (spin(tile, cos, sin) * (HEAD**-0.5)).astype(BF)
        for g in range(KV_HEADS):
            tile = halves[1, :, (g + 1) * 128 : (g + 2) * 128]
            tile = jnp.where(lane(tile.shape) < HEAD, spin(tile, cos, sin), tile)
            kv_out[:, g * 128 : (g + 1) * 128] = tile.astype(BF)

    return body


def project(info, base, parts, gain, weight, cosine, sine, after=()):
    outs = [((ROWS, D), F32), ((ROWS, D), BF), ((ROWS, QP), BF), ((ROWS, 2 * KW), BF)]
    scratch = [pltpu.VMEM((2, ROWS, HALF), F32)]
    return call(project_body(len(parts)), outs, 2.5, scratch, smem=1)(
        info, base, *parts, gain, *weight, cosine, sine, after=after
    )


def step_place(info, t):
    first, second = info[2], info[3]
    count = first // 4 + 1
    early = t < count
    block = jnp.where(early, 0, 1)
    chunk = jnp.where(early, t, t - count)
    place = jnp.where(early, first, second)
    return block, chunk, place


def causal(place, chunk):
    rows = lax.broadcasted_iota(jnp.int32, (BLK, CHUNK), 0) + place * BLK
    cols = lax.broadcasted_iota(jnp.int32, (BLK, CHUNK), 1) + chunk * CHUNK
    one = rows >= cols
    return jnp.concatenate([one] * GROUP, axis=0)


def head_tile(ref, block, head, upper):
    j = head // 2
    tile = ref[block * BLK : (block + 1) * BLK, j * 128 : (j + 1) * 128].astype(F32)
    if (head % 2 == 1) != upper:
        tile = pltpu.roll(tile, 64, 1)
    keep = (lane(tile.shape) >= HEAD) if upper else (lane(tile.shape) < HEAD)
    return jnp.where(keep, tile, 0.0)


def attend_body(count):
    def body(*refs):
        info, q_ref = refs[0], refs[1]
        pieces = refs[2 : 2 + count]
        (own, other, x_ref, gain, mixed_out, lse_out, kvs, resid_out, second_out) = refs[
            2 + count : 11 + count
        ]
        qh, top, total, acc, halves = refs[11 + count :]
        side = info[0]
        number = 0
        for piece in pieces:
            for b in range(piece.shape[0] // BLK):
                at = pl.multiple_of(info[4 + number] * BLK, BLK)
                kvs[pl.ds(at, BLK), :] = piece[b * BLK : (b + 1) * BLK, :]
                number += 1
        for i in range(2):
            for g in range(KV_HEADS):
                for r in range(GROUP):
                    qh[i, g, r * BLK : (r + 1) * BLK, :] = head_tile(
                        q_ref, i, g * GROUP + r, False
                    ).astype(BF)
        top[...] = jnp.full(top.shape, NEG, F32)
        total[...] = jnp.zeros(total.shape, F32)
        acc[...] = jnp.zeros(acc.shape, F32)

        def step(t, carry):
            block, chunk, place = step_place(info, t)
            allowed = causal(place, chunk)
            at = pl.multiple_of(chunk * CHUNK, CHUNK)
            for g in range(KV_HEADS):
                keys = kvs[pl.ds(at, CHUNK), g * 128 : (g + 1) * 128]
                scores = dot(qh[block, g], keys, NT)
                scores = jnp.where(allowed, scores, NEG)
                old = top[block, g]
                new = jnp.maximum(old, jnp.max(scores, axis=1, keepdims=True))
                probs = jnp.exp(scores - jnp.concatenate([new, new], axis=1))
                shrink = jnp.exp(old - new)
                top[block, g] = new
                total[block, g] = shrink * total[block, g] + jnp.sum(probs, axis=1, keepdims=True)
                acc[block, g] = shrink * acc[block, g] + dot(probs.astype(BF), keys)
            return carry

        lax.fori_loop(0, STEPS, step, 0)
        for i in range(2):
            heads = []
            for g in range(KV_HEADS):
                sums = total[i, g]
                result = acc[i, g] / sums
                lse_out[i, g] = top[i, g] + jnp.log(sums)
                for r in range(GROUP):
                    heads.append(result[r * BLK : (r + 1) * BLK, :])
            for j in range(8):
                low = pltpu.roll(heads[2 * j], 64, 1)
                rows = slice(i * BLK, (i + 1) * BLK)
                if j < 7:
                    tile = jnp.where(lane(low.shape) < HEAD, low, heads[2 * j + 1])
                    mixed_out[rows, j * 128 : (j + 1) * 128] = tile.astype(BF)
                else:
                    mixed_out[rows, 896:960] = low[:, :64].astype(BF)
        halves[side] = dot(mixed_out[...], own[:, HALF:])
        halves[1 - side] = dot(mixed_out[...], other[:, HALF:])
        resid = x_ref[...] + jnp.concatenate([halves[0], halves[1]], axis=1)
        resid_out[...] = resid
        second_out[...] = normalise(resid, gain[...]).astype(BF)

    return body


def attend(info, q, pieces, wo, x, gain, after=()):
    outs = [
        ((ROWS, D), BF),
        ((2, KV_HEADS, GROUP * BLK, 128), F32),
        ((SEQ, 2 * KW), BF),
        ((ROWS, D), F32),
        ((ROWS, D), BF),
    ]
    shape = (2, KV_HEADS, GROUP * BLK, 128)
    scratch = [pltpu.VMEM(shape, BF)] + [pltpu.VMEM(shape, F32)] * 3
    scratch.append(pltpu.VMEM((2, ROWS, D // 2), F32))
    return call(attend_body(len(pieces)), outs, 12.0, scratch, smem=1)(
        info, q, *pieces, *wo, x, gain, after=after
    )


def feed_body(layer, info, second, own, other, wd, gu_out, hidden_out, part_out):
    side = info[0]
    columns = slice(layer * FF // 4, (layer + 1) * FF // 4)
    gu_out[side] = dot(second[...], own[:, columns])
    gu_out[1 - side] = dot(second[...], other[:, columns])
    gate, up = gu_out[0], gu_out[1]
    hidden = (gate / (1.0 + jnp.exp(-gate)) * up).astype(BF)
    hidden_out[...] = hidden
    part_out[...] = dot(hidden, wd[...]).astype(BF)


def feed(layer, info, second, wgu, wd):
    outs = [((2, ROWS, FF // 4), F32), ((ROWS, FF // 4), BF), ((ROWS, D), BF)]
    body = partial(feed_body, layer)
    return call(body, outs, 1.0, smem=1)(info, second, *wgu, wd)


def feed_back_body(layer, info, grad_low, gu, own, other, wd, dgu_out, part_out):
    side = info[0]
    columns = slice(layer * FF // 4, (layer + 1) * FF // 4)
    d_hidden = dot(grad_low[...], wd[...], NT)
    gate, up = gu[0], gu[1]
    sig = 1.0 / (1.0 + jnp.exp(-gate))
    d_gate = d_hidden * up * sig * (1.0 + gate * (1.0 - sig))
    d_up = d_hidden * gate * sig
    dgu_out[0] = d_gate.astype(BF)
    dgu_out[1] = d_up.astype(BF)
    part = dot(dgu_out[side], own[:, columns], NT) + dot(dgu_out[1 - side], other[:, columns], NT)
    part_out[...] = part.astype(BF)


def feed_back(layer, info, grad_low, gu, wgu, wd):
    outs = [((2, ROWS, FF // 4), BF), ((ROWS, D), BF)]
    body = partial(feed_back_body, layer)
    return call(body, outs, 1.3, smem=1)(info, grad_low, gu, *wgu, wd)


def attend_back_body(
    info, p0, p1, p2, p3, grad, resid, gain, own, other, normed, mixed, q_ref, lse, kvs, cosine, sine,
    d_resid_out, d_low_out, dc_out, dq_out, ahead_out, o0, o1, o2, o3,
    qd, delta, dq, dkv, dm, mx, halves,
):
    d_second = p0[...].astype(F32) + p1[...].astype(F32) + p2[...].astype(F32) + p3[...].astype(F32)
    dx, dc = norm_back(resid[...], gain[...], d_second)
    dc_out[...] = dc
    d_resid = grad[...] + dx
    d_resid_out[...] = d_resid
    low = d_resid.astype(BF)
    d_low_out[...] = low
    side = info[0]
    halves[0] = d_resid[:, : D // 2].astype(BF)
    halves[1] = d_resid[:, D // 2 :].astype(BF)
    d_mixed = dot(halves[side], own[:, HALF:], NT) + dot(halves[1 - side], other[:, HALF:], NT)
    ahead_out[:, :D] = normed[...]
    ahead_out[:, QP : QP + D] = mixed[...]
    ahead_out[:, D:QP] = jnp.zeros((ROWS, QP - D), BF)
    dm[:, :D] = d_mixed.astype(BF)
    dm[:, D:] = jnp.zeros((ROWS, QP - D), BF)
    mx[:, :D] = mixed[...]
    mx[:, D:] = jnp.zeros((ROWS, QP - D), BF)
    span = GROUP * BLK
    for i in range(2):
        for g in range(KV_HEADS):
            for r in range(GROUP):
                head = g * GROUP + r
                there = slice(r * BLK, (r + 1) * BLK)
                qd[i, g, there, :] = head_tile(q_ref, i, head, False).astype(BF)
                do = head_tile(dm, i, head, True)
                qd[i, g, span + r * BLK : span + (r + 1) * BLK, :] = do.astype(BF)
                dots = jnp.sum(do * head_tile(mx, i, head, True), axis=1, keepdims=True)
                delta[i, g, there, :] = jnp.broadcast_to(dots, (BLK, 128))
    dq[...] = jnp.zeros(dq.shape, F32)
    dkv[...] = jnp.zeros(dkv.shape, F32)

    def step(t, carry):
        block, chunk, place = step_place(info, t)
        allowed = causal(place, chunk)
        at = pl.multiple_of(chunk * CHUNK, CHUNK)
        for g in range(KV_HEADS):
            keys = kvs[pl.ds(at, CHUNK), g * 128 : (g + 1) * 128]
            both = dot(qd[block, g], keys, NT)
            scores, d_probs = both[:span], both[span:]
            total = lse[block, g]
            probs = jnp.exp(
                jnp.where(allowed, scores, NEG) - jnp.concatenate([total, total], axis=1)
            )
            shift = delta[block, g]
            d_scores = probs * (d_probs - jnp.concatenate([shift, shift], axis=1))
            d_low = d_scores.astype(BF)
            dq[block, g] += dot(d_low, keys)
            stacked = jnp.concatenate([d_low, probs.astype(BF)], axis=0)
            dkv[pl.ds(at, CHUNK), g * 128 : (g + 1) * 128] += dot(stacked, qd[block, g], TN)
        return carry

    lax.fori_loop(0, STEPS, step, 0)
    for i in range(2):
        rows = slice(i * BLK, (i + 1) * BLK)
        cos, sin = cosine[rows, :], sine[rows, :]
        heads = []
        for g in range(KV_HEADS):
            for r in range(GROUP):
                heads.append(dq[i, g, r * BLK : (r + 1) * BLK, :] * (HEAD**-0.5))
        for j in range(8):
            if j < 7:
                high = pltpu.roll(heads[2 * j + 1], 64, 1)
                tile = jnp.where(lane(high.shape) < HEAD, heads[2 * j], high)
                dq_out[rows, j * 128 : (j + 1) * 128] = spin(tile, cos, -sin).astype(BF)
            else:
                dq_out[rows, 896:960] = spin(heads[14], cos, -sin)[:, :64].astype(BF)
    number = 0
    for out in (o0, o1, o2, o3):
        for b in range(out.shape[0] // BLK):
            at = pl.multiple_of(info[36 + number] * BLK, BLK)
            out[b * BLK : (b + 1) * BLK, :] = dkv[pl.ds(at, BLK), :].astype(BF)
            number += 1


def attend_back(info, parts, grad, resid, gain, wo, normed, mixed, q, lse, kvs, cosine, sine, after=()):
    outs = [
        ((ROWS, D), F32),
        ((ROWS, D), BF),
        ((1, D), F32),
        ((ROWS, D), BF),
        ((ROWS, QP + D), BF),
    ] + [((4 * ROWS, 2 * KW), BF)] * 4
    shape = (2, KV_HEADS, GROUP * BLK, 128)
    scratch = [
        pltpu.VMEM((2, KV_HEADS, 2 * GROUP * BLK, 128), BF),
        pltpu.VMEM(shape, F32),
        pltpu.VMEM(shape, F32),
        pltpu.VMEM((SEQ, 2 * KW), F32),
        pltpu.VMEM((ROWS, QP), BF),
        pltpu.VMEM((ROWS, QP), BF),
        pltpu.VMEM((2, ROWS, D // 2), BF),
    ]
    return call(attend_back_body, outs, 24.0, scratch, smem=1)(
        info, *parts, grad, resid, gain, *wo, normed, mixed, q, lse, kvs, cosine, sine, after=after
    )


def project_back_body(
    info, k0, k1, k2, k3, dq, d_resid, d_low, x_ref, gain, own, other, cosine, sine,
    cut_out, grad_out, dc_out, halves, dkv,
):
    side, z = info[0], info[1]
    sums = k0[...].astype(F32) + k1[...].astype(F32) + k2[...].astype(F32) + k3[...].astype(F32)
    cos, sin = cosine[...], -sine[...]
    halves[0] = dq[:, :HALF]
    halves[1] = jnp.zeros((ROWS, HALF), BF)
    halves[1, :, :HEAD] = dq[:, HALF:]
    for g in range(KV_HEADS):
        tile = sums[:, g * 128 : (g + 1) * 128]
        tile = jnp.where(lane(tile.shape) < HEAD, spin(tile, cos, sin), tile)
        dkv[:, g * 128 : (g + 1) * 128] = tile
        halves[1, :, (g + 1) * 128 : (g + 2) * 128] = tile.astype(BF)
    d_normed = dot(halves[side], own[:, :HALF], NT) + dot(halves[1 - side], other[:, :HALF], NT)
    dx, dc = norm_back(x_ref[...], gain[...], d_normed)
    dc_out[...] = dc
    grad_out[...] = d_resid[...] + dx
    query, low = dq[...].astype(F32), d_low[...].astype(F32)
    quarters = (
        query[:, :640],
        jnp.concatenate([query[:, 640:], dkv[:, :320]], axis=1),
        jnp.concatenate([dkv[:, 320:], low[:, :320]], axis=1),
        low[:, 320:],
    )
    for place in range(4):
        cut_out[(place + 4 - z) % 4] = quarters[place].astype(BF)


def project_back(info, pieces, dq, d_resid, d_low, x, gain, weight, cosine, sine, after=()):
    outs = [((4, ROWS, 640), BF), ((ROWS, D), F32), ((1, D), F32)]
    scratch = [pltpu.VMEM((2, ROWS, HALF), BF), pltpu.VMEM((ROWS, 2 * KW), F32)]
    return call(project_back_body, outs, 3.2, scratch, smem=1)(
        info, *pieces, dq, d_resid, d_low, x, gain, *weight, cosine, sine, after=after
    )


def slot_of(info, c, given):
    place = info[68 + c]
    return (place % 4) * 4 + place // 4 if given else place


def feed_grads_body(*refs):
    info = refs[0]
    seconds, dgus, hiddens, lows = (refs[1 + 4 * i : 5 + 4 * i] for i in range(4))
    keep_out, give_out, left, right, hidden, low, acc, down, group = refs[17:]
    side = info[0]
    for k in range(4):
        rows = slice(k * ROWS, (k + 1) * ROWS)
        left[rows, :] = seconds[k][...]
        hidden[rows, :] = hiddens[k][...]
        low[rows, :] = lows[k][...]
        for h in range(2):
            right[h, rows, :] = dgus[k][h]
    down[...] = dot(hidden[...], low[...], TN)
    group[90:, :] = jnp.zeros((6, 640), F32)
    for turn, out in ((0, keep_out), (1, give_out)):
        half = side if turn == 0 else 1 - side
        acc[...] = dot(left[...], right[half], TN)
        for h in range(2):

            @pl.when(half == h)
            def _():
                for c in range(16):
                    at = 40 * c + 20 * h
                    group[:60, :] = acc[60 * c : 60 * c + 60, :]
                    group[60:80, :] = down[at : at + 20, :640]
                    group[80:90, :320] = down[at : at + 10, 640:]
                    group[80:90, 320:] = down[at + 10 : at + 20, 640:]
                    out[slot_of(info, c, turn)] = group[...].astype(BF)


def feed_grads(info, seconds, dgus, hiddens, lows, after=()):
    rows = 4 * ROWS
    scratch = [
        pltpu.VMEM((rows, D), BF),
        pltpu.VMEM((2, rows, 640), BF),
        pltpu.VMEM((rows, 640), BF),
        pltpu.VMEM((rows, D), BF),
        pltpu.VMEM((D, 640), F32),
        pltpu.VMEM((640, D), F32),
        pltpu.VMEM((96, 640), F32),
    ]
    return call(feed_grads_body, [((16, 96, 640), BF)] * 2, 6.5, scratch, smem=1)(
        info, *seconds, *dgus, *hiddens, *lows, after=after
    )


def attend_grads_body(*refs):
    info = refs[0]
    mines, aheads = refs[1:5], refs[5:9]
    dc_one, dc_two, keep_out, give_out, lhs, mine, acc, group = refs[9:]
    side, z = info[0], info[1]
    for k in range(4):
        rows = slice(k * ROWS, (k + 1) * ROWS)
        for h in range(2):
            mine[h, rows, :] = mines[k][:, h * 320 : (h + 1) * 320].astype(F32).astype(BF)
        lhs[0, rows, :] = aheads[k][:, :D]
        lhs[1, rows, :] = aheads[k][:, QP:]
    group[60:, :] = jnp.zeros((4, 384), F32)
    for turn, out in ((0, keep_out), (1, give_out)):
        h = side if turn == 0 else 1 - side
        which = jnp.where(z + h >= 3, 1, 0)
        acc[:, :320] = dot(lhs[which], mine[h], TN)
        gain_row = jnp.where(h == 0, dc_one[...], dc_two[...])
        first = lax.broadcasted_iota(jnp.int32, (8, D), 0) == 0
        spread = jnp.where(first, jnp.broadcast_to(gain_row, (8, D)), 0.0)
        acc[:, 320:] = dot(spread, jnp.ones((8, 64), F32), TN)
        for c in range(16):
            group[:60, :] = acc[60 * c : 60 * c + 60, :]
            out[slot_of(info, c, turn)] = group[...].astype(BF)


def attend_grads(info, mines, aheads, dc_one, dc_two):
    rows = 4 * ROWS
    scratch = [
        pltpu.VMEM((2, rows, D), BF),
        pltpu.VMEM((2, rows, 320), BF),
        pltpu.VMEM((D, 384), F32),
        pltpu.VMEM((64, 384), F32),
    ]
    return call(attend_grads_body, [((16, 64, 384), BF)] * 2, 3.0, scratch, smem=1)(
        info, *mines, *aheads, dc_one, dc_two
    )


def finish_body(info, p0, p1, p2, p3, *outs):
    n1, gq, gk, gv, go, n2, gate, up = outs[:8]
    placed = outs[8]
    z = info[1]
    for k, piece in enumerate((p0, p1, p2, p3)):
        placed[(z + 4 - k) % 4] = piece[...]
    att = []
    for place in range(4):
        gate[:, 0, place * 640 : (place + 1) * 640] = placed[place, :, :640]
        up[:, 0, place * 640 : (place + 1) * 640] = placed[place, :, 1024:1664]
        att += [placed[place, :, 640:960], placed[place, :, 1664:1984]]
    gq[:, 0, :] = jnp.concatenate(att[:3], axis=1)
    go[:, 0, :] = jnp.concatenate(att[5:], axis=1)
    both = jnp.concatenate(att[3:5], axis=1)
    gk[:, 0, :] = jnp.concatenate([both[:, g * 128 : g * 128 + 64] for g in range(KV_HEADS)], axis=1)
    gv[:, 0, :] = jnp.concatenate([both[:, g * 128 + 64 : g * 128 + 128] for g in range(KV_HEADS)], axis=1)
    total = placed[0] + placed[1] + placed[2] + placed[3]
    n1[...] = total[:, 960:1024]
    n2[...] = total[:, 1984:2048]


def finish(info, pieces):
    widths = [D, KW, KW, D, FF, FF]
    shapes = [(15, 1, width) for width in widths]
    shapes = [(15, 64)] + shapes[:4] + [(15, 64)] + shapes[4:]
    return call(
        finish_body, [(s, F32) for s in shapes], 1.5, [pltpu.VMEM((4, 15, 2048), F32)], smem=1
    )(info, *pieces)


def z_shift(value, steps):
    return lax.ppermute(value, "wsh", [(i, (i + steps) % 4) for i in range(4)])


def ctx_shift(value, steps, core_along_x):
    pairs = []
    for core in range(2):
        for y in range(4):
            for x in range(4):
                to = (y, (x + steps) % 4) if core == core_along_x else ((y + steps) % 4, x)
                pairs.append((core * 16 + y * 4 + x, core * 16 + to[0] * 4 + to[1]))
    return lax.ppermute(value, ("section", "ctx"), pairs)


def gather_shift(value, steps):
    return ctx_shift(value, steps, 0)


def reduce_shift(value, steps):
    return ctx_shift(value, steps, 1)


def swap(value):
    return lax.ppermute(value, "section", [(0, 1), (1, 0)])


def add(first, *others):
    total = first.astype(F32)
    for other in others:
        total = total + other.astype(F32)
    return total


def in_order(pieces, rank):
    stacked = jnp.stack(pieces)
    return [lax.dynamic_index_in_dim(stacked, (rank - z) % 4, 0, False) for z in range(4)]


def shards(
    tokens, cotangent, block_order, norm_one, w_query, w_key, w_value, w_out, norm_two, w_gate, w_up, w_down
):
    section = lax.axis_index("section")
    rank = lax.axis_index("ctx")
    z_rank = lax.axis_index("wsh")
    first_core = section == 0
    quarter = FF // 4

    def both(value):
        other = swap(value)
        return jnp.where(first_core, value, other), jnp.where(first_core, other, value)

    key_value = jnp.concatenate(
        [w_key[0].reshape(-1, KV_HEADS, HEAD), w_value[0].reshape(-1, KV_HEADS, HEAD)], axis=2
    ).reshape(-1, 2 * KW)
    shard_rows = w_query.shape[1]
    low_half = jnp.concatenate([w_query[0][:, :HALF], w_out[0][:, : D // 2]], axis=1)
    high_half = jnp.concatenate(
        [
            w_query[0][:, HALF:],
            jnp.zeros((shard_rows, HEAD), BF),
            key_value,
            jnp.zeros((shard_rows, 128), BF),
            w_out[0][:, D // 2 :],
        ],
        axis=1,
    )
    got = swap(jnp.where(first_core, high_half, low_half))
    layer_half = (jnp.where(first_core, low_half, got), jnp.where(first_core, got, high_half))

    def whole(part):
        full = lax.all_gather(part, "wsh", axis=0, tiled=True)
        return full, swap(full)

    gathered = tuple(whole(part) for part in layer_half)

    gains = jnp.stack([norm_one[0], norm_two[0]])
    gain_parts = [gains] + [z_shift(gains, k) for k in (1, 2, 3)]
    gains = jnp.concatenate(in_order(gain_parts, z_rank), axis=1)
    gain_pair = [g.astype(F32) for g in both(gains)]

    given = swap(jnp.where(first_core, w_up[0], w_gate[0]))
    kind = (jnp.where(first_core, w_gate[0], given), jnp.where(first_core, given, w_up[0]))

    wd = both(w_down[0])

    def none_of(mark):
        return (mark != mark).astype(jnp.int32)

    def send_feed_weights(mark):
        later = none_of(mark)

        def columns(z):
            start = z * quarter + later
            return jnp.concatenate(
                [lax.dynamic_slice_in_dim(k, start, quarter, 1) for k in kind], axis=1
            )

        return [columns(z_rank)] + [z_shift(columns((z_rank + k) % 4), k) for k in (1, 2, 3)]

    def join_feed_weights(parts, mark):
        later = none_of(mark)
        ordered = jnp.zeros((D, 2 * quarter), BF)
        for k, part in enumerate(parts):
            start = ((z_rank - k) % 4) * shard_rows + later
            ordered = lax.dynamic_update_slice_in_dim(ordered, part, start, 0)
        return ordered, swap(ordered)

    own = lax.dynamic_slice_in_dim(block_order, 2 * rank, 2, 0)
    pairs = block_order.reshape(4, 4, 2)
    y, x = rank // 4, rank % 4
    step = jnp.arange(4, dtype=jnp.int32)

    def by_core(table):
        return jnp.where(first_core, table, jnp.swapaxes(table, 0, 1))

    came = by_core(pairs[(y - step) % 4][:, (x - step) % 4]).reshape(32)
    goes = by_core(pairs[(y + step) % 4][:, (x + step) % 4]).reshape(32)
    ahead_y = ((step - y) % 4)[:, None]
    ahead_x = ((step - x) % 4)[None, :]
    slot = jnp.where(first_core, ahead_y * 4 + ahead_x, ahead_x * 4 + ahead_y).reshape(16)
    info = jnp.concatenate([jnp.stack([section, z_rank]), own, came, goes, slot]).astype(jnp.int32)
    offsets = jnp.arange(BLK, dtype=jnp.int32)
    local_pos = (own[:, None] * BLK + offsets[None, :]).reshape(ROWS)
    frequency = jnp.exp(
        jnp.arange(HEAD // 2).astype(F32) * (-2.0 * math.log(ROPE_BASE) / HEAD)
    )
    angle = local_pos.astype(F32)[:, None] * frequency[None, :]
    cos32, sin32 = jnp.cos(angle), jnp.sin(angle)
    cosine = jnp.concatenate([cos32] * 4, axis=1)
    sine = jnp.concatenate([-sin32, sin32, -sin32, sin32], axis=1)

    own_tokens = lax.dynamic_index_in_dim(tokens, section, 0, False)[0]
    own_cotangent = lax.dynamic_index_in_dim(cotangent, section, 0, False)[0]

    def z_gather(value):
        return [value] + [z_shift(value, k) for k in (1, 2, 3)]

    last_lows = z_gather(own_cotangent.astype(BF))
    saved = []
    base, parts = own_tokens, []
    for layer in range(2):
        gain_one = gain_pair[layer][0:1]
        gain_two = gain_pair[layer][1:2]
        x_in, normed, q, kv = project(
            info, base, parts, gain_one, gathered[layer], cosine, sine, after=() if layer else wd
        )
        row = jnp.concatenate([kv] + [gather_shift(kv, k) for k in (1, 2, 3)], axis=0)
        pieces = [row] + [reduce_shift(row, k) for k in (1, 2, 3)]
        if layer == 0:
            sent = send_feed_weights(pieces[1][0, 0] + pieces[2][0, 0] + pieces[3][0, 0])
        mixed, lse, kvs, resid, second = attend(
            info, q, pieces, gathered[layer], x_in, gain_two, after=last_lows[1:] if layer else ()
        )
        if layer == 0:
            wgu = join_feed_weights(sent, second[0, 0])
        seconds = z_gather(second)
        fed = [feed(layer, info, s, wgu, wd[layer]) for s in seconds]
        parts = [fed[0][2]] + [z_shift(fed[k][2], -k) for k in (1, 2, 3)]
        base = resid
        saved.append(
            dict(
                x=x_in, q=q, mixed=mixed, lse=lse, kvs=kvs, resid=resid,
                normed=normed,
                seconds=seconds, gu=[f[0] for f in fed], hidden=[f[1] for f in fed],
            )
        )
    outputs = [saved[1]["x"], add(base, *parts)]

    grad = own_cotangent
    lows = last_lows
    input_grads = [None, None]
    feed_sums = [None, None]
    kept = [None, None]
    order = ()

    def stage_one(half, later=0):
        cut = [lax.dynamic_slice_in_dim(half, 4 * k + later, 4, 0) for k in range(4)]
        return add(cut[0], *[reduce_shift(cut[k], k) for k in (1, 2, 3)])

    def stage_two(stage):
        low = stage.astype(BF)
        return add(stage[0], *[gather_shift(low[k], k) for k in (1, 2, 3)])

    for layer in (1, 0):
        s = saved[layer]
        gain_one = gain_pair[layer][0:1]
        gain_two = gain_pair[layer][1:2]
        back = [feed_back(layer, info, lows[k], s["gu"][k], wgu, wd[layer]) for k in range(4)]
        parts = [back[0][1]] + [z_shift(back[k][1], -k) for k in (1, 2, 3)]
        keep, give = feed_grads(info, s["seconds"], [b[0] for b in back], s["hidden"], lows)
        d_resid, d_low, dc_two, dq, ahead, *goes_out = attend_back(
            info, parts, grad, s["resid"], gain_two, gathered[layer], s["normed"], s["mixed"], s["q"],
            s["lse"], s["kvs"], cosine, sine, after=(keep, *order),
        )
        feed_half = add(keep, swap(give)).astype(BF)
        row = add(goes_out[0], *[reduce_shift(goes_out[k], k) for k in (1, 2, 3)])
        row = row.astype(BF).reshape(4, ROWS, 2 * KW)
        own_pieces = [row[0]] + [gather_shift(row[k], k) for k in (1, 2, 3)]
        aheads = z_gather(ahead)
        if layer == 0:
            kept[1] = attention_grads(none_of(d_low[0, 0]))
        cut, grad, dc_one = project_back(
            info, own_pieces, dq, d_resid, d_low, s["x"], gain_one, gathered[layer], cosine, sine,
            after=tuple(aheads[1:]) if layer else (),
        )
        input_grads[layer] = grad
        feed_stage = stage_one(feed_half, none_of(cut[0, 0, 0]))
        if layer:
            lows = z_gather(grad.astype(BF))
            order = (feed_stage,)
            feed_sums[1] = stage_two(feed_stage)

        def attention_grads(later, cut=cut, aheads=aheads, dc_one=dc_one, dc_two=dc_two):
            mines = [lax.dynamic_index_in_dim(cut, k + later, 0, False) for k in range(4)]
            mines = [mines[0]] + [z_shift(mines[k], k) for k in (1, 2, 3)]
            keep, give = attend_grads(info, mines, aheads, dc_one, dc_two)
            return add(keep, swap(give)).astype(BF)

        if layer == 0:
            kept[0] = attention_grads(0)
    attend_stage = stage_one(jnp.concatenate(kept, axis=2))
    both_sums = stage_two(
        jnp.concatenate([feed_stage, jnp.pad(attend_stage, ((0, 0), (0, 32), (0, 0)))], axis=2)
    )
    feed_sums[0], attend_sum = both_sums[:, :640], both_sums[:64, 640:]
    sums = [
        jnp.concatenate(
            [feed_sums[layer], jnp.pad(attend_sum[:, layer * 384 : (layer + 1) * 384], ((0, 32), (0, 0)))],
            axis=1,
        )
        for layer in range(2)
    ]

    mine = jnp.where(first_core, sums[0], sums[1])
    other = swap(jnp.where(first_core, sums[1], sums[0]))
    halves = (jnp.where(first_core, mine, other), jnp.where(first_core, other, mine))
    joined = jnp.concatenate([h[:60] for h in halves], axis=1).reshape(4, 15, 2048)
    pieces = [lax.dynamic_index_in_dim(joined, z_rank, 0, False)] + [
        z_shift(lax.dynamic_index_in_dim(joined, (z_rank + k) % 4, 0, False), k) for k in (1, 2, 3)
    ]
    down = jnp.concatenate(
        [
            jnp.concatenate(
                [h[60:80, :640], jnp.concatenate([h[80:90, :320], h[80:90, 320:640]], axis=0)], axis=1
            )
            for h in halves
        ],
        axis=0,
    )
    moves = [(c * 4 + z, (4 * z + c // 4) * 4 + c % 4) for c in range(16) for z in range(4)]
    grad_down = lax.ppermute(down, ("ctx", "wsh"), moves)[None]
    sum_one, gq, gk, gv, go, sum_two, gate, up = finish(info, pieces)
    grad_query, grad_key, grad_value, grad_out, grad_gate, grad_up = (
        jnp.swapaxes(g, 0, 1) for g in (gq, gk, gv, go, gate, up)
    )

    def arranged(pair):
        mine = jnp.where(first_core, pair[0], pair[1])
        other = swap(jnp.where(first_core, pair[1], pair[0]))
        first = jnp.where(first_core, mine, other)
        last = jnp.where(first_core, other, mine)
        return jnp.stack([first, last])[None, :, None]

    return (
        arranged(outputs),
        arranged(input_grads),
        sum_one[:, 0][None],
        grad_query,
        grad_key,
        grad_value,
        grad_out,
        sum_two[:, 0][None],
        grad_gate,
        grad_up,
        grad_down,
    )


def solution(mesh):
    rows = P(None, "wsh", "ctx", None)
    gain = P("section", "wsh")
    weight = P("section", "wsh", None)
    in_specs = (rows, rows, P(), gain, weight, weight, weight, weight, gain, weight, weight, weight)
    result = P("section", None, "wsh", "ctx", None)
    gain_out = P("section", ("ctx", "wsh"))
    weight_out = P("section", ("ctx", "wsh"), None)
    out_specs = (
        result, result, gain_out, weight_out, weight_out, weight_out, weight_out, gain_out,
        weight_out, weight_out, weight_out,
    )
    return jax.shard_map(shards, mesh=mesh, in_specs=in_specs, out_specs=out_specs, check_vma=False)
```

time: 735 us -> 626 us (0.85)
  waiting for transfers between devices: 256 us -> 186 us
  Pallas kernels: 98.2 us -> 163 us
  other arithmetic: 81 us -> 39.4 us
  starting transfers between devices: 148 us -> 121 us
  local copies, waits for them, and re-layouts: 103 us -> 81.6 us
  matrix products: 19.8 us -> 0 us
    ppermute x48 -> x39, waiting for transfers between devices: 128 us -> 60.1 us  [ctx_shift(): return lax.ppermute(value, ('section', 'ctx'), pairs)]
    pallas_call x24 -> x29, Pallas kernels: 98.2 us -> 163 us  [run(): pl.pallas_call(inner, in_specs=in_specs, out_specs=[pl.BlockSpec(memory_s...]
    all_gather x2, waiting for transfers between devices: 67.8 us -> 29.1 us  [whole(): full = lax.all_gather(part, 'wsh', axis=0, tiled=True)]
    ppermute x45, waiting for transfers between devices: 46.3 us -> 81.1 us  [z_shift(): return lax.ppermute(value, 'wsh', [(i, (i + steps) % 4) for i in range(4)])]
    dot_general x8 -> x0, matrix products: 19.8 us -> none  [dot(): return lax.dot_general(left, right, dims, preferred_element_type=F32)]
    convert_element_type x14 -> x8, other arithmetic: 29.8 us -> 10.8 us  [the longest x2 5.44 us: shards(): feed_half = add(keep, swap(give)).astype(BF)]
    dynamic_update_slice x0 -> x4, local copies, waits for them, and re-layouts: none -> 16.7 us  [join_feed_weights(): ordered = lax.dynamic_update_slice_in_dim(ordered, part, start, 0)]
    ppermute x48 -> x39, starting transfers between devices: 78 us -> 61.9 us  [ctx_shift(): return lax.ppermute(value, ('section', 'ctx'), pairs)]
  transfers between devices with their start and end apart: 109 -> 101, of which waited for: 48 -> 42; matrix products, arithmetic and copies ran while one was open for 23% -> 13% of each run, Pallas kernels for 13% -> 20%
where the time goes in v2:
time: 626 us; the launch traced here: 615 us
  waiting for transfers between devices  186 us (30%)
  Pallas kernels  163 us (26%)
  starting transfers between devices  121 us (19%)
  local copies, waits for them, and re-layouts  81.6 us (13%)
  other arithmetic  39.4 us (6%)
  between operations  23.5 us (4%)
    pallas_call x29, Pallas kernels, run(): pl.pallas_call(inner, in_specs=in_specs, out_specs=[pl.BlockSpec(memory_s...  163 us
    ppermute x45, waiting for transfers between devices, z_shift(): return lax.ppermute(value, 'wsh', [(i, (i + steps) % 4) for i in range(4)])  81.1 us
    ppermute x39, starting transfers between devices, ctx_shift(): return lax.ppermute(value, ('section', 'ctx'), pairs)  61.9 us
    ppermute x39, waiting for transfers between devices, ctx_shift(): return lax.ppermute(value, ('section', 'ctx'), pairs)  60.1 us
    ppermute x45, starting transfers between devices, z_shift(): return lax.ppermute(value, 'wsh', [(i, (i + steps) % 4) for i in range(4)])  52.9 us
    unnamed x226, local copies, waits for them, and re-layouts  39 us
    all_gather x2, waiting for transfers between devices, whole(): full = lax.all_gather(part, 'wsh', axis=0, tiled=True)  29.1 us
    dynamic_update_slice x4, local copies, waits for them, and re-layouts, join_feed_weights(): ordered = lax.dynamic_update_slice_in_dim(ordered, part, start, 0)  16.7 us
  transfers between devices with their start and end apart: 101, of which 42 were waited for; matrix products, arithmetic and copies ran while one was open for 13% of the time, Pallas kernels for 20%

profile of v2, /device:TPU:16, one launch (start us, length us, event | category | flops | bytes accessed | tf_op | source)
XLA Modules:
  0.0 614.9 jit_solution(16375084334186169165)
XLA Ops:
  24.1 29.1 %all-gather.3.cloned.1.call-done.refs_3_.refs_6_.refs_8_.refs_10_ = bf16[960,1376]{1,0:T(8,128)(2,1)} async-done(((bf16[240,1376]{1,0:T(8,128)(2,1)}), bf16[960,1376]{1,0:T(8,128)(2,1)}) %all-gather.3.cloned.1.call-update) | async-done | bytes 2641936 | tf_op jit(solution)/shard_map/all_gather | solution.py:600
  63.9 4.8 shard_map.203
  91.1 6.5 %collective-permute-done.11.refs_4_ = bf16[512,640]{1,0:T(8,128)(2,1)S(1)} collective-permute-done((bf16[512,640]{1,0:T(8,128)(2,1)S(1)}, bf16[512,640]{1,0:T(8,128)(2,1)S(1)}, u32[]{:S(2)}, u32[]{:S(2)}) %collective-permute-start.11) | collective-permute-done | bytes 655392 | tf_op jit(solution)/shard_map/ppermute | solution.py:541
  112.4 12.6 %shard_map.204 = (bf16[128,960]{1,0:T(8,128)(2,1)S(1)}, f32[2,5,192,128]{3,2,1,0:T(8,128)S(1)}, bf16[2048,640]{1,0:T(8,128)(2,1)}, f32[128,960]{1,0:T(8,128)S(1)}, bf16[128,960]{1,0:T(8,128)(2,1)S(1)}) custom-call(s32[84]{0:T(128)S(1)} %concatenate.69.refs_0_, bf16[128,1024]{1,0:T(8,128)(2,1)S(1)} %get-tuple-element.109.refs_1_.refs_12_, ...), custom_call_target="tpu_custom_call" | custom-call | flops 13200000000 | bytes 43200000 | tf_op jit(solution)/shard_map/pallas_call | solution.py:51
  140.3 4.6 dynamic_update_slice.14
  144.9 4.6 dynamic_update_slice.15.refs_2_.refs_3_
  153.3 11.9 %collective-permute-done.18.refs_1_.refs_2_ = bf16[128,960]{1,0:T(8,128)(2,1)S(1)} collective-permute-done((bf16[128,960]{1,0:T(8,128)(2,1)S(1)}, bf16[128,960]{1,0:T(8,128)(2,1)S(1)}, u32[]{:S(2)}, u32[]{:S(2)}) %collective-permute-start.18) | collective-permute-done | bytes 245792 | tf_op jit(solution)/shard_map/ppermute | solution.py:531
  213.6 8.2 %collective-permute-done.31.refs_10_.refs_1_.refs_14_ = bf16[128,960]{1,0:T(8,128)(2,1)S(1)} collective-permute-done((bf16[128,960]{1,0:T(8,128)(2,1)S(1)}, bf16[128,960]{1,0:T(8,128)(2,1)S(1)}, u32[]{:S(2)}, u32[]{:S(2)}) %collective-permute-start.31) | collective-permute-done | bytes 245792 | tf_op jit(solution)/shard_map/ppermute | solution.py:531
  221.8 6.4 %collective-permute-done.33.refs_12_.refs_1_.refs_16_ = bf16[128,960]{1,0:T(8,128)(2,1)S(1)} collective-permute-done((bf16[128,960]{1,0:T(8,128)(2,1)S(1)}, bf16[128,960]{1,0:T(8,128)(2,1)S(1)}, u32[]{:S(2)}, u32[]{:S(2)}) %collective-permute-start.33) | collective-permute-done | bytes 245792 | tf_op jit(solution)/shard_map/ppermute | solution.py:531
  228.2 12.4 %shard_map.210 = (bf16[128,960]{1,0:T(8,128)(2,1)S(1)}, f32[2,5,192,128]{3,2,1,0:T(8,128)}, bf16[2048,640]{1,0:T(8,128)(2,1)}, f32[128,960]{1,0:T(8,128)S(1)}, bf16[128,960]{1,0:T(8,128)(2,1)S(1)}) custom-call(s32[84]{0:T(128)S(1)} %concatenate.69.refs_0_, bf16[128,1024]{1,0:T(8,128)(2,1)S(1)} %copy-done.81, ...), custom_call_target="tpu_custom_call" | custom-call | flops 13200000000 | bytes 43200000 | tf_op jit(solution)/shard_map/pallas_call | solution.py:51
  274.1 6.2 %shard_map.219 = (bf16[16,96,640]{2,1,0:T(8,128)(2,1)S(1)}, bf16[16,96,640]{2,1,0:T(8,128)(2,1)}) custom-call(s32[84]{0:T(128)S(1)} %concatenate.69.refs_0_, bf16[128,960]{1,0:T(8,128)(2,1)S(1)} %get-tuple-element.122.refs_1_, bf16[128,960]{1,0:T(8,128)(2,1)S(1)} %collective-permute-done.34.refs_1_.refs_2_, ...), custom_call_target="tpu_custom_call" | custom-call | flops 7150000128 | bytes 23400000 | tf_op jit(solution)/shard_map/pallas_call | solution.py:51
  281.7 24.7 %shard_map.220 = (f32[128,960]{1,0:T(8,128)S(1)}, bf16[128,960]{1,0:T(8,128)(2,1)S(1)}, f32[1,960]{1,0:T(1,128)S(1)}, bf16[128,960]{1,0:T(8,128)(2,1)S(1)}, bf16...) custom-call(s32[84]{0:T(128)S(1)} %concatenate.69.refs_0_, ...), custom_call_target="tpu_custom_call" | custom-call | flops 26400000000 | bytes 86400000 | tf_op jit(solution)/shard_map/pallas_call | solution.py:51
  311.9 6.2 %collective-permute-done.46 = bf16[512,640]{1,0:T(8,128)(2,1)S(1)} collective-permute-done((bf16[512,640]{1,0:T(8,128)(2,1)}, bf16[512,640]{1,0:T(8,128)(2,1)S(1)}, u32[]{:S(2)}, u32[]{:S(2)}) %collective-permute-start.46) | collective-permute-done | bytes 655392 | tf_op jit(solution)/shard_map/ppermute | solution.py:541
  322.8 6.9 %collective-permute-done.44 = bf16[512,640]{1,0:T(8,128)(2,1)S(1)} collective-permute-done((bf16[512,640]{1,0:T(8,128)(2,1)S(1)}, bf16[512,640]{1,0:T(8,128)(2,1)S(1)}, u32[]{:S(2)}, u32[]{:S(2)}) %collective-permute-start.44) | collective-permute-done | bytes 655392 | tf_op jit(solution)/shard_map/ppermute | solution.py:541
  358.3 4.3 shard_map.221
  395.6 6.8 %shard_map.226 = (bf16[16,96,640]{2,1,0:T(8,128)(2,1)S(1)}, bf16[16,96,640]{2,1,0:T(8,128)(2,1)}) custom-call(s32[84]{0:T(128)S(1)} %concatenate.69.refs_0_, bf16[128,960]{1,0:T(8,128)(2,1)S(1)} %copy-done.22, bf16[128,960]{1,0:T(8,128)(2,1)S(1)} %copy-done.24, bf16[128,960]{1,0:T(8,128)(2,1)S(1)} %copy-done.26, bf16[128,960]{1,0:T(8,128)(2,1)S(1)} %copy-done.28, ...), custom_call_target="tpu_custom_call" | custom-call | flops 7150000128 | bytes 23400000 | tf_op jit(solution)/shard_map/pallas_call | solution.py:51
  412.0 6.7 %collective-permute-done.58.refs_4_ = bf16[128,960]{1,0:T(8,128)(2,1)S(1)} collective-permute-done((bf16[128,960]{1,0:T(8,128)(2,1)S(1)}, bf16[128,960]{1,0:T(8,128)(2,1)S(1)}, u32[]{:S(2)}, u32[]{:S(2)}) %collective-permute-start.58) | collective-permute-done | bytes 245792 | tf_op jit(solution)/shard_map/ppermute | solution.py:531
  418.7 24.8 %shard_map.227 = (f32[128,960]{1,0:T(8,128)S(1)}, bf16[128,960]{1,0:T(8,128)(2,1)S(1)}, f32[1,960]{1,0:T(1,128)S(1)}, bf16[128,960]{1,0:T(8,128)(2,1)S(1)}, bf16...) custom-call(s32[84]{0:T(128)S(1)} %concatenate.69.refs_0_, ...), custom_call_target="tpu_custom_call" | custom-call | flops 26400000000 | bytes 86400000 | tf_op jit(solution)/shard_map/pallas_call | solution.py:51
  467.5 4.7 collective-permute-start.67
  480.2 4.3 shard_map.228
  484.5 11.0 %collective-permute-done.81.refs_2_ = bf16[128,640]{1,0:T(8,128)(2,1)S(1)} collective-permute-done((bf16[128,640]{1,0:T(8,128)(2,1)S(1)}, bf16[128,640]{1,0:T(8,128)(2,1)S(1)}, u32[]{:S(2)}, u32[]{:S(2)}) %collective-permute-start.81) | collective-permute-done | bytes 163872 | tf_op jit(solution)/shard_map/ppermute | solution.py:531
  497.4 15.7 %collective-permute-done.83.refs_4_ = bf16[128,640]{1,0:T(8,128)(2,1)S(1)} collective-permute-done((bf16[128,640]{1,0:T(8,128)(2,1)S(1)}, bf16[128,640]{1,0:T(8,128)(2,1)S(1)}, u32[]{:S(2)}, u32[]{:S(2)}) %collective-permute-start.83) | collective-permute-done | bytes 163872 | tf_op jit(solution)/shard_map/ppermute | solution.py:531
  585.0 4.7 collective-permute-start.98
  593.9 13.1 %collective-permute-done.98 = f32[40,960]{1,0:T(8,128)S(1)} collective-permute-done((f32[40,960]{1,0:T(8,128)S(1)}, f32[40,960]{1,0:T(8,128)S(1)}, u32[]{:S(2)}, u32[]{:S(2)}) %collective-permute-start.98) | collective-permute-done | bytes 153632 | tf_op jit(solution)/shard_map/ppermute | solution.py:780
  (559 shorter events, 350.1 us)
Async XLA Ops:
  7.2 46.0 %all-gather.3.cloned.1.call-start = ((), (), s32[]{:S(2)}) async-start(), calls=%async_computation | async-start | bytes 3379200 | tf_op jit(solution)/shard_map/all_gather | solution.py:600
  14.7 134.9 %all-gather.5.cloned.1.call-start = ((), (), s32[]{:S(2)}) async-start(), calls=%async_computation.1 | async-start | bytes 3379200 | tf_op jit(solution)/shard_map/all_gather | solution.py:600
  14.8 41.5 %collective-permute-start.2 = (bf16[2,240]{1,0:T(2,128)(2,1)S(1)}, bf16[2,240]{1,0:T(2,128)(2,1)S(1)}, u32[]{:S(2)}, u32[]{:S(2)}) collective-permute-start(bf16[2,240]{1,0:T(2,128)(2,1)S(1)} %pad_maximum_fusion.12), channel_id=1, source_target_pairs={{0,3},{1,0},{2,1},{3,2},{4,7},{5,4},{6,5},{7,6},{8,11},{9,8},{10,9... | collective-permute-start | bytes 2888 | tf_op jit(solution)/shard_map/ppermute | solution.py:531
  18.9 38.0 %collective-permute-start.1 = (bf16[2,240]{1,0:T(2,128)(2,1)S(1)}, bf16[2,240]{1,0:T(2,128)(2,1)S(1)}, u32[]{:S(2)}, u32[]{:S(2)}) collective-permute-start(bf16[2,240]{1,0:T(2,128)(2,1)S(1)} %pad_maximum_fusion.12), channel_id=1, source_target_pairs={{0,2},{1,3},{2,0},{3,1},{4,6},{5,7},{6,4},{7,5},{8,10},{9,11},{10,... | collective-permute-start | bytes 2888 | tf_op jit(solution)/shard_map/ppermute | solution.py:531
  18.9 38.0 %collective-permute-start = (bf16[2,240]{1,0:T(2,128)(2,1)S(1)}, bf16[2,240]{1,0:T(2,128)(2,1)S(1)}, u32[]{:S(2)}, u32[]{:S(2)}) collective-permute-start(bf16[2,240]{1,0:T(2,128)(2,1)S(1)} %pad_maximum_fusion.12), channel_id=1, source_target_pairs={{0,1},{1,2},{2,3},{3,0},{4,5},{5,6},{6,7},{7,4},{8,9},{9,10},{10,1... | collective-permute-start | bytes 2888 | tf_op jit(solution)/shard_map/ppermute | solution.py:531
  20.2 39.7 %collective-permute-start.6 = (bf16[640,960]{0,1:T(8,128)(2,1)}, bf16[640,960]{0,1:T(8,128)(2,1)}, u32[]{:S(2)}, u32[]{:S(2)}) collective-permute-start(bf16[640,960]{0,1:T(8,128)(2,1)} %bitcast.126), channel_id=1, source_target_pairs={{0,64},{64,0},{1,65},{65,1},{2,66},{66,2},{3,67},{67,3},{4,68},{68... | collective-permute-start | bytes 3686408 | tf_op jit(solution)/shard_map/ppermute | solution.py:553
  56.3 26.8 %collective-permute-start.13 = (bf16[240,2560]{1,0:T(8,128)(2,1)}, bf16[240,2560]{1,0:T(8,128)(2,1)}, u32[]{:S(2)}, u32[]{:S(2)}) collective-permute-start(bf16[240,2560]{1,0:T(8,128)(2,1)} %bitcast_select_fusion.3), channel_id=1, source_target_pairs={{0,64},{64,0},{1,65},{65,1},{2,66},{66,2},{3,67},{67,3},{4,68},{68... | collective-permute-start | bytes 3686408 | tf_op jit(solution)/shard_map/ppermute | solution.py:553
  105.9 30.2 %collective-permute-start.14 = (bf16[240,1280]{1,0:T(8,128)(2,1)}, bf16[240,1280]{1,0:T(8,128)(2,1)}, u32[]{:S(2)}, u32[]{:S(2)}) collective-permute-start(bf16[240,1280]{1,0:T(8,128)(2,1)} %pad_maximum_fusion.2), channel_id=1, source_target_pairs={{0,1},{1,2},{2,3},{3,0},{4,5},{5,6},{6,7},{7,4},{8,9},{9,10},{10,1... | collective-permute-start | bytes 1843208 | tf_op jit(solution)/shard_map/ppermute | solution.py:531
  107.3 32.9 %collective-permute-start.15 = (bf16[240,1280]{1,0:T(8,128)(2,1)}, bf16[240,1280]{1,0:T(8,128)(2,1)}, u32[]{:S(2)}, u32[]{:S(2)}) collective-permute-start(bf16[240,1280]{1,0:T(8,128)(2,1)} %pad_maximum_fusion.3), channel_id=1, source_target_pairs={{0,2},{1,3},{2,0},{3,1},{4,6},{5,7},{6,4},{7,5},{8,10},{9,11},{10,... | collective-permute-start | bytes 1843208 | tf_op jit(solution)/shard_map/ppermute | solution.py:531
  109.9 35.0 %collective-permute-start.16 = (bf16[240,1280]{1,0:T(8,128)(2,1)}, bf16[240,1280]{1,0:T(8,128)(2,1)}, u32[]{:S(2)}, u32[]{:S(2)}) collective-permute-start(bf16[240,1280]{1,0:T(8,128)(2,1)} %pad_maximum_fusion.4), channel_id=1, source_target_pairs={{0,3},{1,0},{2,1},{3,2},{4,7},{5,4},{6,5},{7,6},{8,11},{9,8},{10,9... | collective-permute-start | bytes 1843208 | tf_op jit(solution)/shard_map/ppermute | solution.py:531
  149.6 36.4 %collective-permute-start.24 = (bf16[960,1376]{1,0:T(8,128)(2,1)}, bf16[960,1376]{1,0:T(8,128)(2,1)S(1)}, u32[]{:S(2)}, u32[]{:S(2)}) collective-permute-start(bf16[960,1376]{1,0:T(8,128)(2,1)} %all-gather.5.cloned.1.call-done.refs_7_.refs_6_.refs_8_.refs_10_), channel_id=1, source_target_pairs={{0,64},{64,0},{1,65},{65,1},{2,66},{66,2},{3,67},{67,3},{4,68},{68... | collective-permute-start | bytes 7925768 | tf_op jit(solution)/shard_map/ppermute | solution.py:553
  151.4 23.8 %collective-permute-start.22 = (bf16[128,960]{1,0:T(8,128)(2,1)S(1)}, bf16[128,960]{1,0:T(8,128)(2,1)S(1)}, u32[]{:S(2)}, u32[]{:S(2)}) collective-permute-start(bf16[128,960]{1,0:T(8,128)(2,1)S(1)} %get-tuple-element.113.refs_1_), channel_id=1, source_target_pairs={{0,3},{1,0},{2,1},{3,2},{4,7},{5,4},{6,5},{7,6},{8,11},{9,8},{10,9... | collective-permute-start | bytes 737288 | tf_op jit(solution)/shard_map/ppermute | solution.py:531
  205.8 22.3 %collective-permute-start.28 = (bf16[512,640]{1,0:T(8,128)(2,1)S(1)}, bf16[512,640]{1,0:T(8,128)(2,1)S(1)}, u32[]{:S(2)}, u32[]{:S(2)}) collective-permute-start(bf16[512,640]{1,0:T(8,128)(2,1)S(1)} %constant_dynamic-update-slice_fusion.4.refs_2_), channel_id=1, source_target_pairs={{0,16},{4,20},{8,24},{12,28},{16,32},{20,36},{24,40},{28,44},{32,4... | collective-permute-start | bytes 1966088 | tf_op jit(solution)/shard_map/ppermute | solution.py:541
  240.7 25.9 %collective-permute-start.38 = (bf16[128,960]{1,0:T(8,128)(2,1)S(1)}, bf16[128,960]{1,0:T(8,128)(2,1)S(1)}, u32[]{:S(2)}, u32[]{:S(2)}) collective-permute-start(bf16[128,960]{1,0:T(8,128)(2,1)S(1)} %get-tuple-element.122.refs_1_), channel_id=1, source_target_pairs={{0,3},{1,0},{2,1},{3,2},{4,7},{5,4},{6,5},{7,6},{8,11},{9,8},{10,9... | collective-permute-start | bytes 737288 | tf_op jit(solution)/shard_map/ppermute | solution.py:531
  256.0 25.6 %collective-permute-start.41 = (bf16[128,960]{1,0:T(8,128)(2,1)S(1)}, bf16[128,960]{1,0:T(8,128)(2,1)S(1)}, u32[]{:S(2)}, u32[]{:S(2)}) collective-permute-start(bf16[128,960]{1,0:T(8,128)(2,1)S(1)} %get-tuple-element.130), channel_id=1, source_target_pairs={{0,3},{1,0},{2,1},{3,2},{4,7},{5,4},{6,5},{7,6},{8,11},{9,8},{10,9... | collective-permute-start | bytes 737288 | tf_op jit(solution)/shard_map/ppermute | solution.py:531
  311.5 76.9 %collective-permute-start.59 = (bf16[16,96,640]{2,1,0:T(8,128)(2,1)}, bf16[16,96,640]{2,1,0:T(8,128)(2,1)}, u32[]{:S(2)}, u32[]{:S(2)}) collective-permute-start(bf16[16,96,640]{2,1,0:T(8,128)(2,1)} %get-tuple-element.178), channel_id=1, source_target_pairs={{0,64},{64,0},{1,65},{65,1},{2,66},{66,2},{3,67},{67,3},{4,68},{68... | collective-permute-start | bytes 5898248 | tf_op jit(solution)/shard_map/ppermute | solution.py:553
  343.0 22.1 %collective-permute-start.39 = (bf16[128,960]{1,0:T(8,128)(2,1)}, bf16[128,960]{1,0:T(8,128)(2,1)S(1)}, u32[]{:S(2)}, u32[]{:S(2)}) collective-permute-start(bf16[128,960]{1,0:T(8,128)(2,1)} %copy-done.51), channel_id=1, source_target_pairs={{0,1},{1,2},{2,3},{3,0},{4,5},{5,6},{6,7},{7,4},{8,9},{9,10},{10,1... | collective-permute-start | bytes 737288 | tf_op jit(solution)/shard_map/ppermute | solution.py:531
  366.3 83.2 %collective-permute-start.40 = (f32[128,960]{1,0:T(8,128)}, f32[128,960]{1,0:T(8,128)}, u32[]{:S(2)}, u32[]{:S(2)}) collective-permute-start(f32[128,960]{1,0:T(8,128)} %get-tuple-element.264), channel_id=1, source_target_pairs={{0,64},{64,0},{1,65},{65,1},{2,66},{66,2},{3,67},{67,3},{4,68},{68... | collective-permute-start | bytes 1474568 | tf_op jit(solution)/shard_map/ppermute | solution.py:553
  381.3 27.9 %collective-permute-start.54 = (bf16[128,960]{1,0:T(8,128)(2,1)S(1)}, bf16[128,960]{1,0:T(8,128)(2,1)S(1)}, u32[]{:S(2)}, u32[]{:S(2)}) collective-permute-start(bf16[128,960]{1,0:T(8,128)(2,1)S(1)} %get-tuple-element.160), channel_id=1, source_target_pairs={{0,3},{1,0},{2,1},{3,2},{4,7},{5,4},{6,5},{7,6},{8,11},{9,8},{10,9... | collective-permute-start | bytes 737288 | tf_op jit(solution)/shard_map/ppermute | solution.py:531
  454.5 73.6 %collective-permute-start.70 = (bf16[16,96,640]{2,1,0:T(8,128)(2,1)}, bf16[16,96,640]{2,1,0:T(8,128)(2,1)}, u32[]{:S(2)}, u32[]{:S(2)}) collective-permute-start(bf16[16,96,640]{2,1,0:T(8,128)(2,1)} %get-tuple-element.188), channel_id=1, source_target_pairs={{0,64},{64,0},{1,65},{65,1},{2,66},{66,2},{3,67},{67,3},{4,68},{68... | collective-permute-start | bytes 5898248 | tf_op jit(solution)/shard_map/ppermute | solution.py:553
  456.9 56.2 %collective-permute-start.77 = (bf16[128,1984]{1,0:T(8,128)(2,1)}, bf16[128,1984]{1,0:T(8,128)(2,1)}, u32[]{:S(2)}, u32[]{:S(2)}) collective-permute-start(bf16[128,1984]{1,0:T(8,128)(2,1)} %get-tuple-element.190.refs_5_), channel_id=1, source_target_pairs={{0,1},{1,2},{2,3},{3,0},{4,5},{5,6},{6,7},{7,4},{8,9},{9,10},{10,1... | collective-permute-start | bytes 1523720 | tf_op jit(solution)/shard_map/ppermute | solution.py:531
  476.5 39.6 %collective-permute-start.78 = (bf16[128,1984]{1,0:T(8,128)(2,1)}, bf16[128,1984]{1,0:T(8,128)(2,1)S(1)}, u32[]{:S(2)}, u32[]{:S(2)}) collective-permute-start(bf16[128,1984]{1,0:T(8,128)(2,1)} %get-tuple-element.190.refs_5_), channel_id=1, source_target_pairs={{0,2},{1,3},{2,0},{3,1},{4,6},{5,7},{6,4},{7,5},{8,10},{9,11},{10,... | collective-permute-start | bytes 1523720 | tf_op jit(solution)/shard_map/ppermute | solution.py:531
  495.5 25.1 %collective-permute-start.79 = (bf16[128,1984]{1,0:T(8,128)(2,1)}, bf16[128,1984]{1,0:T(8,128)(2,1)S(1)}, u32[]{:S(2)}, u32[]{:S(2)}) collective-permute-start(bf16[128,1984]{1,0:T(8,128)(2,1)} %get-tuple-element.190.refs_5_), channel_id=1, source_target_pairs={{0,3},{1,0},{2,1},{3,2},{4,7},{5,4},{6,5},{7,6},{8,11},{9,8},{10,9... | collective-permute-start | bytes 1523720 | tf_op jit(solution)/shard_map/ppermute | solution.py:531
  550.4 26.8 %collective-permute-start.69 = (f32[128,960]{1,0:T(8,128)}, f32[128,960]{1,0:T(8,128)S(1)}, u32[]{:S(2)}, u32[]{:S(2)}) collective-permute-start(f32[128,960]{1,0:T(8,128)} %broadcast_select_fusion.3), channel_id=1, source_target_pairs={{0,64},{64,0},{1,65},{65,1},{2,66},{66,2},{3,67},{67,3},{4,68},{68... | collective-permute-start | bytes 1474568 | tf_op jit(solution)/shard_map/ppermute | solution.py:553
  (185 other events, 2104.8 us)
Sparse Core Ops, SparseCore 0:
  14.9 38.2 all-gather.2
  71.9 35.7 all-gather.4

commit v3 on v2

--- a/solution.py
+++ b/solution.py
@@ -27,7 +27,7 @@
 QP = 1024
 HALF = 896
 NEG = -1e30
-VMEM_BYTES = 48 * 1024 * 1024
+MIB = 1024 * 1024
 
 NN = (((1,), (0,)), ((), ()))
 NT = (((1,), (1,)), ((), ()))
@@ -38,7 +38,7 @@
     return lax.dot_general(left, right, dims, preferred_element_type=F32)
 
 
-def call(body, outs, micros, scratch=(), smem=0):
+def call(body, outs, micros, mib, scratch=(), smem=0):
     def run(*args, after=()):
         count = len(args)
         in_specs = [
@@ -57,7 +57,7 @@
             cost_estimate=pl.CostEstimate(
                 flops=int(micros * 1.1e9), bytes_accessed=int(micros * 3.6e6), transcendentals=0
             ),
-            compiler_params=pltpu.CompilerParams(vmem_limit_bytes=VMEM_BYTES),
+            compiler_params=pltpu.CompilerParams(vmem_limit_bytes=mib * MIB),
         )(*args, *after)
         return out
 
@@ -90,7 +90,15 @@
     def body(*refs):
         info, base = refs[:2]
         parts = refs[2 : 2 + count]
-        (gain, own, other, cosine, sine, x_out, normed_out, q_out, kv_out, halves) = refs[2 + count :]
+        gain, own, other, cosine, sine = refs[2 + count : 7 + count]
+        if count:
+            normed_in, mixed_in = refs[7 + count : 9 + count]
+            x_out, normed_out, q_out, kv_out, ahead_out, halves = refs[9 + count :]
+            ahead_out[:, :D] = normed_in[...]
+            ahead_out[:, D:QP] = jnp.zeros((ROWS, QP - D), BF)
+            ahead_out[:, QP:] = mixed_in[...]
+        else:
+            x_out, normed_out, q_out, kv_out, halves = refs[7:]
         side = info[0]
         x = base[...]
         for part in parts:
@@ -112,11 +120,13 @@
     return body
 
 
-def project(info, base, parts, gain, weight, cosine, sine, after=()):
+def project(info, base, parts, gain, weight, cosine, sine, ahead=()):
     outs = [((ROWS, D), F32), ((ROWS, D), BF), ((ROWS, QP), BF), ((ROWS, 2 * KW), BF)]
+    if ahead:
+        outs.append(((ROWS, QP + D), BF))
     scratch = [pltpu.VMEM((2, ROWS, HALF), F32)]
-    return call(project_body(len(parts)), outs, 2.5, scratch, smem=1)(
-        info, base, *parts, gain, *weight, cosine, sine, after=after
+    return call(project_body(len(parts)), outs, 2.5, 16, scratch, smem=1)(
+        info, base, *parts, gain, *weight, cosine, sine, *ahead
     )
 
 
@@ -225,7 +235,7 @@
     shape = (2, KV_HEADS, GROUP * BLK, 128)
     scratch = [pltpu.VMEM(shape, BF)] + [pltpu.VMEM(shape, F32)] * 3
     scratch.append(pltpu.VMEM((2, ROWS, D // 2), F32))
-    return call(attend_body(len(pieces)), outs, 12.0, scratch, smem=1)(
+    return call(attend_body(len(pieces)), outs, 12.0, 24, scratch, smem=1)(
         info, q, *pieces, *wo, x, gain, after=after
     )
 
@@ -233,7 +243,7 @@
 def feed_body(layer, info, second, own, other, wd, gu_out, hidden_out, part_out):
     side = info[0]
     columns = slice(layer * FF // 4, (layer + 1) * FF // 4)
-    gu_out[side] = dot(second[...], own[:, columns])
+    gu_out[side] = dot(second[...], own[...])
     gu_out[1 - side] = dot(second[...], other[:, columns])
     gate, up = gu_out[0], gu_out[1]
     hidden = (gate / (1.0 + jnp.exp(-gate)) * up).astype(BF)
@@ -241,10 +251,10 @@
     part_out[...] = dot(hidden, wd[...]).astype(BF)
 
 
-def feed(layer, info, second, wgu, wd):
+def feed(layer, info, second, wgu, wd, after=()):
     outs = [((2, ROWS, FF // 4), F32), ((ROWS, FF // 4), BF), ((ROWS, D), BF)]
     body = partial(feed_body, layer)
-    return call(body, outs, 1.0, smem=1)(info, second, *wgu, wd)
+    return call(body, outs, 1.0, 12, smem=1)(info, second, *wgu, wd, after=after)
 
 
 def feed_back_body(layer, info, grad_low, gu, own, other, wd, dgu_out, part_out):
@@ -257,14 +267,14 @@
     d_up = d_hidden * gate * sig
     dgu_out[0] = d_gate.astype(BF)
     dgu_out[1] = d_up.astype(BF)
-    part = dot(dgu_out[side], own[:, columns], NT) + dot(dgu_out[1 - side], other[:, columns], NT)
+    part = dot(dgu_out[side], own[...], NT) + dot(dgu_out[1 - side], other[:, columns], NT)
     part_out[...] = part.astype(BF)
 
 
 def feed_back(layer, info, grad_low, gu, wgu, wd):
     outs = [((2, ROWS, FF // 4), BF), ((ROWS, D), BF)]
     body = partial(feed_back_body, layer)
-    return call(body, outs, 1.3, smem=1)(info, grad_low, gu, *wgu, wd)
+    return call(body, outs, 1.3, 12, smem=1)(info, grad_low, gu, *wgu, wd)
 
 
 def attend_back_body(
@@ -365,7 +375,7 @@
         pltpu.VMEM((ROWS, QP), BF),
         pltpu.VMEM((2, ROWS, D // 2), BF),
     ]
-    return call(attend_back_body, outs, 24.0, scratch, smem=1)(
+    return call(attend_back_body, outs, 24.0, 32, scratch, smem=1)(
         info, *parts, grad, resid, gain, *wo, normed, mixed, q, lse, kvs, cosine, sine, after=after
     )
 
@@ -403,7 +413,7 @@
 def project_back(info, pieces, dq, d_resid, d_low, x, gain, weight, cosine, sine, after=()):
     outs = [((4, ROWS, 640), BF), ((ROWS, D), F32), ((1, D), F32)]
     scratch = [pltpu.VMEM((2, ROWS, HALF), BF), pltpu.VMEM((ROWS, 2 * KW), F32)]
-    return call(project_back_body, outs, 3.2, scratch, smem=1)(
+    return call(project_back_body, outs, 3.2, 16, scratch, smem=1)(
         info, *pieces, dq, d_resid, d_low, x, gain, *weight, cosine, sine, after=after
     )
 
@@ -454,7 +464,7 @@
         pltpu.VMEM((640, D), F32),
         pltpu.VMEM((96, 640), F32),
     ]
-    return call(feed_grads_body, [((16, 96, 640), BF)] * 2, 6.5, scratch, smem=1)(
+    return call(feed_grads_body, [((16, 96, 640), BF)] * 2, 6.5, 24, scratch, smem=1)(
         info, *seconds, *dgus, *hiddens, *lows, after=after
     )
 
@@ -492,7 +502,7 @@
         pltpu.VMEM((D, 384), F32),
         pltpu.VMEM((64, 384), F32),
     ]
-    return call(attend_grads_body, [((16, 64, 384), BF)] * 2, 3.0, scratch, smem=1)(
+    return call(attend_grads_body, [((16, 64, 384), BF)] * 2, 3.0, 16, scratch, smem=1)(
         info, *mines, *aheads, dc_one, dc_two
     )
 
@@ -523,7 +533,7 @@
     shapes = [(15, 1, width) for width in widths]
     shapes = [(15, 64)] + shapes[:4] + [(15, 64)] + shapes[4:]
     return call(
-        finish_body, [(s, F32) for s in shapes], 1.5, [pltpu.VMEM((4, 15, 2048), F32)], smem=1
+        finish_body, [(s, F32) for s in shapes], 1.5, 8, [pltpu.VMEM((4, 15, 2048), F32)], smem=1
     )(info, *pieces)
 
 
@@ -628,11 +638,9 @@
 
     def join_feed_weights(parts, mark):
         later = none_of(mark)
-        ordered = jnp.zeros((D, 2 * quarter), BF)
-        for k, part in enumerate(parts):
-            start = ((z_rank - k) % 4) * shard_rows + later
-            ordered = lax.dynamic_update_slice_in_dim(ordered, part, start, 0)
-        return ordered, swap(ordered)
+        ordered = jnp.concatenate(in_order(parts, z_rank + later), axis=0)
+        other = swap(ordered)
+        return [(ordered[:, layer * quarter : (layer + 1) * quarter], other) for layer in range(2)]
 
     own = lax.dynamic_slice_in_dim(block_order, 2 * rank, 2, 0)
     pairs = block_order.reshape(4, 4, 2)
@@ -670,20 +678,24 @@
     for layer in range(2):
         gain_one = gain_pair[layer][0:1]
         gain_two = gain_pair[layer][1:2]
-        x_in, normed, q, kv = project(
-            info, base, parts, gain_one, gathered[layer], cosine, sine, after=() if layer else wd
+        ahead = (saved[0]["normed"], saved[0]["mixed"]) if layer else ()
+        x_in, normed, q, kv, *ahead = project(
+            info, base, parts, gain_one, gathered[layer], cosine, sine, ahead
         )
+        if layer:
+            first_aheads = z_gather(ahead[0])
         row = jnp.concatenate([kv] + [gather_shift(kv, k) for k in (1, 2, 3)], axis=0)
         pieces = [row] + [reduce_shift(row, k) for k in (1, 2, 3)]
         if layer == 0:
             sent = send_feed_weights(pieces[1][0, 0] + pieces[2][0, 0] + pieces[3][0, 0])
         mixed, lse, kvs, resid, second = attend(
-            info, q, pieces, gathered[layer], x_in, gain_two, after=last_lows[1:] if layer else ()
+            info, q, pieces, gathered[layer], x_in, gain_two, after=last_lows[1:] if layer else wd
         )
         if layer == 0:
             wgu = join_feed_weights(sent, second[0, 0])
         seconds = z_gather(second)
-        fed = [feed(layer, info, s, wgu, wd[layer]) for s in seconds]
+        after = first_aheads[1:] if layer else ()
+        fed = [feed(layer, info, s, wgu[layer], wd[layer], after) for s in seconds]
         parts = [fed[0][2]] + [z_shift(fed[k][2], -k) for k in (1, 2, 3)]
         base = resid
         saved.append(
@@ -714,7 +726,7 @@
         s = saved[layer]
         gain_one = gain_pair[layer][0:1]
         gain_two = gain_pair[layer][1:2]
-        back = [feed_back(layer, info, lows[k], s["gu"][k], wgu, wd[layer]) for k in range(4)]
+        back = [feed_back(layer, info, lows[k], s["gu"][k], wgu[layer], wd[layer]) for k in range(4)]
         parts = [back[0][1]] + [z_shift(back[k][1], -k) for k in (1, 2, 3)]
         keep, give = feed_grads(info, s["seconds"], [b[0] for b in back], s["hidden"], lows)
         d_resid, d_low, dc_two, dq, ahead, *goes_out = attend_back(
@@ -725,7 +737,7 @@
         row = add(goes_out[0], *[reduce_shift(goes_out[k], k) for k in (1, 2, 3)])
         row = row.astype(BF).reshape(4, ROWS, 2 * KW)
         own_pieces = [row[0]] + [gather_shift(row[k], k) for k in (1, 2, 3)]
-        aheads = z_gather(ahead)
+        aheads = z_gather(ahead) if layer else first_aheads
         if layer == 0:
             kept[1] = attention_grads(none_of(d_low[0, 0]))
         cut, grad, dc_one = project_back(

time: 626 us -> 580 us (0.927)
  Pallas kernels: 163 us -> 128 us
  waiting for transfers between devices: 186 us -> 172 us
  starting transfers between devices: 121 us -> 130 us
    pallas_call x29, Pallas kernels: 163 us -> 128 us  [run(): pl.pallas_call(inner, in_specs=in_specs, out_specs=[pl.BlockSpec(memory_s...]
    dynamic_update_slice x4 -> x0, local copies, waits for them, and re-layouts: 16.7 us -> none  [join_feed_weights(): ordered = lax.dynamic_update_slice_in_dim(ordered, part, start, 0)]
    ppermute x45, waiting for transfers between devices: 81.1 us -> 68.4 us  [z_shift(): return lax.ppermute(value, 'wsh', [(i, (i + steps) % 4) for i in range(4)])]
    unnamed x226 -> x314, local copies, waits for them, and re-layouts: 39 us -> 46.4 us
  transfers between devices with their start and end apart: 101 -> 101, of which waited for: 42 -> 34; matrix products, arithmetic and copies ran while one was open for 13% -> 12% of each run, Pallas kernels for 20% -> 18%
where the time goes in v3:
time: 580 us; the launch traced here: 570 us
  waiting for transfers between devices  172 us (30%)
  starting transfers between devices  130 us (22%)
  Pallas kernels  128 us (22%)
  local copies, waits for them, and re-layouts  76.2 us (13%)
  other arithmetic  38.3 us (7%)
  between operations  24.1 us (4%)
    pallas_call x29, Pallas kernels, run(): pl.pallas_call(inner, in_specs=in_specs, out_specs=[pl.BlockSpec(memory_s...  128 us
    ppermute x45, waiting for transfers between devices, z_shift(): return lax.ppermute(value, 'wsh', [(i, (i + steps) % 4) for i in range(4)])  68.4 us
    ppermute x39, starting transfers between devices, ctx_shift(): return lax.ppermute(value, ('section', 'ctx'), pairs)  67 us
    ppermute x45, starting transfers between devices, z_shift(): return lax.ppermute(value, 'wsh', [(i, (i + steps) % 4) for i in range(4)])  56.1 us
    ppermute x39, waiting for transfers between devices, ctx_shift(): return lax.ppermute(value, ('section', 'ctx'), pairs)  55.7 us
    unnamed x314, local copies, waits for them, and re-layouts  46.4 us
    all_gather x2, waiting for transfers between devices, whole(): full = lax.all_gather(part, 'wsh', axis=0, tiled=True)  32.6 us
    ppermute x1, waiting for transfers between devices, shards(): grad_down = lax.ppermute(down, ('ctx', 'wsh'), moves)[None]  13 us
  transfers between devices with their start and end apart: 101, of which 34 were waited for; matrix products, arithmetic and copies ran while one was open for 12% of the time, Pallas kernels for 18%

profile of v3, /device:TPU:16, one launch (start us, length us, event | category | flops | bytes accessed | tf_op | source)
XLA Modules:
  0.0 569.6 jit_solution(12297485813646356413)
XLA Ops:
  20.6 32.6 %all-gather.3.cloned.1.call-done.refs_3_.refs_6_.refs_8_.refs_10_ = bf16[960,1376]{1,0:T(8,128)(2,1)} async-done(((bf16[240,1376]{1,0:T(8,128)(2,1)}), bf16[960,1376]{1,0:T(8,128)(2,1)}) %all-gather.3.cloned.1.call-update) | async-done | bytes 2641936 | tf_op jit(solution)/shard_map/all_gather | solution.py:610
  90.3 4.4 collective-permute-done.9.refs_3_
  96.1 5.6 collective-permute-done.10.refs_4_
  116.8 10.6 %shard_map.204 = (bf16[128,960]{1,0:T(8,128)(2,1)S(1)}, f32[2,5,192,128]{3,2,1,0:T(8,128)S(1)}, bf16[2048,640]{1,0:T(8,128)(2,1)S(1)}, f32[128,960]{1,0:T(8,128)S(1)}, bf16[128,960]{1,0:T(8,128)(2,1)S(1)}) custom-call(s32[84]{0:T(128)S(1)} %concatenate.72.refs_0_, bf16[128,1024]{1,0:T(8,128)(2,1)S(1)} %copy-done.127, bf16[512,640]{1,0:T(8,128)(2,1)S(1)} %copy-done.58, ...), custom_call_target="tpu_custom_call" | custom-call | flops 13200000000 | bytes 43200000 | tf_op jit(solution)/shard_map/pallas_call | solution.py:51
  133.7 9.9 %collective-permute-done.14 = bf16[240,1280]{1,0:T(8,128)(2,1)} collective-permute-done((bf16[240,1280]{1,0:T(8,128)(2,1)}, bf16[240,1280]{1,0:T(8,128)(2,1)}, u32[]{:S(2)}, u32[]{:S(2)}) %collective-permute-start.14) | collective-permute-done | bytes 614432 | tf_op jit(solution)/shard_map/ppermute | solution.py:541
  155.1 7.7 %collective-permute-done.18.refs_1_.refs_2_ = bf16[128,960]{1,0:T(8,128)(2,1)S(1)} collective-permute-done((bf16[128,960]{1,0:T(8,128)(2,1)S(1)}, bf16[128,960]{1,0:T(8,128)(2,1)S(1)}, u32[]{:S(2)}, u32[]{:S(2)}) %collective-permute-start.18) | collective-permute-done | bytes 245792 | tf_op jit(solution)/shard_map/ppermute | solution.py:541
  177.7 4.5 collective-permute-done.23.refs_5_
  204.0 11.0 %collective-permute-done.31.refs_10_.refs_1_.refs_14_ = bf16[128,960]{1,0:T(8,128)(2,1)S(1)} collective-permute-done((bf16[128,960]{1,0:T(8,128)(2,1)S(1)}, bf16[128,960]{1,0:T(8,128)(2,1)S(1)}, u32[]{:S(2)}, u32[]{:S(2)}) %collective-permute-start.31) | collective-permute-done | bytes 245792 | tf_op jit(solution)/shard_map/ppermute | solution.py:541
  217.2 4.7 collective-permute-done.33.refs_12_.refs_1_.refs_16_
  227.7 9.4 %shard_map.210 = (bf16[128,960]{1,0:T(8,128)(2,1)S(1)}, f32[2,5,192,128]{3,2,1,0:T(8,128)S(1)}, bf16[2048,640]{1,0:T(8,128)(2,1)S(1)}, f32[128,960]{1,0:T(8,128)S(1)}, bf16[128,960]{1,0:T(8,128)(2,1)S(1)}) custom-call(s32[84]{0:T(128)S(1)} %concatenate.72.refs_0_, bf16[128,1024]{1,0:T(8,128)(2,1)S(1)} %copy-done.114, ...), custom_call_target="tpu_custom_call" | custom-call | flops 13200000000 | bytes 43200000 | tf_op jit(solution)/shard_map/pallas_call | solution.py:51
  243.6 4.8 collective-permute-done.36.refs_7_.refs_8_
  264.8 5.5 collective-permute-start.46
  270.3 6.2 %shard_map.219 = (bf16[16,96,640]{2,1,0:T(8,128)(2,1)S(1)}, bf16[16,96,640]{2,1,0:T(8,128)(2,1)}) custom-call(s32[84]{0:T(128)S(1)} %concatenate.72.refs_0_, bf16[128,960]{1,0:T(8,128)(2,1)S(1)} %get-tuple-element.124.refs_1_, bf16[128,960]{1,0:T(8,128)(2,1)S(1)} %collective-permute-done.37.refs_1_.refs_2_, ...), custom_call_target="tpu_custom_call" | custom-call | flops 7150000128 | bytes 23400000 | tf_op jit(solution)/shard_map/pallas_call | solution.py:51
  276.6 21.4 %shard_map.220 = (f32[128,960]{1,0:T(8,128)S(1)}, bf16[128,960]{1,0:T(8,128)(2,1)S(1)}, f32[1,960]{1,0:T(1,128)S(1)}, bf16[128,960]{1,0:T(8,128)(2,1)S(1)}, bf16...) custom-call(s32[84]{0:T(128)S(1)} %concatenate.72.refs_0_, ...), custom_call_target="tpu_custom_call" | custom-call | flops 26400000000 | bytes 86400000 | tf_op jit(solution)/shard_map/pallas_call | solution.py:51
  304.2 4.4 collective-permute-done.49
  311.4 8.7 %collective-permute-done.47 = bf16[512,640]{1,0:T(8,128)(2,1)S(1)} collective-permute-done((bf16[512,640]{1,0:T(8,128)(2,1)S(1)}, bf16[512,640]{1,0:T(8,128)(2,1)S(1)}, u32[]{:S(2)}, u32[]{:S(2)}) %collective-permute-start.47) | collective-permute-done | bytes 655392 | tf_op jit(solution)/shard_map/ppermute | solution.py:551
  322.4 8.7 %collective-permute-done.53.refs_14_.refs_6_ = bf16[128,1984]{1,0:T(8,128)(2,1)S(1)} collective-permute-done((bf16[128,1984]{1,0:T(8,128)(2,1)}, bf16[128,1984]{1,0:T(8,128)(2,1)S(1)}, u32[]{:S(2)}, u32[]{:S(2)}) %collective-permute-start.53) | collective-permute-done | bytes 507936 | tf_op jit(solution)/shard_map/ppermute | solution.py:541
  384.9 5.7 %shard_map.226 = (bf16[16,96,640]{2,1,0:T(8,128)(2,1)S(1)}, bf16[16,96,640]{2,1,0:T(8,128)(2,1)S(1)}) custom-call(s32[84]{0:T(128)S(1)} %concatenate.72.refs_0_, bf16[128,960]{1,0:T(8,128)(2,1)S(1)} %copy-done.41, bf16[128,960]{1,0:T(8,128)(2,1)S(1)} %copy-done.43, bf16[128,960]{1,0:T(8,128)(2,1)S(1)} %copy-done.45, bf16[128,960]{1,0:T(8,128)(2,1)S(1)} %copy-done.47, ...), custom_call_target="tpu_custom_call" | custom-call | flops 7150000128 | bytes 23400000 | tf_op jit(solution)/shard_map/pallas_call | solution.py:51
  400.3 6.6 %collective-permute-done.61.refs_4_ = bf16[128,960]{1,0:T(8,128)(2,1)S(1)} collective-permute-done((bf16[128,960]{1,0:T(8,128)(2,1)S(1)}, bf16[128,960]{1,0:T(8,128)(2,1)S(1)}, u32[]{:S(2)}, u32[]{:S(2)}) %collective-permute-start.61) | collective-permute-done | bytes 245792 | tf_op jit(solution)/shard_map/ppermute | solution.py:541
  407.1 23.1 %shard_map.227 = (f32[128,960]{1,0:T(8,128)S(1)}, bf16[128,960]{1,0:T(8,128)(2,1)S(1)}, f32[1,960]{1,0:T(1,128)S(1)}, bf16[128,960]{1,0:T(8,128)(2,1)S(1)}, bf16...) custom-call(s32[84]{0:T(128)S(1)} %concatenate.72.refs_0_, ...), custom_call_target="tpu_custom_call" | custom-call | flops 26400000000 | bytes 86400000 | tf_op jit(solution)/shard_map/pallas_call | solution.py:51
  472.0 4.2 shard_map.230
  504.8 5.9 %collective-permute-start.85 = (bf16[4,64,768]{2,1,0:T(8,128)(2,1)}, bf16[4,64,768]{2,1,0:T(8,128)(2,1)}, u32[]{:S(2)}, u32[]{:S(2)}) collective-permute-start(bf16[4,64,768]{2,1,0:T(8,128)(2,1)} %get-tuple-element.282), channel_id=1, source_target_pairs={{0,16},{4,20},{8,24},{12,28},{16,32},{20,36},{24,40},{28,44},{32,4... | collective-permute-start | bytes 1179656 | tf_op jit(solution)/shard_map/ppermute | solution.py:551
  539.9 6.0 %collective-permute-start.98 = (f32[40,960]{1,0:T(8,128)S(1)}, f32[40,960]{1,0:T(8,128)S(1)}, u32[]{:S(2)}, u32[]{:S(2)}) collective-permute-start(f32[40,960]{1,0:T(8,128)S(1)} %maximum_maximum_fusion), channel_id=1, source_target_pairs={{0,0},{1,16},{2,32},{3,48},{4,1},{5,17},{6,33},{7,49},{8,2},{9,18}... | collective-permute-start | bytes 460808 | tf_op jit(solution)/shard_map/ppermute | solution.py:792
  548.6 13.0 %collective-permute-done.98 = f32[40,960]{1,0:T(8,128)S(1)} collective-permute-done((f32[40,960]{1,0:T(8,128)S(1)}, f32[40,960]{1,0:T(8,128)S(1)}, u32[]{:S(2)}, u32[]{:S(2)}) %collective-permute-start.98) | collective-permute-done | bytes 153632 | tf_op jit(solution)/shard_map/ppermute | solution.py:792
  (646 shorter events, 320.6 us)
Async XLA Ops:
  7.2 46.0 %all-gather.3.cloned.1.call-start = ((), (), s32[]{:S(2)}) async-start(), calls=%async_computation | async-start | bytes 3379200 | tf_op jit(solution)/shard_map/all_gather | solution.py:610
  14.8 132.4 %all-gather.5.cloned.1.call-start = ((), (), s32[]{:S(2)}) async-start(), calls=%async_computation.1 | async-start | bytes 3379200 | tf_op jit(solution)/shard_map/all_gather | solution.py:610
  14.8 45.1 %collective-permute-start.2 = (bf16[2,240]{1,0:T(2,128)(2,1)S(1)}, bf16[2,240]{1,0:T(2,128)(2,1)S(1)}, u32[]{:S(2)}, u32[]{:S(2)}) collective-permute-start(bf16[2,240]{1,0:T(2,128)(2,1)S(1)} %pad_maximum_fusion.13), channel_id=1, source_target_pairs={{0,3},{1,0},{2,1},{3,2},{4,7},{5,4},{6,5},{7,6},{8,11},{9,8},{10,9... | collective-permute-start | bytes 2888 | tf_op jit(solution)/shard_map/ppermute | solution.py:541
  18.9 41.6 %collective-permute-start.1 = (bf16[2,240]{1,0:T(2,128)(2,1)S(1)}, bf16[2,240]{1,0:T(2,128)(2,1)S(1)}, u32[]{:S(2)}, u32[]{:S(2)}) collective-permute-start(bf16[2,240]{1,0:T(2,128)(2,1)S(1)} %pad_maximum_fusion.13), channel_id=1, source_target_pairs={{0,2},{1,3},{2,0},{3,1},{4,6},{5,7},{6,4},{7,5},{8,10},{9,11},{10,... | collective-permute-start | bytes 2888 | tf_op jit(solution)/shard_map/ppermute | solution.py:541
  18.9 41.6 %collective-permute-start = (bf16[2,240]{1,0:T(2,128)(2,1)S(1)}, bf16[2,240]{1,0:T(2,128)(2,1)S(1)}, u32[]{:S(2)}, u32[]{:S(2)}) collective-permute-start(bf16[2,240]{1,0:T(2,128)(2,1)S(1)} %pad_maximum_fusion.13), channel_id=1, source_target_pairs={{0,1},{1,2},{2,3},{3,0},{4,5},{5,6},{6,7},{7,4},{8,9},{9,10},{10,1... | collective-permute-start | bytes 2888 | tf_op jit(solution)/shard_map/ppermute | solution.py:541
  20.2 44.2 %collective-permute-start.12 = (bf16[640,960]{0,1:T(8,128)(2,1)}, bf16[640,960]{0,1:T(8,128)(2,1)}, u32[]{:S(2)}, u32[]{:S(2)}) collective-permute-start(bf16[640,960]{0,1:T(8,128)(2,1)} %bitcast.139), channel_id=1, source_target_pairs={{0,64},{64,0},{1,65},{65,1},{2,66},{66,2},{3,67},{67,3},{4,68},{68... | collective-permute-start | bytes 3686408 | tf_op jit(solution)/shard_map/ppermute | solution.py:563
  59.9 27.4 %collective-permute-start.13 = (bf16[240,2560]{1,0:T(8,128)(2,1)}, bf16[240,2560]{1,0:T(8,128)(2,1)}, u32[]{:S(2)}, u32[]{:S(2)}) collective-permute-start(bf16[240,2560]{1,0:T(8,128)(2,1)} %bitcast_select_fusion.3), channel_id=1, source_target_pairs={{0,64},{64,0},{1,65},{65,1},{2,66},{66,2},{3,67},{67,3},{4,68},{68... | collective-permute-start | bytes 3686408 | tf_op jit(solution)/shard_map/ppermute | solution.py:563
  111.4 22.2 %collective-permute-start.16 = (bf16[240,1280]{1,0:T(8,128)(2,1)}, bf16[240,1280]{1,0:T(8,128)(2,1)}, u32[]{:S(2)}, u32[]{:S(2)}) collective-permute-start(bf16[240,1280]{1,0:T(8,128)(2,1)} %pad_maximum_fusion.5), channel_id=1, source_target_pairs={{0,3},{1,0},{2,1},{3,2},{4,7},{5,4},{6,5},{7,6},{8,11},{9,8},{10,9... | collective-permute-start | bytes 1843208 | tf_op jit(solution)/shard_map/ppermute | solution.py:541
  115.8 27.8 %collective-permute-start.14 = (bf16[240,1280]{1,0:T(8,128)(2,1)}, bf16[240,1280]{1,0:T(8,128)(2,1)}, u32[]{:S(2)}, u32[]{:S(2)}) collective-permute-start(bf16[240,1280]{1,0:T(8,128)(2,1)} %pad_maximum_fusion.3), channel_id=1, source_target_pairs={{0,1},{1,2},{2,3},{3,0},{4,5},{5,6},{6,7},{7,4},{8,9},{9,10},{10,1... | collective-permute-start | bytes 1843208 | tf_op jit(solution)/shard_map/ppermute | solution.py:541
  147.2 28.1 %collective-permute-start.24 = (bf16[960,1376]{1,0:T(8,128)(2,1)}, bf16[960,1376]{1,0:T(8,128)(2,1)S(1)}, u32[]{:S(2)}, u32[]{:S(2)}) collective-permute-start(bf16[960,1376]{1,0:T(8,128)(2,1)} %all-gather.5.cloned.1.call-done.refs_7_.refs_6_.refs_8_.refs_10_), channel_id=1, source_target_pairs={{0,64},{64,0},{1,65},{65,1},{2,66},{66,2},{3,67},{67,3},{4,68},{68... | collective-permute-start | bytes 7925768 | tf_op jit(solution)/shard_map/ppermute | solution.py:563
  197.8 24.1 %collective-permute-start.28 = (bf16[512,640]{1,0:T(8,128)(2,1)S(1)}, bf16[512,640]{1,0:T(8,128)(2,1)S(1)}, u32[]{:S(2)}, u32[]{:S(2)}) collective-permute-start(bf16[512,640]{1,0:T(8,128)(2,1)S(1)} %constant_dynamic-update-slice_fusion.4.refs_2_), channel_id=1, source_target_pairs={{0,16},{4,20},{8,24},{12,28},{16,32},{20,36},{24,40},{28,44},{32,4... | collective-permute-start | bytes 1966088 | tf_op jit(solution)/shard_map/ppermute | solution.py:551
  199.6 24.6 %collective-permute-start.29 = (bf16[512,640]{1,0:T(8,128)(2,1)S(1)}, bf16[512,640]{1,0:T(8,128)(2,1)S(1)}, u32[]{:S(2)}, u32[]{:S(2)}) collective-permute-start(bf16[512,640]{1,0:T(8,128)(2,1)S(1)} %constant_dynamic-update-slice_fusion.4.refs_2_), channel_id=1, source_target_pairs={{0,32},{4,36},{8,40},{12,44},{16,48},{20,52},{24,56},{28,60},{32,0... | collective-permute-start | bytes 1966088 | tf_op jit(solution)/shard_map/ppermute | solution.py:551
  200.6 23.5 %collective-permute-start.30 = (bf16[512,640]{1,0:T(8,128)(2,1)S(1)}, bf16[512,640]{1,0:T(8,128)(2,1)S(1)}, u32[]{:S(2)}, u32[]{:S(2)}) collective-permute-start(bf16[512,640]{1,0:T(8,128)(2,1)S(1)} %constant_dynamic-update-slice_fusion.4.refs_2_), channel_id=1, source_target_pairs={{0,48},{4,52},{8,56},{12,60},{16,0},{20,4},{24,8},{28,12},{32,16},... | collective-permute-start | bytes 1966088 | tf_op jit(solution)/shard_map/ppermute | solution.py:551
  215.1 28.5 %collective-permute-start.34 = (bf16[128,1984]{1,0:T(8,128)(2,1)S(1)}, bf16[128,1984]{1,0:T(8,128)(2,1)S(1)}, u32[]{:S(2)}, u32[]{:S(2)}) collective-permute-start(bf16[128,1984]{1,0:T(8,128)(2,1)S(1)} %copy-done.81), channel_id=1, source_target_pairs={{0,1},{1,2},{2,3},{3,0},{4,5},{5,6},{6,7},{7,4},{8,9},{9,10},{10,1... | collective-permute-start | bytes 1523720 | tf_op jit(solution)/shard_map/ppermute | solution.py:541
  221.9 26.4 %collective-permute-start.36 = (bf16[128,1984]{1,0:T(8,128)(2,1)S(1)}, bf16[128,1984]{1,0:T(8,128)(2,1)S(1)}, u32[]{:S(2)}, u32[]{:S(2)}) collective-permute-start(bf16[128,1984]{1,0:T(8,128)(2,1)S(1)} %copy-done.81), channel_id=1, source_target_pairs={{0,3},{1,0},{2,1},{3,2},{4,7},{5,4},{6,5},{7,6},{8,11},{9,8},{10,9... | collective-permute-start | bytes 1523720 | tf_op jit(solution)/shard_map/ppermute | solution.py:541
  237.4 23.8 %collective-permute-start.41 = (bf16[128,960]{1,0:T(8,128)(2,1)S(1)}, bf16[128,960]{1,0:T(8,128)(2,1)S(1)}, u32[]{:S(2)}, u32[]{:S(2)}) collective-permute-start(bf16[128,960]{1,0:T(8,128)(2,1)S(1)} %get-tuple-element.124.refs_1_), channel_id=1, source_target_pairs={{0,3},{1,0},{2,1},{3,2},{4,7},{5,4},{6,5},{7,6},{8,11},{9,8},{10,9... | collective-permute-start | bytes 737288 | tf_op jit(solution)/shard_map/ppermute | solution.py:541
  303.7 74.6 %collective-permute-start.62 = (bf16[16,96,640]{2,1,0:T(8,128)(2,1)}, bf16[16,96,640]{2,1,0:T(8,128)(2,1)}, u32[]{:S(2)}, u32[]{:S(2)}) collective-permute-start(bf16[16,96,640]{2,1,0:T(8,128)(2,1)} %get-tuple-element.179), channel_id=1, source_target_pairs={{0,64},{64,0},{1,65},{65,1},{2,66},{66,2},{3,67},{67,3},{4,68},{68... | collective-permute-start | bytes 5898248 | tf_op jit(solution)/shard_map/ppermute | solution.py:563
  303.7 27.4 %collective-permute-start.53 = (bf16[128,1984]{1,0:T(8,128)(2,1)}, bf16[128,1984]{1,0:T(8,128)(2,1)S(1)}, u32[]{:S(2)}, u32[]{:S(2)}) collective-permute-start(bf16[128,1984]{1,0:T(8,128)(2,1)} %get-tuple-element.158.refs_5_), channel_id=1, source_target_pairs={{0,1},{1,2},{2,3},{3,0},{4,5},{5,6},{6,7},{7,4},{8,9},{9,10},{10,1... | collective-permute-start | bytes 1523720 | tf_op jit(solution)/shard_map/ppermute | solution.py:541
  308.6 23.9 %collective-permute-start.54 = (bf16[128,1984]{1,0:T(8,128)(2,1)}, bf16[128,1984]{1,0:T(8,128)(2,1)S(1)}, u32[]{:S(2)}, u32[]{:S(2)}) collective-permute-start(bf16[128,1984]{1,0:T(8,128)(2,1)} %get-tuple-element.158.refs_5_), channel_id=1, source_target_pairs={{0,2},{1,3},{2,0},{3,1},{4,6},{5,7},{6,4},{7,5},{8,10},{9,11},{10,... | collective-permute-start | bytes 1523720 | tf_op jit(solution)/shard_map/ppermute | solution.py:541
  311.4 24.7 %collective-permute-start.55 = (bf16[128,1984]{1,0:T(8,128)(2,1)}, bf16[128,1984]{1,0:T(8,128)(2,1)}, u32[]{:S(2)}, u32[]{:S(2)}) collective-permute-start(bf16[128,1984]{1,0:T(8,128)(2,1)} %get-tuple-element.158.refs_5_), channel_id=1, source_target_pairs={{0,3},{1,0},{2,1},{3,2},{4,7},{5,4},{6,5},{7,6},{8,11},{9,8},{10,9... | collective-permute-start | bytes 1523720 | tf_op jit(solution)/shard_map/ppermute | solution.py:541
  358.2 76.1 %collective-permute-start.43 = (f32[128,960]{1,0:T(8,128)}, f32[128,960]{1,0:T(8,128)}, u32[]{:S(2)}, u32[]{:S(2)}) collective-permute-start(f32[128,960]{1,0:T(8,128)} %get-tuple-element.264), channel_id=1, source_target_pairs={{0,64},{64,0},{1,65},{65,1},{2,66},{66,2},{3,67},{67,3},{4,68},{68... | collective-permute-start | bytes 1474568 | tf_op jit(solution)/shard_map/ppermute | solution.py:563
  372.6 24.7 %collective-permute-start.57 = (bf16[128,960]{1,0:T(8,128)(2,1)S(1)}, bf16[128,960]{1,0:T(8,128)(2,1)S(1)}, u32[]{:S(2)}, u32[]{:S(2)}) collective-permute-start(bf16[128,960]{1,0:T(8,128)(2,1)S(1)} %get-tuple-element.163), channel_id=1, source_target_pairs={{0,3},{1,0},{2,1},{3,2},{4,7},{5,4},{6,5},{7,6},{8,11},{9,8},{10,9... | collective-permute-start | bytes 737288 | tf_op jit(solution)/shard_map/ppermute | solution.py:541
  439.2 43.4 %collective-permute-start.73 = (bf16[16,96,640]{2,1,0:T(8,128)(2,1)}, bf16[16,96,640]{2,1,0:T(8,128)(2,1)}, u32[]{:S(2)}, u32[]{:S(2)}) collective-permute-start(bf16[16,96,640]{2,1,0:T(8,128)(2,1)} %copy-done.73), channel_id=1, source_target_pairs={{0,64},{64,0},{1,65},{65,1},{2,66},{66,2},{3,67},{67,3},{4,68},{68... | collective-permute-start | bytes 5898248 | tf_op jit(solution)/shard_map/ppermute | solution.py:563
  441.8 27.2 %collective-permute-start.81 = (bf16[128,640]{1,0:T(8,128)(2,1)S(1)}, bf16[128,640]{1,0:T(8,128)(2,1)S(1)}, u32[]{:S(2)}, u32[]{:S(2)}) collective-permute-start(bf16[128,640]{1,0:T(8,128)(2,1)S(1)} %get-tuple-element.312), channel_id=1, source_target_pairs={{0,1},{1,2},{2,3},{3,0},{4,5},{5,6},{6,7},{7,4},{8,9},{9,10},{10,1... | collective-permute-start | bytes 491528 | tf_op jit(solution)/shard_map/ppermute | solution.py:541
  (229 other events, 2595.6 us)
Sparse Core Ops, SparseCore 0:
  14.9 38.2 all-gather.2
  64.6 36.1 all-gather.4

commit v4 on v3

--- a/solution.py
+++ b/solution.py
@@ -62,6 +62,25 @@
         return out
 
     return run
+
+
+def token(*arrays):
+    return jnp.stack([a[(0,) * a.ndim].astype(F32) for a in arrays])
+
+
+def hold(arrays, mark):
+    count = len(arrays)
+
+    def body(*refs):
+        del refs
+
+    return pl.pallas_call(
+        body,
+        in_specs=[pl.BlockSpec(memory_space=pl.ANY)] * (count + 1),
+        out_specs=[pl.BlockSpec(memory_space=pl.ANY)] * count,
+        out_shape=[jax.ShapeDtypeStruct(a.shape, a.dtype) for a in arrays],
+        input_output_aliases={i: i for i in range(count)},
+    )(*arrays, mark)
 
 
 def lane(shape):
@@ -235,7 +254,7 @@
     shape = (2, KV_HEADS, GROUP * BLK, 128)
     scratch = [pltpu.VMEM(shape, BF)] + [pltpu.VMEM(shape, F32)] * 3
     scratch.append(pltpu.VMEM((2, ROWS, D // 2), F32))
-    return call(attend_body(len(pieces)), outs, 12.0, 24, scratch, smem=1)(
+    return call(attend_body(len(pieces)), outs, 12.0, 18, scratch, smem=1)(
         info, q, *pieces, *wo, x, gain, after=after
     )
 
@@ -375,7 +394,7 @@
         pltpu.VMEM((ROWS, QP), BF),
         pltpu.VMEM((2, ROWS, D // 2), BF),
     ]
-    return call(attend_back_body, outs, 24.0, 32, scratch, smem=1)(
+    return call(attend_back_body, outs, 24.0, 22, scratch, smem=1)(
         info, *parts, grad, resid, gain, *wo, normed, mixed, q, lse, kvs, cosine, sine, after=after
     )
 
@@ -464,7 +483,7 @@
         pltpu.VMEM((640, D), F32),
         pltpu.VMEM((96, 640), F32),
     ]
-    return call(feed_grads_body, [((16, 96, 640), BF)] * 2, 6.5, 24, scratch, smem=1)(
+    return call(feed_grads_body, [((16, 96, 640), BF)] * 2, 6.5, 20, scratch, smem=1)(
         info, *seconds, *dgus, *hiddens, *lows, after=after
     )
 
@@ -494,7 +513,7 @@
             out[slot_of(info, c, turn)] = group[...].astype(BF)
 
 
-def attend_grads(info, mines, aheads, dc_one, dc_two):
+def attend_grads(info, mines, aheads, dc_one, dc_two, after=()):
     rows = 4 * ROWS
     scratch = [
         pltpu.VMEM((2, rows, D), BF),
@@ -503,7 +522,7 @@
         pltpu.VMEM((64, 384), F32),
     ]
     return call(attend_grads_body, [((16, 64, 384), BF)] * 2, 3.0, 16, scratch, smem=1)(
-        info, *mines, *aheads, dc_one, dc_two
+        info, *mines, *aheads, dc_one, dc_two, after=after
     )
 
 
@@ -606,12 +625,6 @@
     got = swap(jnp.where(first_core, high_half, low_half))
     layer_half = (jnp.where(first_core, low_half, got), jnp.where(first_core, got, high_half))
 
-    def whole(part):
-        full = lax.all_gather(part, "wsh", axis=0, tiled=True)
-        return full, swap(full)
-
-    gathered = tuple(whole(part) for part in layer_half)
-
     gains = jnp.stack([norm_one[0], norm_two[0]])
     gain_parts = [gains] + [z_shift(gains, k) for k in (1, 2, 3)]
     gains = jnp.concatenate(in_order(gain_parts, z_rank), axis=1)
@@ -625,16 +638,17 @@
     def none_of(mark):
         return (mark != mark).astype(jnp.int32)
 
+    def columns(z):
+        start = z * quarter
+        return jnp.concatenate(
+            [lax.dynamic_slice_in_dim(k, start, quarter, 1) for k in kind], axis=1
+        )
+
+    feed_columns = [columns((z_rank + k) % 4) for k in range(4)]
+
     def send_feed_weights(mark):
-        later = none_of(mark)
-
-        def columns(z):
-            start = z * quarter + later
-            return jnp.concatenate(
-                [lax.dynamic_slice_in_dim(k, start, quarter, 1) for k in kind], axis=1
-            )
-
-        return [columns(z_rank)] + [z_shift(columns((z_rank + k) % 4), k) for k in (1, 2, 3)]
+        sent = hold(feed_columns[1:], mark)
+        return feed_columns[:1] + [z_shift(sent[k - 1], k) for k in (1, 2, 3)]
 
     def join_feed_weights(parts, mark):
         later = none_of(mark)
@@ -673,6 +687,17 @@
         return [value] + [z_shift(value, k) for k in (1, 2, 3)]
 
     last_lows = z_gather(own_cotangent.astype(BF))
+
+    def whole(part, *before):
+        full = lax.all_gather(part, "wsh", axis=0, tiled=True)
+        if before:
+            (full,) = hold([full], token(*before))
+        return full, swap(full)
+
+    gathered = (
+        whole(layer_half[0], info, cosine, sine, own_tokens, *wd, *last_lows[1:], *feed_columns, *gain_pair),
+        whole(layer_half[1]),
+    )
     saved = []
     base, parts = own_tokens, []
     for layer in range(2):
@@ -687,14 +712,14 @@
         row = jnp.concatenate([kv] + [gather_shift(kv, k) for k in (1, 2, 3)], axis=0)
         pieces = [row] + [reduce_shift(row, k) for k in (1, 2, 3)]
         if layer == 0:
-            sent = send_feed_weights(pieces[1][0, 0] + pieces[2][0, 0] + pieces[3][0, 0])
+            sent = send_feed_weights(token(*pieces[1:]))
         mixed, lse, kvs, resid, second = attend(
-            info, q, pieces, gathered[layer], x_in, gain_two, after=last_lows[1:] if layer else wd
+            info, q, pieces, gathered[layer], x_in, gain_two, after=() if layer else (token(*wd),)
         )
+        seconds = z_gather(second)
         if layer == 0:
-            wgu = join_feed_weights(sent, second[0, 0])
-        seconds = z_gather(second)
-        after = first_aheads[1:] if layer else ()
+            wgu = join_feed_weights(sent, seconds[1][0, 0])
+        after = (token(*first_aheads[1:]),) if layer else ()
         fed = [feed(layer, info, s, wgu[layer], wd[layer], after) for s in seconds]
         parts = [fed[0][2]] + [z_shift(fed[k][2], -k) for k in (1, 2, 3)]
         base = resid
@@ -710,12 +735,11 @@
     grad = own_cotangent
     lows = last_lows
     input_grads = [None, None]
-    feed_sums = [None, None]
+    feed_halves = [None, None]
     kept = [None, None]
-    order = ()
-
-    def stage_one(half, later=0):
-        cut = [lax.dynamic_slice_in_dim(half, 4 * k + later, 4, 0) for k in range(4)]
+
+    def stage_one(half):
+        cut = [half[4 * k : 4 * k + 4] for k in range(4)]
         return add(cut[0], *[reduce_shift(cut[k], k) for k in (1, 2, 3)])
 
     def stage_two(stage):
@@ -731,9 +755,9 @@
         keep, give = feed_grads(info, s["seconds"], [b[0] for b in back], s["hidden"], lows)
         d_resid, d_low, dc_two, dq, ahead, *goes_out = attend_back(
             info, parts, grad, s["resid"], gain_two, gathered[layer], s["normed"], s["mixed"], s["q"],
-            s["lse"], s["kvs"], cosine, sine, after=(keep, *order),
+            s["lse"], s["kvs"], cosine, sine, after=(token(keep),),
         )
-        feed_half = add(keep, swap(give)).astype(BF)
+        feed_halves[layer] = add(keep, swap(give)).astype(BF)
         row = add(goes_out[0], *[reduce_shift(goes_out[k], k) for k in (1, 2, 3)])
         row = row.astype(BF).reshape(4, ROWS, 2 * KW)
         own_pieces = [row[0]] + [gather_shift(row[k], k) for k in (1, 2, 3)]
@@ -742,28 +766,30 @@
             kept[1] = attention_grads(none_of(d_low[0, 0]))
         cut, grad, dc_one = project_back(
             info, own_pieces, dq, d_resid, d_low, s["x"], gain_one, gathered[layer], cosine, sine,
-            after=tuple(aheads[1:]) if layer else (),
+            after=(token(*aheads[1:]),) if layer else (),
         )
         input_grads[layer] = grad
-        feed_stage = stage_one(feed_half, none_of(cut[0, 0, 0]))
         if layer:
             lows = z_gather(grad.astype(BF))
-            order = (feed_stage,)
-            feed_sums[1] = stage_two(feed_stage)
-
-        def attention_grads(later, cut=cut, aheads=aheads, dc_one=dc_one, dc_two=dc_two):
+
+        def attention_grads(later, after=(), cut=cut, aheads=aheads, dc_one=dc_one, dc_two=dc_two):
             mines = [lax.dynamic_index_in_dim(cut, k + later, 0, False) for k in range(4)]
             mines = [mines[0]] + [z_shift(mines[k], k) for k in (1, 2, 3)]
-            keep, give = attend_grads(info, mines, aheads, dc_one, dc_two)
+            keep, give = attend_grads(info, mines, aheads, dc_one, dc_two, after)
             return add(keep, swap(give)).astype(BF)
 
         if layer == 0:
-            kept[0] = attention_grads(0)
+            feed_stage = stage_one(jnp.concatenate(hold(feed_halves, token(cut)), axis=1))
+            kept[0] = attention_grads(0, (token(feed_stage),))
     attend_stage = stage_one(jnp.concatenate(kept, axis=2))
     both_sums = stage_two(
-        jnp.concatenate([feed_stage, jnp.pad(attend_stage, ((0, 0), (0, 32), (0, 0)))], axis=2)
-    )
-    feed_sums[0], attend_sum = both_sums[:, :640], both_sums[:64, 640:]
+        jnp.concatenate(
+            [feed_stage[:, :96], feed_stage[:, 96:], jnp.pad(attend_stage, ((0, 0), (0, 32), (0, 0)))],
+            axis=2,
+        )
+    )
+    feed_sums = (both_sums[:, :640], both_sums[:, 640:1280])
+    attend_sum = both_sums[:64, 1280:]
     sums = [
         jnp.concatenate(
             [feed_sums[layer], jnp.pad(attend_sum[:, layer * 384 : (layer + 1) * 384], ((0, 32), (0, 0)))],

time: 580 us -> 576 us (level)
  waiting for transfers between devices: 172 us -> 147 us
  starting transfers between devices: 130 us -> 142 us
  other arithmetic: 38.3 us -> 46.2 us
    all_gather x2, waiting for transfers between devices: 32.6 us -> 0.02 us  [whole(): full = lax.all_gather(part, 'wsh', axis=0, tiled=True)]
    ppermute x45, starting transfers between devices: 56.1 us -> 71.7 us  [z_shift(): return lax.ppermute(value, 'wsh', [(i, (i + steps) % 4) for i in range(4)])]
    ppermute x39 -> x33, waiting for transfers between devices: 55.7 us -> 68 us  [ctx_shift(): return lax.ppermute(value, ('section', 'ctx'), pairs)]
    slice x7 -> x28, local copies, waits for them, and re-layouts: 3.13 us -> 14.3 us  [the longest x24 13.4 us: token(): return jnp.stack([a[(0,) * a.ndim].astype(F32) for a in arrays])]
    unnamed x314 -> x249, local copies, waits for them, and re-layouts: 46.4 us -> 36.9 us
    another operation x0 -> x1, local copies, waits for them, and re-layouts: none -> 9.37 us  [token(): return jnp.stack([a[(0,) * a.ndim].astype(F32) for a in arrays])]
    ppermute x45, waiting for transfers between devices: 68.4 us -> 60.4 us  [z_shift(): return lax.ppermute(value, 'wsh', [(i, (i + steps) % 4) for i in range(4)])]
    another operation x0 -> x4, other arithmetic: none -> 6.63 us  [token(): return jnp.stack([a[(0,) * a.ndim].astype(F32) for a in arrays])]
  transfers between devices with their start and end apart: 101 -> 95, of which waited for: 34 -> 42; matrix products, arithmetic and copies ran while one was open for 12% -> 15% of each run, Pallas kernels for 18% -> 16%
where the time goes in v4:
time: 576 us; the launch traced here: 566 us
  waiting for transfers between devices  147 us (26%)
  starting transfers between devices  142 us (25%)
  Pallas kernels  126 us (22%)
  local copies, waits for them, and re-layouts  81.7 us (14%)
  other arithmetic  46.2 us (8%)
  between operations  22.3 us (4%)
    pallas_call x29, Pallas kernels, run(): pl.pallas_call(inner, in_specs=in_specs, out_specs=[pl.BlockSpec(memory_s...  126 us
    ppermute x45, starting transfers between devices, z_shift(): return lax.ppermute(value, 'wsh', [(i, (i + steps) % 4) for i in range(4)])  71.7 us
    ppermute x33, waiting for transfers between devices, ctx_shift(): return lax.ppermute(value, ('section', 'ctx'), pairs)  68 us
    ppermute x33, starting transfers between devices, ctx_shift(): return lax.ppermute(value, ('section', 'ctx'), pairs)  62.3 us
    ppermute x45, waiting for transfers between devices, z_shift(): return lax.ppermute(value, 'wsh', [(i, (i + steps) % 4) for i in range(4)])  60.4 us
    unnamed x249, local copies, waits for them, and re-layouts  36.9 us
    slice x24, local copies, waits for them, and re-layouts, token(): return jnp.stack([a[(0,) * a.ndim].astype(F32) for a in arrays])  13.4 us
    ppermute x1, waiting for transfers between devices, shards(): grad_down = lax.ppermute(down, ('ctx', 'wsh'), moves)[None]  13.1 us
  transfers between devices with their start and end apart: 95, of which 42 were waited for; matrix products, arithmetic and copies ran while one was open for 15% of the time, Pallas kernels for 16%

profile of v4, /device:TPU:16, one launch (start us, length us, event | category | flops | bytes accessed | tf_op | source)
XLA Modules:
  0.0 565.5 jit_solution(16426233770351458234)
XLA Ops:
  42.2 6.3 %collective-permute-done.7.refs_1_.refs_15_ = bf16[128,960]{1,0:T(8,128)(2,1)S(1)} collective-permute-done((bf16[128,960]{1,0:T(8,128)(2,1)S(1)}, bf16[128,960]{1,0:T(8,128)(2,1)S(1)}, u32[]{:S(2)}, u32[]{:S(2)}) %collective-permute-start.7) | collective-permute-done | bytes 245792 | tf_op jit(solution)/shard_map/ppermute | solution.py:560
  64.3 9.4 %stack.215.refs_1_ = f32[15]{0:T(128)} concatenate(f32[1]{0:T(128)} %bitcast.22, f32[1]{0:T(128)} %bitcast.23, f32[1]{0:T(128)} %bitcast.24, f32[1]{0:T(128)} %bitcast.25, bf16[1]{0:T(256)(128)(2,1)} %bitcast.42, bf16[1]{0:T(256)(128)(2,1)} %bitcast.43, bf16[1]{0:T(256)(128)(2,1)} %bitcast.96, bf16[1]{0:T(256)(128)(2,1)} %bitcast.97, bf16[1]{0:T(256)(128)(2,1)} %bitcast.98, ...), dimensions={0} | concatenate | bytes 102 | tf_op jit(solution)/shard_map/stack | solution.py:68
  102.1 12.7 %collective-permute-done.16.refs_5_ = bf16[512,640]{1,0:T(8,128)(2,1)S(1)} collective-permute-done((bf16[512,640]{1,0:T(8,128)(2,1)S(1)}, bf16[512,640]{1,0:T(8,128)(2,1)S(1)}, u32[]{:S(2)}, u32[]{:S(2)}) %collective-permute-start.16) | collective-permute-done | bytes 655392 | tf_op jit(solution)/shard_map/ppermute | solution.py:570
  131.8 10.6 %shard_map.205 = (bf16[128,960]{1,0:T(8,128)(2,1)S(1)}, f32[2,5,192,128]{3,2,1,0:T(8,128)S(1)}, bf16[2048,640]{1,0:T(8,128)(2,1)S(1)}, f32[128,960]{1,0:T(8,128)S(1)}, bf16[128,960]{1,0:T(8,128)(2,1)S(1)}) custom-call(s32[84]{0:T(128)S(1)} %concatenate.75.refs_0_, bf16[128,1024]{1,0:T(8,128)(2,1)S(1)} %copy-done.81, bf16[512,640]{1,0:T(8,128)(2,1)S(1)} %copy-done.42, ...), custom_call_target="tpu_custom_call" | custom-call | flops 13200000000 | bytes 43200000 | tf_op jit(solution)/shard_map/pallas_call | solution.py:51
  145.8 9.8 %collective-permute-done.20.refs_1_.refs_2_ = bf16[128,960]{1,0:T(8,128)(2,1)S(1)} collective-permute-done((bf16[128,960]{1,0:T(8,128)(2,1)S(1)}, bf16[128,960]{1,0:T(8,128)(2,1)S(1)}, u32[]{:S(2)}, u32[]{:S(2)}) %collective-permute-start.20) | collective-permute-done | bytes 245792 | tf_op jit(solution)/shard_map/ppermute | solution.py:560
  183.3 5.0 collective-permute-done.26.refs_5_
  195.9 10.5 %collective-permute-start.30 = (bf16[128,640]{1,0:T(8,128)(2,1)S(1)}, bf16[128,640]{1,0:T(8,128)(2,1)S(1)}, u32[]{:S(2)}, u32[]{:S(2)}) collective-permute-start(bf16[128,640]{1,0:T(8,128)(2,1)S(1)} %get-tuple-element.130), channel_id=1, source_target_pairs={{0,12},{4,0},{8,4},{12,8},{16,28},{20,16},{24,20},{28,24},{32,44},... | collective-permute-start | bytes 491528 | tf_op jit(solution)/shard_map/ppermute | solution.py:570
  216.5 13.6 %collective-permute-done.35.refs_7_ = bf16[128,1984]{1,0:T(8,128)(2,1)S(1)} collective-permute-done((bf16[128,1984]{1,0:T(8,128)(2,1)S(1)}, bf16[128,1984]{1,0:T(8,128)(2,1)S(1)}, u32[]{:S(2)}, u32[]{:S(2)}) %collective-permute-start.35) | collective-permute-done | bytes 507936 | tf_op jit(solution)/shard_map/ppermute | solution.py:560
  231.4 5.9 %collective-permute-done.34.refs_6_ = bf16[128,1984]{1,0:T(8,128)(2,1)S(1)} collective-permute-done((bf16[128,1984]{1,0:T(8,128)(2,1)S(1)}, bf16[128,1984]{1,0:T(8,128)(2,1)S(1)}, u32[]{:S(2)}, u32[]{:S(2)}) %collective-permute-start.34) | collective-permute-done | bytes 507936 | tf_op jit(solution)/shard_map/ppermute | solution.py:560
  238.6 9.3 %shard_map.212 = (bf16[128,960]{1,0:T(8,128)(2,1)S(1)}, f32[2,5,192,128]{3,2,1,0:T(8,128)S(1)}, bf16[2048,640]{1,0:T(8,128)(2,1)S(1)}, f32[128,960]{1,0:T(8,128)S(1)}, bf16[128,960]{1,0:T(8,128)(2,1)S(1)}) custom-call(s32[84]{0:T(128)S(1)} %concatenate.75.refs_0_, bf16[128,1024]{1,0:T(8,128)(2,1)S(1)} %get-tuple-element.129.refs_1_.refs_12_, ...), custom_call_target="tpu_custom_call" | custom-call | flops 13200000000 | bytes 43200000 | tf_op jit(solution)/shard_map/pallas_call | solution.py:51
  258.1 5.0 collective-permute-done.37.refs_1_.refs_2_
  278.4 6.2 %shard_map.221 = (bf16[16,96,640]{2,1,0:T(8,128)(2,1)S(1)}, bf16[16,96,640]{2,1,0:T(8,128)(2,1)}) custom-call(s32[84]{0:T(128)S(1)} %concatenate.75.refs_0_, bf16[128,960]{1,0:T(8,128)(2,1)S(1)} %get-tuple-element.132.refs_1_, bf16[128,960]{1,0:T(8,128)(2,1)S(1)} %collective-permute-done.37.refs_1_.refs_2_, ...), custom_call_target="tpu_custom_call" | custom-call | flops 7150000128 | bytes 23400000 | tf_op jit(solution)/shard_map/pallas_call | solution.py:51
  287.1 20.5 %shard_map.222 = (f32[128,960]{1,0:T(8,128)S(1)}, bf16[128,960]{1,0:T(8,128)(2,1)S(1)}, f32[1,960]{1,0:T(1,128)S(1)}, bf16[128,960]{1,0:T(8,128)(2,1)S(1)}, bf16...) custom-call(s32[84]{0:T(128)S(1)} %concatenate.75.refs_0_, ...), custom_call_target="tpu_custom_call" | custom-call | flops 26400000000 | bytes 86400000 | tf_op jit(solution)/shard_map/pallas_call | solution.py:51
  321.3 9.1 %collective-permute-done.47 = bf16[512,640]{1,0:T(8,128)(2,1)S(1)} collective-permute-done((bf16[512,640]{1,0:T(8,128)(2,1)S(1)}, bf16[512,640]{1,0:T(8,128)(2,1)S(1)}, u32[]{:S(2)}, u32[]{:S(2)}) %collective-permute-start.47) | collective-permute-done | bytes 655392 | tf_op jit(solution)/shard_map/ppermute | solution.py:570
  367.1 6.4 %shard_map.228 = (bf16[16,96,640]{2,1,0:T(8,128)(2,1)S(1)}, bf16[16,96,640]{2,1,0:T(8,128)(2,1)}) custom-call(s32[84]{0:T(128)S(1)} %concatenate.75.refs_0_, bf16[128,960]{1,0:T(8,128)(2,1)S(1)} %copy-done.31, bf16[128,960]{1,0:T(8,128)(2,1)S(1)} %copy-done.33, bf16[128,960]{1,0:T(8,128)(2,1)S(1)} %collective-permute-done.23.refs_1_.refs_3_, ...), custom_call_target="tpu_custom_call" | custom-call | flops 7150000128 | bytes 23400000 | tf_op jit(solution)/shard_map/pallas_call | solution.py:51
  376.2 23.0 %shard_map.229 = (f32[128,960]{1,0:T(8,128)S(1)}, bf16[128,960]{1,0:T(8,128)(2,1)S(1)}, f32[1,960]{1,0:T(1,128)S(1)}, bf16[128,960]{1,0:T(8,128)(2,1)S(1)}, bf16...) custom-call(s32[84]{0:T(128)S(1)} %concatenate.75.refs_0_, ...), custom_call_target="tpu_custom_call" | custom-call | flops 26400000000 | bytes 86400000 | tf_op jit(solution)/shard_map/pallas_call | solution.py:51
  402.2 6.1 %collective-permute-start.63 = (bf16[512,640]{1,0:T(8,128)(2,1)}, bf16[512,640]{1,0:T(8,128)(2,1)}, u32[]{:S(2)}, u32[]{:S(2)}) collective-permute-start(bf16[512,640]{1,0:T(8,128)(2,1)} %get-tuple-element.189), channel_id=1, source_target_pairs={{0,32},{4,36},{8,40},{12,44},{16,48},{20,52},{24,56},{28,60},{32,0... | collective-permute-start | bytes 1966088 | tf_op jit(solution)/shard_map/ppermute | solution.py:570
  417.3 6.9 %collective-permute-done.62 = bf16[512,640]{1,0:T(8,128)(2,1)} collective-permute-done((bf16[512,640]{1,0:T(8,128)(2,1)}, bf16[512,640]{1,0:T(8,128)(2,1)}, u32[]{:S(2)}, u32[]{:S(2)}) %collective-permute-start.62) | collective-permute-done | bytes 655392 | tf_op jit(solution)/shard_map/ppermute | solution.py:570
  451.1 5.2 collective-permute-start.72
  473.7 5.2 collective-permute-done.71
  495.2 5.8 %collective-permute-start.83 = (bf16[4,64,768]{2,1,0:T(8,128)(2,1)}, bf16[4,64,768]{2,1,0:T(8,128)(2,1)}, u32[]{:S(2)}, u32[]{:S(2)}) collective-permute-start(bf16[4,64,768]{2,1,0:T(8,128)(2,1)} %get-tuple-element.283), channel_id=1, source_target_pairs={{0,32},{4,36},{8,40},{12,44},{16,48},{20,52},{24,56},{28,60},{32,0... | collective-permute-start | bytes 1179656 | tf_op jit(solution)/shard_map/ppermute | solution.py:570
  516.5 4.5 collective-permute-done.87
  535.6 6.1 %collective-permute-start.92 = (f32[40,960]{1,0:T(8,128)S(1)}, f32[40,960]{1,0:T(8,128)S(1)}, u32[]{:S(2)}, u32[]{:S(2)}) collective-permute-start(f32[40,960]{1,0:T(8,128)S(1)} %maximum_maximum_fusion), channel_id=1, source_target_pairs={{0,0},{1,16},{2,32},{3,48},{4,1},{5,17},{6,33},{7,49},{8,2},{9,18}... | collective-permute-start | bytes 460808 | tf_op jit(solution)/shard_map/ppermute | solution.py:818
  544.5 13.1 %collective-permute-done.92 = f32[40,960]{1,0:T(8,128)S(1)} collective-permute-done((f32[40,960]{1,0:T(8,128)S(1)}, f32[40,960]{1,0:T(8,128)S(1)}, u32[]{:S(2)}, u32[]{:S(2)}) %collective-permute-start.92) | collective-permute-done | bytes 153632 | tf_op jit(solution)/shard_map/ppermute | solution.py:818
  (593 shorter events, 327.1 us)
Async XLA Ops:
  7.2 66.5 %all-gather.3.cloned.1.call-start = ((), (), s32[]{:S(2)}) async-start(), calls=%async_computation | async-start | bytes 3379200 | tf_op jit(solution)/shard_map/all_gather | solution.py:692
  14.7 147.1 %all-gather.5.cloned.1.call-start = ((), (), s32[]{:S(2)}) async-start(), calls=%async_computation.1 | async-start | bytes 3379200 | tf_op jit(solution)/shard_map/all_gather | solution.py:692
  20.2 33.5 %collective-permute-start.5 = (bf16[640,960]{0,1:T(8,128)(2,1)}, bf16[640,960]{0,1:T(8,128)(2,1)}, u32[]{:S(2)}, u32[]{:S(2)}) collective-permute-start(bf16[640,960]{0,1:T(8,128)(2,1)} %bitcast.163), channel_id=1, source_target_pairs={{0,64},{64,0},{1,65},{65,1},{2,66},{66,2},{3,67},{67,3},{4,68},{68... | collective-permute-start | bytes 3686408 | tf_op jit(solution)/shard_map/ppermute | solution.py:582
  29.1 31.9 %collective-permute-start.9 = (bf16[240,2560]{1,0:T(8,128)(2,1)}, bf16[240,2560]{1,0:T(8,128)(2,1)}, u32[]{:S(2)}, u32[]{:S(2)}) collective-permute-start(bf16[240,2560]{1,0:T(8,128)(2,1)} %bitcast_select_fusion.3), channel_id=1, source_target_pairs={{0,64},{64,0},{1,65},{65,1},{2,66},{66,2},{3,67},{67,3},{4,68},{68... | collective-permute-start | bytes 3686408 | tf_op jit(solution)/shard_map/ppermute | solution.py:582
  32.0 21.1 %collective-permute-start.8 = (bf16[128,960]{1,0:T(8,128)(2,1)S(1)}, bf16[128,960]{1,0:T(8,128)(2,1)S(1)}, u32[]{:S(2)}, u32[]{:S(2)}) collective-permute-start(bf16[128,960]{1,0:T(8,128)(2,1)S(1)} %bitcast_convert_fusion.refs_1_.refs_13_), channel_id=1, source_target_pairs={{0,3},{1,0},{2,1},{3,2},{4,7},{5,4},{6,5},{7,6},{8,11},{9,8},{10,9... | collective-permute-start | bytes 737288 | tf_op jit(solution)/shard_map/ppermute | solution.py:560
  95.0 22.5 %collective-permute-start.14 = (bf16[512,640]{1,0:T(8,128)(2,1)S(1)}, bf16[512,640]{1,0:T(8,128)(2,1)S(1)}, u32[]{:S(2)}, u32[]{:S(2)}) collective-permute-start(bf16[512,640]{1,0:T(8,128)(2,1)S(1)} %constant_dynamic-update-slice_fusion.refs_2_), channel_id=1, source_target_pairs={{0,16},{4,20},{8,24},{12,28},{16,32},{20,36},{24,40},{28,44},{32,4... | collective-permute-start | bytes 1966088 | tf_op jit(solution)/shard_map/ppermute | solution.py:570
  121.4 36.8 %collective-permute-start.19 = (bf16[240,1280]{1,0:T(8,128)(2,1)}, bf16[240,1280]{1,0:T(8,128)(2,1)}, u32[]{:S(2)}, u32[]{:S(2)}) collective-permute-start(bf16[240,1280]{1,0:T(8,128)(2,1)} %get-tuple-element.121), channel_id=1, source_target_pairs={{0,3},{1,0},{2,1},{3,2},{4,7},{5,4},{6,5},{7,6},{8,11},{9,8},{10,9... | collective-permute-start | bytes 1843208 | tf_op jit(solution)/shard_map/ppermute | solution.py:560
  122.2 36.1 %collective-permute-start.18 = (bf16[240,1280]{1,0:T(8,128)(2,1)}, bf16[240,1280]{1,0:T(8,128)(2,1)}, u32[]{:S(2)}, u32[]{:S(2)}) collective-permute-start(bf16[240,1280]{1,0:T(8,128)(2,1)} %get-tuple-element.120), channel_id=1, source_target_pairs={{0,2},{1,3},{2,0},{3,1},{4,6},{5,7},{6,4},{7,5},{8,10},{9,11},{10,... | collective-permute-start | bytes 1843208 | tf_op jit(solution)/shard_map/ppermute | solution.py:560
  124.1 34.1 %collective-permute-start.17 = (bf16[240,1280]{1,0:T(8,128)(2,1)}, bf16[240,1280]{1,0:T(8,128)(2,1)}, u32[]{:S(2)}, u32[]{:S(2)}) collective-permute-start(bf16[240,1280]{1,0:T(8,128)(2,1)} %get-tuple-element.119), channel_id=1, source_target_pairs={{0,1},{1,2},{2,3},{3,0},{4,5},{5,6},{6,7},{7,4},{8,9},{9,10},{10,1... | collective-permute-start | bytes 1843208 | tf_op jit(solution)/shard_map/ppermute | solution.py:560
  194.6 21.3 %collective-permute-start.36 = (bf16[128,1984]{1,0:T(8,128)(2,1)S(1)}, bf16[128,1984]{1,0:T(8,128)(2,1)S(1)}, u32[]{:S(2)}, u32[]{:S(2)}) collective-permute-start(bf16[128,1984]{1,0:T(8,128)(2,1)S(1)} %get-tuple-element.133.refs_5_), channel_id=1, source_target_pairs={{0,3},{1,0},{2,1},{3,2},{4,7},{5,4},{6,5},{7,6},{8,11},{9,8},{10,9... | collective-permute-start | bytes 1523720 | tf_op jit(solution)/shard_map/ppermute | solution.py:560
  210.1 28.4 %collective-permute-start.31 = (bf16[512,640]{1,0:T(8,128)(2,1)S(1)}, bf16[512,640]{1,0:T(8,128)(2,1)S(1)}, u32[]{:S(2)}, u32[]{:S(2)}) collective-permute-start(bf16[512,640]{1,0:T(8,128)(2,1)S(1)} %constant_dynamic-update-slice_fusion.4.refs_2_), channel_id=1, source_target_pairs={{0,16},{4,20},{8,24},{12,28},{16,32},{20,36},{24,40},{28,44},{32,4... | collective-permute-start | bytes 1966088 | tf_op jit(solution)/shard_map/ppermute | solution.py:570
  211.5 27.1 %collective-permute-start.32 = (bf16[512,640]{1,0:T(8,128)(2,1)S(1)}, bf16[512,640]{1,0:T(8,128)(2,1)S(1)}, u32[]{:S(2)}, u32[]{:S(2)}) collective-permute-start(bf16[512,640]{1,0:T(8,128)(2,1)S(1)} %constant_dynamic-update-slice_fusion.4.refs_2_), channel_id=1, source_target_pairs={{0,32},{4,36},{8,40},{12,44},{16,48},{20,52},{24,56},{28,60},{32,0... | collective-permute-start | bytes 1966088 | tf_op jit(solution)/shard_map/ppermute | solution.py:570
  212.6 26.0 %collective-permute-start.33 = (bf16[512,640]{1,0:T(8,128)(2,1)S(1)}, bf16[512,640]{1,0:T(8,128)(2,1)S(1)}, u32[]{:S(2)}, u32[]{:S(2)}) collective-permute-start(bf16[512,640]{1,0:T(8,128)(2,1)S(1)} %constant_dynamic-update-slice_fusion.4.refs_2_), channel_id=1, source_target_pairs={{0,48},{4,52},{8,56},{12,60},{16,0},{20,4},{24,8},{28,12},{32,16},... | collective-permute-start | bytes 1966088 | tf_op jit(solution)/shard_map/ppermute | solution.py:570
  215.9 21.4 %collective-permute-start.34 = (bf16[128,1984]{1,0:T(8,128)(2,1)S(1)}, bf16[128,1984]{1,0:T(8,128)(2,1)S(1)}, u32[]{:S(2)}, u32[]{:S(2)}) collective-permute-start(bf16[128,1984]{1,0:T(8,128)(2,1)S(1)} %get-tuple-element.133.refs_5_), channel_id=1, source_target_pairs={{0,1},{1,2},{2,3},{3,0},{4,5},{5,6},{6,7},{7,4},{8,9},{9,10},{10,1... | collective-permute-start | bytes 1523720 | tf_op jit(solution)/shard_map/ppermute | solution.py:560
  344.9 83.1 %collective-permute-start.70 = (bf16[16,96,640]{2,1,0:T(8,128)(2,1)}, bf16[16,96,640]{2,1,0:T(8,128)(2,1)}, u32[]{:S(2)}, u32[]{:S(2)}) collective-permute-start(bf16[16,96,640]{2,1,0:T(8,128)(2,1)} %get-tuple-element.196), channel_id=1, source_target_pairs={{0,64},{64,0},{1,65},{65,1},{2,66},{66,2},{3,67},{67,3},{4,68},{68... | collective-permute-start | bytes 5898248 | tf_op jit(solution)/shard_map/ppermute | solution.py:582
  354.0 22.1 %collective-permute-start.57 = (bf16[128,960]{1,0:T(8,128)(2,1)S(1)}, bf16[128,960]{1,0:T(8,128)(2,1)S(1)}, u32[]{:S(2)}, u32[]{:S(2)}) collective-permute-start(bf16[128,960]{1,0:T(8,128)(2,1)S(1)} %get-tuple-element.171), channel_id=1, source_target_pairs={{0,3},{1,0},{2,1},{3,2},{4,7},{5,4},{6,5},{7,6},{8,11},{9,8},{10,9... | collective-permute-start | bytes 737288 | tf_op jit(solution)/shard_map/ppermute | solution.py:560
  376.0 68.1 %collective-permute-start.69 = (bf16[16,96,640]{2,1,0:T(8,128)(2,1)}, bf16[16,96,640]{2,1,0:T(8,128)(2,1)}, u32[]{:S(2)}, u32[]{:S(2)}) collective-permute-start(bf16[16,96,640]{2,1,0:T(8,128)(2,1)} %get-tuple-element.195), channel_id=1, source_target_pairs={{0,64},{64,0},{1,65},{65,1},{2,66},{66,2},{3,67},{67,3},{4,68},{68... | collective-permute-start | bytes 5898248 | tf_op jit(solution)/shard_map/ppermute | solution.py:582
  415.1 36.1 %collective-permute-start.42 = (bf16[128,960]{1,0:T(8,128)(2,1)}, bf16[128,960]{1,0:T(8,128)(2,1)}, u32[]{:S(2)}, u32[]{:S(2)}) collective-permute-start(bf16[128,960]{1,0:T(8,128)(2,1)} %copy-done.66), channel_id=1, source_target_pairs={{0,1},{1,2},{2,3},{3,0},{4,5},{5,6},{6,7},{7,4},{8,9},{9,10},{10,1... | collective-permute-start | bytes 737288 | tf_op jit(solution)/shard_map/ppermute | solution.py:560
  434.7 21.6 %collective-permute-start.40 = (bf16[128,960]{1,0:T(8,128)(2,1)}, bf16[128,960]{1,0:T(8,128)(2,1)}, u32[]{:S(2)}, u32[]{:S(2)}) collective-permute-start(bf16[128,960]{1,0:T(8,128)(2,1)} %get-tuple-element.136), channel_id=1, source_target_pairs={{0,2},{1,3},{2,0},{3,1},{4,6},{5,7},{6,4},{7,5},{8,10},{9,11},{10,... | collective-permute-start | bytes 737288 | tf_op jit(solution)/shard_map/ppermute | solution.py:560
  435.4 21.0 %collective-permute-start.38 = (bf16[128,960]{1,0:T(8,128)(2,1)}, bf16[128,960]{1,0:T(8,128)(2,1)}, u32[]{:S(2)}, u32[]{:S(2)}) collective-permute-start(bf16[128,960]{1,0:T(8,128)(2,1)} %get-tuple-element.135), channel_id=1, source_target_pairs={{0,3},{1,0},{2,1},{3,2},{4,7},{5,4},{6,5},{7,6},{8,11},{9,8},{10,9... | collective-permute-start | bytes 737288 | tf_op jit(solution)/shard_map/ppermute | solution.py:560
  437.5 21.7 %collective-permute-start.78 = (bf16[128,640]{1,0:T(8,128)(2,1)}, bf16[128,640]{1,0:T(8,128)(2,1)}, u32[]{:S(2)}, u32[]{:S(2)}) collective-permute-start(bf16[128,640]{1,0:T(8,128)(2,1)} %get-tuple-element.316), channel_id=1, source_target_pairs={{0,1},{1,2},{2,3},{3,0},{4,5},{5,6},{6,7},{7,4},{8,9},{9,10},{10,1... | collective-permute-start | bytes 491528 | tf_op jit(solution)/shard_map/ppermute | solution.py:560
  456.3 22.6 %collective-permute-start.71 = (bf16[4,192,640]{2,1,0:T(8,128)(2,1)S(1)}, bf16[4,192,640]{2,1,0:T(8,128)(2,1)S(1)}, u32[]{:S(2)}, u32[]{:S(2)}) collective-permute-start(bf16[4,192,640]{2,1,0:T(8,128)(2,1)S(1)} %get-tuple-element.265), channel_id=1, source_target_pairs={{0,16},{4,20},{8,24},{12,28},{16,32},{20,36},{24,40},{28,44},{32,4... | collective-permute-start | bytes 2949128 | tf_op jit(solution)/shard_map/ppermute | solution.py:570
  463.4 25.1 %collective-permute-start.43 = (f32[128,960]{1,0:T(8,128)}, f32[128,960]{1,0:T(8,128)}, u32[]{:S(2)}, u32[]{:S(2)}) collective-permute-start(f32[128,960]{1,0:T(8,128)} %get-tuple-element.261), channel_id=1, source_target_pairs={{0,64},{64,0},{1,65},{65,1},{2,66},{66,2},{3,67},{67,3},{4,68},{68... | collective-permute-start | bytes 1474568 | tf_op jit(solution)/shard_map/ppermute | solution.py:582
  535.6 22.0 %collective-permute-start.92 = (f32[40,960]{1,0:T(8,128)S(1)}, f32[40,960]{1,0:T(8,128)S(1)}, u32[]{:S(2)}, u32[]{:S(2)}) collective-permute-start(f32[40,960]{1,0:T(8,128)S(1)} %maximum_maximum_fusion), channel_id=1, source_target_pairs={{0,0},{1,16},{2,32},{3,48},{4,1},{5,17},{6,33},{7,49},{8,2},{9,18}... | collective-permute-start | bytes 460808 | tf_op jit(solution)/shard_map/ppermute | solution.py:818
  (190 other events, 1826.3 us)
Sparse Core Ops, SparseCore 0:
  14.8 48.5 all-gather.2
  78.3 36.5 all-gather.4

commit v5 on v4

--- a/solution.py
+++ b/solution.py
@@ -111,11 +111,11 @@
         parts = refs[2 : 2 + count]
         gain, own, other, cosine, sine = refs[2 + count : 7 + count]
         if count:
-            normed_in, mixed_in = refs[7 + count : 9 + count]
-            x_out, normed_out, q_out, kv_out, ahead_out, halves = refs[9 + count :]
-            ahead_out[:, :D] = normed_in[...]
-            ahead_out[:, D:QP] = jnp.zeros((ROWS, QP - D), BF)
-            ahead_out[:, QP:] = mixed_in[...]
+            ahead_in = refs[7 + count : 10 + count]
+            x_out, normed_out, q_out, kv_out, ahead_out, halves = refs[10 + count :]
+            ahead_out[...] = jnp.zeros((ROWS, 2 * QP + D), BF)
+            for i in range(3):
+                ahead_out[:, i * QP : i * QP + D] = ahead_in[i][...]
         else:
             x_out, normed_out, q_out, kv_out, halves = refs[7:]
         side = info[0]
@@ -142,7 +142,7 @@
 def project(info, base, parts, gain, weight, cosine, sine, ahead=()):
     outs = [((ROWS, D), F32), ((ROWS, D), BF), ((ROWS, QP), BF), ((ROWS, 2 * KW), BF)]
     if ahead:
-        outs.append(((ROWS, QP + D), BF))
+        outs.append(((ROWS, 2 * QP + D), BF))
     scratch = [pltpu.VMEM((2, ROWS, HALF), F32)]
     return call(project_body(len(parts)), outs, 2.5, 16, scratch, smem=1)(
         info, base, *parts, gain, *weight, cosine, sine, *ahead
@@ -270,10 +270,10 @@
     part_out[...] = dot(hidden, wd[...]).astype(BF)
 
 
-def feed(layer, info, second, wgu, wd, after=()):
+def feed(layer, info, second, wgu, wd):
     outs = [((2, ROWS, FF // 4), F32), ((ROWS, FF // 4), BF), ((ROWS, D), BF)]
     body = partial(feed_body, layer)
-    return call(body, outs, 1.0, 12, smem=1)(info, second, *wgu, wd, after=after)
+    return call(body, outs, 1.0, 12, smem=1)(info, second, *wgu, wd)
 
 
 def feed_back_body(layer, info, grad_low, gu, own, other, wd, dgu_out, part_out):
@@ -490,15 +490,15 @@
 
 def attend_grads_body(*refs):
     info = refs[0]
-    mines, aheads = refs[1:5], refs[5:9]
-    dc_one, dc_two, keep_out, give_out, lhs, mine, acc, group = refs[9:]
+    mines, ahead = refs[1:5], refs[5]
+    dc_one, dc_two, keep_out, give_out, lhs, mine, acc, group = refs[6:]
     side, z = info[0], info[1]
     for k in range(4):
         rows = slice(k * ROWS, (k + 1) * ROWS)
         for h in range(2):
             mine[h, rows, :] = mines[k][:, h * 320 : (h + 1) * 320].astype(F32).astype(BF)
-        lhs[0, rows, :] = aheads[k][:, :D]
-        lhs[1, rows, :] = aheads[k][:, QP:]
+        lhs[0, rows, :] = ahead[(z + 4 - k) % 4, :, :D]
+        lhs[1, rows, :] = ahead[(z + 4 - k) % 4, :, QP : QP + D]
     group[60:, :] = jnp.zeros((4, 384), F32)
     for turn, out in ((0, keep_out), (1, give_out)):
         h = side if turn == 0 else 1 - side
@@ -513,7 +513,7 @@
             out[slot_of(info, c, turn)] = group[...].astype(BF)
 
 
-def attend_grads(info, mines, aheads, dc_one, dc_two, after=()):
+def attend_grads(info, mines, ahead, dc_one, dc_two, after=()):
     rows = 4 * ROWS
     scratch = [
         pltpu.VMEM((2, rows, D), BF),
@@ -522,7 +522,7 @@
         pltpu.VMEM((64, 384), F32),
     ]
     return call(attend_grads_body, [((16, 64, 384), BF)] * 2, 3.0, 16, scratch, smem=1)(
-        info, *mines, *aheads, dc_one, dc_two, after=after
+        info, *mines, ahead, dc_one, dc_two, after=after
     )
 
 
@@ -633,8 +633,6 @@
     given = swap(jnp.where(first_core, w_up[0], w_gate[0]))
     kind = (jnp.where(first_core, w_gate[0], given), jnp.where(first_core, given, w_up[0]))
 
-    wd = both(w_down[0])
-
     def none_of(mark):
         return (mark != mark).astype(jnp.int32)
 
@@ -646,9 +644,10 @@
 
     feed_columns = [columns((z_rank + k) % 4) for k in range(4)]
 
-    def send_feed_weights(mark):
-        sent = hold(feed_columns[1:], mark)
-        return feed_columns[:1] + [z_shift(sent[k - 1], k) for k in (1, 2, 3)]
+    def send_feed_weights(early, late):
+        after, before = hold([feed_columns[1], feed_columns[3]], early)
+        (across,) = hold([feed_columns[2]], late)
+        return [feed_columns[0], z_shift(after, 1), z_shift(across, 2), z_shift(before, 3)]
 
     def join_feed_weights(parts, mark):
         later = none_of(mark)
@@ -669,7 +668,8 @@
     ahead_y = ((step - y) % 4)[:, None]
     ahead_x = ((step - x) % 4)[None, :]
     slot = jnp.where(first_core, ahead_y * 4 + ahead_x, ahead_x * 4 + ahead_y).reshape(16)
-    info = jnp.concatenate([jnp.stack([section, z_rank]), own, came, goes, slot]).astype(jnp.int32)
+    place = jnp.stack([section, z_rank]).astype(jnp.int32)
+    info = jnp.concatenate([place, own, came, goes, slot]).astype(jnp.int32)
     offsets = jnp.arange(BLK, dtype=jnp.int32)
     local_pos = (own[:, None] * BLK + offsets[None, :]).reshape(ROWS)
     frequency = jnp.exp(
@@ -686,41 +686,36 @@
     def z_gather(value):
         return [value] + [z_shift(value, k) for k in (1, 2, 3)]
 
-    last_lows = z_gather(own_cotangent.astype(BF))
-
-    def whole(part, *before):
+    last_low = own_cotangent.astype(BF)
+
+    def whole(part):
         full = lax.all_gather(part, "wsh", axis=0, tiled=True)
-        if before:
-            (full,) = hold([full], token(*before))
         return full, swap(full)
 
-    gathered = (
-        whole(layer_half[0], info, cosine, sine, own_tokens, *wd, *last_lows[1:], *feed_columns, *gain_pair),
-        whole(layer_half[1]),
-    )
+    gathered = tuple(whole(part) for part in layer_half)
     saved = []
     base, parts = own_tokens, []
     for layer in range(2):
         gain_one = gain_pair[layer][0:1]
         gain_two = gain_pair[layer][1:2]
-        ahead = (saved[0]["normed"], saved[0]["mixed"]) if layer else ()
+        ahead = (saved[0]["normed"], saved[0]["mixed"], last_low) if layer else ()
         x_in, normed, q, kv, *ahead = project(
-            info, base, parts, gain_one, gathered[layer], cosine, sine, ahead
+            place, base, parts, gain_one, gathered[layer], cosine, sine, ahead
         )
         if layer:
-            first_aheads = z_gather(ahead[0])
+            first_ahead = lax.all_gather(ahead[0], "wsh")
         row = jnp.concatenate([kv] + [gather_shift(kv, k) for k in (1, 2, 3)], axis=0)
         pieces = [row] + [reduce_shift(row, k) for k in (1, 2, 3)]
         if layer == 0:
-            sent = send_feed_weights(token(*pieces[1:]))
+            sent = send_feed_weights(token(row), token(pieces[1]))
+            wd = both(hold([w_down[0]], token(kv))[0])
         mixed, lse, kvs, resid, second = attend(
-            info, q, pieces, gathered[layer], x_in, gain_two, after=() if layer else (token(*wd),)
+            info, q, pieces, gathered[layer], x_in, gain_two, after=() if layer else (token(wd[0]),)
         )
         seconds = z_gather(second)
         if layer == 0:
-            wgu = join_feed_weights(sent, seconds[1][0, 0])
-        after = (token(*first_aheads[1:]),) if layer else ()
-        fed = [feed(layer, info, s, wgu[layer], wd[layer], after) for s in seconds]
+            wgu = join_feed_weights(sent, second[0, 0])
+        fed = [feed(layer, place, s, wgu[layer], wd[layer]) for s in seconds]
         parts = [fed[0][2]] + [z_shift(fed[k][2], -k) for k in (1, 2, 3)]
         base = resid
         saved.append(
@@ -733,7 +728,9 @@
     outputs = [saved[1]["x"], add(base, *parts)]
 
     grad = own_cotangent
-    lows = last_lows
+    lows = [last_low] + [
+        lax.dynamic_index_in_dim(first_ahead, (z_rank - k) % 4, 0, False)[:, 2 * QP :] for k in (1, 2, 3)
+    ]
     input_grads = [None, None]
     feed_halves = [None, None]
     kept = [None, None]
@@ -750,7 +747,7 @@
         s = saved[layer]
         gain_one = gain_pair[layer][0:1]
         gain_two = gain_pair[layer][1:2]
-        back = [feed_back(layer, info, lows[k], s["gu"][k], wgu[layer], wd[layer]) for k in range(4)]
+        back = [feed_back(layer, place, lows[k], s["gu"][k], wgu[layer], wd[layer]) for k in range(4)]
         parts = [back[0][1]] + [z_shift(back[k][1], -k) for k in (1, 2, 3)]
         keep, give = feed_grads(info, s["seconds"], [b[0] for b in back], s["hidden"], lows)
         d_resid, d_low, dc_two, dq, ahead, *goes_out = attend_back(
@@ -761,25 +758,25 @@
         row = add(goes_out[0], *[reduce_shift(goes_out[k], k) for k in (1, 2, 3)])
         row = row.astype(BF).reshape(4, ROWS, 2 * KW)
         own_pieces = [row[0]] + [gather_shift(row[k], k) for k in (1, 2, 3)]
-        aheads = z_gather(ahead) if layer else first_aheads
+        ahead = lax.all_gather(ahead, "wsh") if layer else first_ahead
         if layer == 0:
             kept[1] = attention_grads(none_of(d_low[0, 0]))
         cut, grad, dc_one = project_back(
             info, own_pieces, dq, d_resid, d_low, s["x"], gain_one, gathered[layer], cosine, sine,
-            after=(token(*aheads[1:]),) if layer else (),
+            after=(token(ahead),) if layer else (),
         )
         input_grads[layer] = grad
         if layer:
             lows = z_gather(grad.astype(BF))
 
-        def attention_grads(later, after=(), cut=cut, aheads=aheads, dc_one=dc_one, dc_two=dc_two):
+        def attention_grads(later, after=(), cut=cut, ahead=ahead, dc_one=dc_one, dc_two=dc_two):
             mines = [lax.dynamic_index_in_dim(cut, k + later, 0, False) for k in range(4)]
             mines = [mines[0]] + [z_shift(mines[k], k) for k in (1, 2, 3)]
-            keep, give = attend_grads(info, mines, aheads, dc_one, dc_two, after)
+            keep, give = attend_grads(info, mines, ahead, dc_one, dc_two, after)
             return add(keep, swap(give)).astype(BF)
 
         if layer == 0:
-            feed_stage = stage_one(jnp.concatenate(hold(feed_halves, token(cut)), axis=1))
+            feed_stage = stage_one(jnp.concatenate(hold(feed_halves, token(row)), axis=1))
             kept[0] = attention_grads(0, (token(feed_stage),))
     attend_stage = stage_one(jnp.concatenate(kept, axis=2))
     both_sums = stage_two(

time: 576 us -> 558 us (0.969)
  starting transfers between devices: 142 us -> 116 us
  local copies, waits for them, and re-layouts: 81.7 us -> 96.6 us
  other arithmetic: 46.2 us -> 37.7 us
    ppermute x45 -> x36, waiting for transfers between devices: 60.4 us -> 23.5 us  [z_shift(): return lax.ppermute(value, 'wsh', [(i, (i + steps) % 4) for i in range(4)])]
    all_gather x2, waiting for transfers between devices: 0.02 us -> 29.7 us  [whole(): full = lax.all_gather(part, 'wsh', axis=0, tiled=True)]
    unnamed x249 -> x365, local copies, waits for them, and re-layouts: 36.9 us -> 59.8 us
    ppermute x45 -> x36, starting transfers between devices: 71.7 us -> 56.4 us  [z_shift(): return lax.ppermute(value, 'wsh', [(i, (i + steps) % 4) for i in range(4)])]
    ppermute x33, starting transfers between devices: 62.3 us -> 51 us  [ctx_shift(): return lax.ppermute(value, ('section', 'ctx'), pairs)]
    another operation x1 -> x0, local copies, waits for them, and re-layouts: 9.37 us -> none  [token(): return jnp.stack([a[(0,) * a.ndim].astype(F32) for a in arrays])]
    slice x24 -> x8, local copies, waits for them, and re-layouts: 13.4 us -> 4.8 us  [token(): return jnp.stack([a[(0,) * a.ndim].astype(F32) for a in arrays])]
    another operation x4 -> x1, other arithmetic: 6.63 us -> 0.07 us  [shards(): place = jnp.stack([section, z_rank]).astype(jnp.int32)]
  transfers between devices with their start and end apart: 95 -> 88, of which waited for: 42 -> 39; matrix products, arithmetic and copies ran while one was open for 15% -> 12% of each run, Pallas kernels for 16% -> 18%
where the time goes in v5:
time: 558 us; the launch traced here: 548 us
  waiting for transfers between devices  145 us (26%)
  Pallas kernels  130 us (23%)
  starting transfers between devices  116 us (21%)
  local copies, waits for them, and re-layouts  96.6 us (17%)
  other arithmetic  37.7 us (7%)
  between operations  23.9 us (4%)
    pallas_call x29, Pallas kernels, run(): pl.pallas_call(inner, in_specs=in_specs, out_specs=[pl.BlockSpec(memory_s...  129 us
    ppermute x33, waiting for transfers between devices, ctx_shift(): return lax.ppermute(value, ('section', 'ctx'), pairs)  70.3 us
    unnamed x365, local copies, waits for them, and re-layouts  59.8 us
    ppermute x36, starting transfers between devices, z_shift(): return lax.ppermute(value, 'wsh', [(i, (i + steps) % 4) for i in range(4)])  56.4 us
    ppermute x33, starting transfers between devices, ctx_shift(): return lax.ppermute(value, ('section', 'ctx'), pairs)  51 us
    all_gather x2, waiting for transfers between devices, whole(): full = lax.all_gather(part, 'wsh', axis=0, tiled=True)  29.7 us
    ppermute x36, waiting for transfers between devices, z_shift(): return lax.ppermute(value, 'wsh', [(i, (i + steps) % 4) for i in range(4)])  23.5 us
    ppermute x1, waiting for transfers between devices, shards(): grad_down = lax.ppermute(down, ('ctx', 'wsh'), moves)[None]  13.8 us
  transfers between devices with their start and end apart: 88, of which 39 were waited for; matrix products, arithmetic and copies ran while one was open for 12% of the time, Pallas kernels for 18%

profile of v5, /device:TPU:16, one launch (start us, length us, event | category | flops | bytes accessed | tf_op | source)
XLA Modules:
  0.0 548.2 jit_solution(7842681121354259211)
XLA Ops:
  24.9 29.7 %all-gather.7.cloned.1.call-done.refs_3_.refs_6_.refs_8_.refs_10_ = bf16[960,1376]{1,0:T(8,128)(2,1)} async-done(((bf16[240,1376]{1,0:T(8,128)(2,1)}), bf16[960,1376]{1,0:T(8,128)(2,1)}) %all-gather.7.cloned.1.call-update) | async-done | bytes 2641936 | tf_op jit(solution)/shard_map/all_gather | solution.py:692
  111.2 10.6 %shard_map.205 = (bf16[128,960]{1,0:T(8,128)(2,1)S(1)}, f32[2,5,192,128]{3,2,1,0:T(8,128)S(1)}, bf16[2048,640]{1,0:T(8,128)(2,1)S(1)}, f32[128,960]{1,0:T(8,128)S(1)}, bf16[128,960]{1,0:T(8,128)(2,1)S(1)}) custom-call(s32[84]{0:T(128)S(1)} %concatenate.76.refs_0_, bf16[128,1024]{1,0:T(8,128)(2,1)S(1)} %copy-done.135, ...), custom_call_target="tpu_custom_call" | custom-call | flops 13200000000 | bytes 43200000 | tf_op jit(solution)/shard_map/pallas_call | solution.py:51
  139.9 7.5 %collective-permute-done.22.refs_1_.refs_4_ = bf16[128,960]{1,0:T(8,128)(2,1)S(1)} collective-permute-done((bf16[128,960]{1,0:T(8,128)(2,1)S(1)}, bf16[128,960]{1,0:T(8,128)(2,1)S(1)}, u32[]{:S(2)}, u32[]{:S(2)}) %collective-permute-start.22) | collective-permute-done | bytes 245792 | tf_op jit(solution)/shard_map/ppermute | solution.py:560
  152.2 5.2 collective-permute-start.21
  178.5 4.2 collective-permute-done.25
  188.0 6.4 %collective-permute-done.28.refs_3_ = bf16[512,640]{1,0:T(8,128)(2,1)S(1)} collective-permute-done((bf16[512,640]{1,0:T(8,128)(2,1)S(1)}, bf16[512,640]{1,0:T(8,128)(2,1)S(1)}, u32[]{:S(2)}, u32[]{:S(2)}) %collective-permute-start.28) | collective-permute-done | bytes 655392 | tf_op jit(solution)/shard_map/ppermute | solution.py:570
  194.4 7.9 %collective-permute-done.29.refs_4_ = bf16[512,640]{1,0:T(8,128)(2,1)S(1)} collective-permute-done((bf16[512,640]{1,0:T(8,128)(2,1)S(1)}, bf16[512,640]{1,0:T(8,128)(2,1)S(1)}, u32[]{:S(2)}, u32[]{:S(2)}) %collective-permute-start.29) | collective-permute-done | bytes 655392 | tf_op jit(solution)/shard_map/ppermute | solution.py:570
  206.3 10.7 %shard_map.213 = (bf16[128,960]{1,0:T(8,128)(2,1)S(1)}, f32[2,5,192,128]{3,2,1,0:T(8,128)S(1)}, bf16[2048,640]{1,0:T(8,128)(2,1)S(1)}, f32[128,960]{1,0:T(8,128)S(1)}, bf16[128,960]{1,0:T(8,128)(2,1)S(1)}) custom-call(s32[84]{0:T(128)S(1)} %concatenate.76.refs_0_, bf16[128,1024]{1,0:T(8,128)(2,1)S(1)} %copy-done.125, ...), custom_call_target="tpu_custom_call" | custom-call | flops 13200000000 | bytes 43200000 | tf_op jit(solution)/shard_map/pallas_call | solution.py:51
  249.1 4.1 collective-permute-start.39
  255.8 4.9 shard_map.222
  264.7 21.7 %shard_map.223 = (f32[128,960]{1,0:T(8,128)S(1)}, bf16[128,960]{1,0:T(8,128)(2,1)S(1)}, f32[1,960]{1,0:T(1,128)S(1)}, bf16[128,960]{1,0:T(8,128)(2,1)S(1)}, bf16...) custom-call(s32[84]{0:T(128)S(1)} %concatenate.76.refs_0_, ...), custom_call_target="tpu_custom_call" | custom-call | flops 26400000000 | bytes 86400000 | tf_op jit(solution)/shard_map/pallas_call | solution.py:51
  298.2 5.6 %collective-permute-done.41 = bf16[512,640]{1,0:T(8,128)(2,1)S(1)} collective-permute-done((bf16[512,640]{1,0:T(8,128)(2,1)}, bf16[512,640]{1,0:T(8,128)(2,1)S(1)}, u32[]{:S(2)}, u32[]{:S(2)}) %collective-permute-start.41) | collective-permute-done | bytes 655392 | tf_op jit(solution)/shard_map/ppermute | solution.py:570
  303.7 7.9 %collective-permute-done.42 = bf16[512,640]{1,0:T(8,128)(2,1)S(1)} collective-permute-done((bf16[512,640]{1,0:T(8,128)(2,1)}, bf16[512,640]{1,0:T(8,128)(2,1)S(1)}, u32[]{:S(2)}, u32[]{:S(2)}) %collective-permute-start.42) | collective-permute-done | bytes 655392 | tf_op jit(solution)/shard_map/ppermute | solution.py:570
  319.4 4.9 all-gather.13.cloned.1.call-done
  347.1 3.9 collective-permute-done.51.refs_1_.refs_16_
  363.8 6.3 %shard_map.229 = (bf16[16,96,640]{2,1,0:T(8,128)(2,1)S(1)}, bf16[16,96,640]{2,1,0:T(8,128)(2,1)}) custom-call(s32[84]{0:T(128)S(1)} %concatenate.76.refs_0_, bf16[128,960]{1,0:T(8,128)(2,1)S(1)} %copy-done.40, bf16[128,960]{1,0:T(8,128)(2,1)S(1)} %copy-done.46, bf16[128,960]{1,0:T(8,128)(2,1)S(1)} %copy-done.44, bf16[128,960]{1,0:T(8,128)(2,1)S(1)} %copy-done.42, ...), custom_call_target="tpu_custom_call" | custom-call | flops 7150000128 | bytes 23400000 | tf_op jit(solution)/shard_map/pallas_call | solution.py:51
  372.1 23.2 %shard_map.230 = (f32[128,960]{1,0:T(8,128)S(1)}, bf16[128,960]{1,0:T(8,128)(2,1)S(1)}, f32[1,960]{1,0:T(1,128)S(1)}, bf16[128,960]{1,0:T(8,128)(2,1)S(1)}, bf16...) custom-call(s32[84]{0:T(128)S(1)} %concatenate.76.refs_0_, ...), custom_call_target="tpu_custom_call" | custom-call | flops 26400000000 | bytes 86400000 | tf_op jit(solution)/shard_map/pallas_call | solution.py:51
  408.0 5.3 collective-permute-done.54
  444.2 4.1 shard_map.234
  469.1 4.1 shard_map.233
  487.2 5.4 collective-permute-done.74
  500.5 7.7 %collective-permute-done.76 = bf16[96,2048]{1,0:T(8,128)(2,1)S(1)} collective-permute-done((bf16[96,2048]{1,0:T(8,128)(2,1)S(1)}, bf16[96,2048]{1,0:T(8,128)(2,1)S(1)}, u32[]{:S(2)}, u32[]{:S(2)}) %collective-permute-start.76) | collective-permute-done | bytes 393248 | tf_op jit(solution)/shard_map/ppermute | solution.py:570
  518.9 5.2 collective-permute-start.83
  526.8 13.8 %collective-permute-done.83 = f32[40,960]{1,0:T(8,128)S(1)} collective-permute-done((f32[40,960]{1,0:T(8,128)S(1)}, f32[40,960]{1,0:T(8,128)S(1)}, u32[]{:S(2)}, u32[]{:S(2)}) %collective-permute-start.83) | collective-permute-done | bytes 153632 | tf_op jit(solution)/shard_map/ppermute | solution.py:815
  (683 shorter events, 313.9 us)
Async XLA Ops:
  7.2 47.3 %all-gather.7.cloned.1.call-start = ((), (), s32[]{:S(2)}) async-start(), calls=%async_computation | async-start | bytes 3379200 | tf_op jit(solution)/shard_map/all_gather | solution.py:692
  16.1 115.1 %all-gather.9.cloned.1.call-start = ((), (), s32[]{:S(2)}) async-start(), calls=%async_computation.1 | async-start | bytes 3379200 | tf_op jit(solution)/shard_map/all_gather | solution.py:692
  16.2 43.6 %collective-permute-start = (bf16[2,240]{1,0:T(2,128)(2,1)S(1)}, bf16[2,240]{1,0:T(2,128)(2,1)S(1)}, u32[]{:S(2)}, u32[]{:S(2)}) collective-permute-start(bf16[2,240]{1,0:T(2,128)(2,1)S(1)} %pad_maximum_fusion.13), channel_id=1, source_target_pairs={{0,1},{1,2},{2,3},{3,0},{4,5},{5,6},{6,7},{7,4},{8,9},{9,10},{10,1... | collective-permute-start | bytes 2888 | tf_op jit(solution)/shard_map/ppermute | solution.py:560
  18.2 41.6 %collective-permute-start.1 = (bf16[2,240]{1,0:T(2,128)(2,1)S(1)}, bf16[2,240]{1,0:T(2,128)(2,1)S(1)}, u32[]{:S(2)}, u32[]{:S(2)}) collective-permute-start(bf16[2,240]{1,0:T(2,128)(2,1)S(1)} %pad_maximum_fusion.13), channel_id=1, source_target_pairs={{0,2},{1,3},{2,0},{3,1},{4,6},{5,7},{6,4},{7,5},{8,10},{9,11},{10,... | collective-permute-start | bytes 2888 | tf_op jit(solution)/shard_map/ppermute | solution.py:560
  21.7 38.0 %collective-permute-start.2 = (bf16[2,240]{1,0:T(2,128)(2,1)S(1)}, bf16[2,240]{1,0:T(2,128)(2,1)S(1)}, u32[]{:S(2)}, u32[]{:S(2)}) collective-permute-start(bf16[2,240]{1,0:T(2,128)(2,1)S(1)} %pad_maximum_fusion.13), channel_id=1, source_target_pairs={{0,3},{1,0},{2,1},{3,2},{4,7},{5,4},{6,5},{7,6},{8,11},{9,8},{10,9... | collective-permute-start | bytes 2888 | tf_op jit(solution)/shard_map/ppermute | solution.py:560
  23.9 41.1 %collective-permute-start.13 = (bf16[240,2560]{1,0:T(8,128)(2,1)}, bf16[240,2560]{1,0:T(8,128)(2,1)}, u32[]{:S(2)}, u32[]{:S(2)}) collective-permute-start(bf16[240,2560]{1,0:T(8,128)(2,1)} %bitcast_select_fusion.1), channel_id=1, source_target_pairs={{0,64},{64,0},{1,65},{65,1},{2,66},{66,2},{3,67},{67,3},{4,68},{68... | collective-permute-start | bytes 3686408 | tf_op jit(solution)/shard_map/ppermute | solution.py:582
  65.0 175.5 %all-gather.11.cloned.1.call-start = ((), (), s32[]{:S(2)}) async-start(), calls=%async_computation.2 | async-start | bytes 3932160 | tf_op jit(solution)/shard_map/all_gather | solution.py:706
  79.1 21.7 %collective-permute-start.12 = (bf16[640,960]{0,1:T(8,128)(2,1)}, bf16[640,960]{0,1:T(8,128)(2,1)}, u32[]{:S(2)}, u32[]{:S(2)}) collective-permute-start(bf16[640,960]{0,1:T(8,128)(2,1)} %copy.93), channel_id=1, source_target_pairs={{0,64},{64,0},{1,65},{65,1},{2,66},{66,2},{3,67},{67,3},{4,68},{68... | collective-permute-start | bytes 3686408 | tf_op jit(solution)/shard_map/ppermute | solution.py:582
  94.4 32.7 %collective-permute-start.14 = (bf16[240,1280]{1,0:T(8,128)(2,1)}, bf16[240,1280]{1,0:T(8,128)(2,1)}, u32[]{:S(2)}, u32[]{:S(2)}) collective-permute-start(bf16[240,1280]{1,0:T(8,128)(2,1)} %get-tuple-element.118), channel_id=1, source_target_pairs={{0,1},{1,2},{2,3},{3,0},{4,5},{5,6},{6,7},{7,4},{8,9},{9,10},{10,1... | collective-permute-start | bytes 1843208 | tf_op jit(solution)/shard_map/ppermute | solution.py:560
  98.9 28.2 %collective-permute-start.16 = (bf16[240,1280]{1,0:T(8,128)(2,1)}, bf16[240,1280]{1,0:T(8,128)(2,1)}, u32[]{:S(2)}, u32[]{:S(2)}) collective-permute-start(bf16[240,1280]{1,0:T(8,128)(2,1)} %get-tuple-element.119), channel_id=1, source_target_pairs={{0,3},{1,0},{2,1},{3,2},{4,7},{5,4},{6,5},{7,6},{8,11},{9,8},{10,9... | collective-permute-start | bytes 1843208 | tf_op jit(solution)/shard_map/ppermute | solution.py:560
  100.8 26.6 %collective-permute-start.15 = (bf16[240,1280]{1,0:T(8,128)(2,1)}, bf16[240,1280]{1,0:T(8,128)(2,1)}, u32[]{:S(2)}, u32[]{:S(2)}) collective-permute-start(bf16[240,1280]{1,0:T(8,128)(2,1)} %shard_map.207), channel_id=1, source_target_pairs={{0,2},{1,3},{2,0},{3,1},{4,6},{5,7},{6,4},{7,5},{8,10},{9,11},{10,... | collective-permute-start | bytes 1843208 | tf_op jit(solution)/shard_map/ppermute | solution.py:560
  131.1 32.4 %collective-permute-start.24 = (bf16[960,1376]{1,0:T(8,128)(2,1)}, bf16[960,1376]{1,0:T(8,128)(2,1)}, u32[]{:S(2)}, u32[]{:S(2)}) collective-permute-start(bf16[960,1376]{1,0:T(8,128)(2,1)} %all-gather.9.cloned.1.call-done.refs_7_.refs_6_.refs_8_.refs_10_), channel_id=1, source_target_pairs={{0,64},{64,0},{1,65},{65,1},{2,66},{66,2},{3,67},{67,3},{4,68},{68... | collective-permute-start | bytes 7925768 | tf_op jit(solution)/shard_map/ppermute | solution.py:582
  136.4 21.0 %collective-permute-start.18 = (bf16[128,960]{1,0:T(8,128)(2,1)S(1)}, bf16[128,960]{1,0:T(8,128)(2,1)S(1)}, u32[]{:S(2)}, u32[]{:S(2)}) collective-permute-start(bf16[128,960]{1,0:T(8,128)(2,1)S(1)} %get-tuple-element.117.refs_1_), channel_id=1, source_target_pairs={{0,1},{1,2},{2,3},{3,0},{4,5},{5,6},{6,7},{7,4},{8,9},{9,10},{10,1... | collective-permute-start | bytes 737288 | tf_op jit(solution)/shard_map/ppermute | solution.py:560
  174.1 150.2 %all-gather.13.cloned.1.call-start = ((), (), s32[]{:S(2)}) async-start(), calls=%async_computation.3 | async-start | bytes 2621440 | tf_op jit(solution)/shard_map/all_gather | solution.py:761
  342.6 55.8 %collective-permute-start.61 = (bf16[16,96,640]{2,1,0:T(8,128)(2,1)S(1)}, bf16[16,96,640]{2,1,0:T(8,128)(2,1)S(1)}, u32[]{:S(2)}, u32[]{:S(2)}) collective-permute-start(bf16[16,96,640]{2,1,0:T(8,128)(2,1)S(1)} %copy-done.79), channel_id=1, source_target_pairs={{0,64},{64,0},{1,65},{65,1},{2,66},{66,2},{3,67},{67,3},{4,68},{68... | collective-permute-start | bytes 5898248 | tf_op jit(solution)/shard_map/ppermute | solution.py:582
  371.3 49.1 %collective-permute-start.60 = (bf16[16,96,640]{2,1,0:T(8,128)(2,1)}, bf16[16,96,640]{2,1,0:T(8,128)(2,1)}, u32[]{:S(2)}, u32[]{:S(2)}) collective-permute-start(bf16[16,96,640]{2,1,0:T(8,128)(2,1)} %get-tuple-element.193), channel_id=1, source_target_pairs={{0,64},{64,0},{1,65},{65,1},{2,66},{66,2},{3,67},{67,3},{4,68},{68... | collective-permute-start | bytes 5898248 | tf_op jit(solution)/shard_map/ppermute | solution.py:582
  398.5 31.1 %collective-permute-start.32 = (bf16[128,960]{1,0:T(8,128)(2,1)}, bf16[128,960]{1,0:T(8,128)(2,1)}, u32[]{:S(2)}, u32[]{:S(2)}) collective-permute-start(bf16[128,960]{1,0:T(8,128)(2,1)} %get-tuple-element.132), channel_id=1, source_target_pairs={{0,3},{1,0},{2,1},{3,2},{4,7},{5,4},{6,5},{7,6},{8,11},{9,8},{10,9... | collective-permute-start | bytes 737288 | tf_op jit(solution)/shard_map/ppermute | solution.py:560
  406.8 23.9 %collective-permute-start.34 = (bf16[128,960]{1,0:T(8,128)(2,1)}, bf16[128,960]{1,0:T(8,128)(2,1)}, u32[]{:S(2)}, u32[]{:S(2)}) collective-permute-start(bf16[128,960]{1,0:T(8,128)(2,1)} %copy-done.86), channel_id=1, source_target_pairs={{0,2},{1,3},{2,0},{3,1},{4,6},{5,7},{6,4},{7,5},{8,10},{9,11},{10,... | collective-permute-start | bytes 737288 | tf_op jit(solution)/shard_map/ppermute | solution.py:560
  432.1 24.0 %collective-permute-start.62 = (bf16[4,192,640]{2,1,0:T(8,128)(2,1)S(1)}, bf16[4,192,640]{2,1,0:T(8,128)(2,1)S(1)}, u32[]{:S(2)}, u32[]{:S(2)}) collective-permute-start(bf16[4,192,640]{2,1,0:T(8,128)(2,1)S(1)} %get-tuple-element.274), channel_id=1, source_target_pairs={{0,16},{4,20},{8,24},{12,28},{16,32},{20,36},{24,40},{28,44},{32,4... | collective-permute-start | bytes 2949128 | tf_op jit(solution)/shard_map/ppermute | solution.py:570
  433.0 26.2 %collective-permute-start.63 = (bf16[4,192,640]{2,1,0:T(8,128)(2,1)S(1)}, bf16[4,192,640]{2,1,0:T(8,128)(2,1)S(1)}, u32[]{:S(2)}, u32[]{:S(2)}) collective-permute-start(bf16[4,192,640]{2,1,0:T(8,128)(2,1)S(1)} %get-tuple-element.276), channel_id=1, source_target_pairs={{0,32},{4,36},{8,40},{12,44},{16,48},{20,52},{24,56},{28,60},{32,0... | collective-permute-start | bytes 2949128 | tf_op jit(solution)/shard_map/ppermute | solution.py:570
  434.9 27.5 %collective-permute-start.64 = (bf16[4,192,640]{2,1,0:T(8,128)(2,1)S(1)}, bf16[4,192,640]{2,1,0:T(8,128)(2,1)S(1)}, u32[]{:S(2)}, u32[]{:S(2)}) collective-permute-start(bf16[4,192,640]{2,1,0:T(8,128)(2,1)S(1)} %get-tuple-element.275), channel_id=1, source_target_pairs={{0,48},{4,52},{8,56},{12,60},{16,0},{20,4},{24,8},{28,12},{32,16},... | collective-permute-start | bytes 2949128 | tf_op jit(solution)/shard_map/ppermute | solution.py:570
  448.8 24.5 %collective-permute-start.37 = (f32[128,960]{1,0:T(8,128)}, f32[128,960]{1,0:T(8,128)}, u32[]{:S(2)}, u32[]{:S(2)}) collective-permute-start(f32[128,960]{1,0:T(8,128)} %get-tuple-element.270), channel_id=1, source_target_pairs={{0,64},{64,0},{1,65},{65,1},{2,66},{66,2},{3,67},{67,3},{4,68},{68... | collective-permute-start | bytes 1474568 | tf_op jit(solution)/shard_map/ppermute | solution.py:582
  451.3 23.1 %collective-permute-start.72 = (bf16[16,64,384]{2,1,0:T(8,128)(2,1)}, bf16[16,64,384]{2,1,0:T(8,128)(2,1)}, u32[]{:S(2)}, u32[]{:S(2)}) collective-permute-start(bf16[16,64,384]{2,1,0:T(8,128)(2,1)} %get-tuple-element.206), channel_id=1, source_target_pairs={{0,64},{64,0},{1,65},{65,1},{2,66},{66,2},{3,67},{67,3},{4,68},{68... | collective-permute-start | bytes 2359304 | tf_op jit(solution)/shard_map/ppermute | solution.py:582
  518.9 21.7 %collective-permute-start.83 = (f32[40,960]{1,0:T(8,128)S(1)}, f32[40,960]{1,0:T(8,128)S(1)}, u32[]{:S(2)}, u32[]{:S(2)}) collective-permute-start(f32[40,960]{1,0:T(8,128)S(1)} %maximum_maximum_fusion), channel_id=1, source_target_pairs={{0,0},{1,16},{2,32},{3,48},{4,1},{5,17},{6,33},{7,49},{8,2},{9,18}... | collective-permute-start | bytes 460808 | tf_op jit(solution)/shard_map/ppermute | solution.py:815
  (241 other events, 1729.6 us)
Sparse Core Ops, SparseCore 0:
  16.2 38.2 all-gather.6
  65.1 38.1 all-gather.8
  174.2 38.7 all-gather.10
  293.0 31.2 all-gather.12

commit v6 on v5

--- a/solution.py
+++ b/solution.py
@@ -296,10 +296,26 @@
     return call(body, outs, 1.3, 12, smem=1)(info, grad_low, gu, *wgu, wd)
 
 
+def feed_both_body(
+    layer, info, second, grad_low, own, other, wd, dgu_out, hidden_out, part_out, back_out, gu
+):
+    feed_body(layer, info, second, own, other, wd, gu, hidden_out, part_out)
+    feed_back_body(layer, info, grad_low, gu, own, other, wd, dgu_out, back_out)
+
+
+def feed_both(layer, info, second, grad_low, wgu, wd):
+    half = (2, ROWS, FF // 4)
+    outs = [(half, BF), ((ROWS, FF // 4), BF), ((ROWS, D), BF), ((ROWS, D), BF)]
+    body = partial(feed_both_body, layer)
+    return call(body, outs, 2.5, 12, [pltpu.VMEM(half, F32)], smem=1)(
+        info, second, grad_low, *wgu, wd
+    )
+
+
 def attend_back_body(
     info, p0, p1, p2, p3, grad, resid, gain, own, other, normed, mixed, q_ref, lse, kvs, cosine, sine,
     d_resid_out, d_low_out, dc_out, dq_out, ahead_out, o0, o1, o2, o3,
-    qd, delta, dq, dkv, dm, mx, halves,
+    qd, qd_turned, delta, dq, dkv, placed, dm, mx, halves,
 ):
     d_second = p0[...].astype(F32) + p1[...].astype(F32) + p2[...].astype(F32) + p3[...].astype(F32)
     dx, dc = norm_back(resid[...], gain[...], d_second)
@@ -330,6 +346,7 @@
                 qd[i, g, span + r * BLK : span + (r + 1) * BLK, :] = do.astype(BF)
                 dots = jnp.sum(do * head_tile(mx, i, head, True), axis=1, keepdims=True)
                 delta[i, g, there, :] = jnp.broadcast_to(dots, (BLK, 128))
+            qd_turned[i, g] = qd[i, g].astype(F32).T.astype(BF)
     dq[...] = jnp.zeros(dq.shape, F32)
     dkv[...] = jnp.zeros(dkv.shape, F32)
 
@@ -350,7 +367,7 @@
             d_low = d_scores.astype(BF)
             dq[block, g] += dot(d_low, keys)
             stacked = jnp.concatenate([d_low, probs.astype(BF)], axis=0)
-            dkv[pl.ds(at, CHUNK), g * 128 : (g + 1) * 128] += dot(stacked, qd[block, g], TN)
+            dkv[chunk, g] += dot(qd_turned[block, g], stacked)
         return carry
 
     lax.fori_loop(0, STEPS, step, 0)
@@ -368,11 +385,15 @@
                 dq_out[rows, j * 128 : (j + 1) * 128] = spin(tile, cos, -sin).astype(BF)
             else:
                 dq_out[rows, 896:960] = spin(heads[14], cos, -sin)[:, :64].astype(BF)
+    for c in range(SEQ // CHUNK):
+        for g in range(KV_HEADS):
+            rows, columns = slice(c * CHUNK, (c + 1) * CHUNK), slice(g * 128, (g + 1) * 128)
+            placed[rows, columns] = dkv[c, g].T.astype(BF)
     number = 0
     for out in (o0, o1, o2, o3):
         for b in range(out.shape[0] // BLK):
             at = pl.multiple_of(info[36 + number] * BLK, BLK)
-            out[b * BLK : (b + 1) * BLK, :] = dkv[pl.ds(at, BLK), :].astype(BF)
+            out[b * BLK : (b + 1) * BLK, :] = placed[pl.ds(at, BLK), :]
             number += 1
 
 
@@ -387,14 +408,16 @@
     shape = (2, KV_HEADS, GROUP * BLK, 128)
     scratch = [
         pltpu.VMEM((2, KV_HEADS, 2 * GROUP * BLK, 128), BF),
+        pltpu.VMEM((2, KV_HEADS, 128, 2 * GROUP * BLK), BF),
         pltpu.VMEM(shape, F32),
         pltpu.VMEM(shape, F32),
-        pltpu.VMEM((SEQ, 2 * KW), F32),
+        pltpu.VMEM((SEQ // CHUNK, KV_HEADS, 128, CHUNK), F32),
+        pltpu.VMEM((SEQ, 2 * KW), BF),
         pltpu.VMEM((ROWS, QP), BF),
         pltpu.VMEM((ROWS, QP), BF),
         pltpu.VMEM((2, ROWS, D // 2), BF),
     ]
-    return call(attend_back_body, outs, 24.0, 22, scratch, smem=1)(
+    return call(attend_back_body, outs, 20.0, 28, scratch, smem=1)(
         info, *parts, grad, resid, gain, *wo, normed, mixed, q, lse, kvs, cosine, sine, after=after
     )
 
@@ -715,7 +738,17 @@
         seconds = z_gather(second)
         if layer == 0:
             wgu = join_feed_weights(sent, second[0, 0])
-        fed = [feed(layer, place, s, wgu[layer], wd[layer]) for s in seconds]
+        if layer:
+            lows = [last_low] + [
+                lax.dynamic_index_in_dim(first_ahead, (z_rank - k) % 4, 0, False)[:, 2 * QP :]
+                for k in (1, 2, 3)
+            ]
+            fed = [
+                feed_both(layer, place, seconds[k], lows[k], wgu[layer], wd[layer])
+                for k in range(4)
+            ]
+        else:
+            fed = [feed(layer, place, s, wgu[layer], wd[layer]) for s in seconds]
         parts = [fed[0][2]] + [z_shift(fed[k][2], -k) for k in (1, 2, 3)]
         base = resid
         saved.append(
@@ -728,9 +761,6 @@
     outputs = [saved[1]["x"], add(base, *parts)]
 
     grad = own_cotangent
-    lows = [last_low] + [
-        lax.dynamic_index_in_dim(first_ahead, (z_rank - k) % 4, 0, False)[:, 2 * QP :] for k in (1, 2, 3)
-    ]
     input_grads = [None, None]
     feed_halves = [None, None]
     kept = [None, None]
@@ -747,7 +777,12 @@
         s = saved[layer]
         gain_one = gain_pair[layer][0:1]
         gain_two = gain_pair[layer][1:2]
-        back = [feed_back(layer, place, lows[k], s["gu"][k], wgu[layer], wd[layer]) for k in range(4)]
+        if layer:
+            back = [(f[0], f[3]) for f in fed]
+        else:
+            back = [
+                feed_back(layer, place, lows[k], s["gu"][k], wgu[layer], wd[layer]) for k in range(4)
+            ]
         parts = [back[0][1]] + [z_shift(back[k][1], -k) for k in (1, 2, 3)]
         keep, give = feed_grads(info, s["seconds"], [b[0] for b in back], s["hidden"], lows)
         d_resid, d_low, dc_two, dq, ahead, *goes_out = attend_back(

time: 558 us -> 552 us (0.989)
  waiting for transfers between devices: 145 us -> 171 us
  starting transfers between devices: 116 us -> 101 us
  Pallas kernels: 130 us -> 117 us
    ppermute x36, waiting for transfers between devices: 23.5 us -> 39.4 us  [z_shift(): return lax.ppermute(value, 'wsh', [(i, (i + steps) % 4) for i in range(4)])]
    pallas_call x29 -> x25, Pallas kernels: 129 us -> 117 us  [run(): pl.pallas_call(inner, in_specs=in_specs, out_specs=[pl.BlockSpec(memory_s...]
    ppermute x36, starting transfers between devices: 56.4 us -> 46.6 us  [z_shift(): return lax.ppermute(value, 'wsh', [(i, (i + steps) % 4) for i in range(4)])]
    ppermute x33, waiting for transfers between devices: 70.3 us -> 79.4 us  [ctx_shift(): return lax.ppermute(value, ('section', 'ctx'), pairs)]
    unnamed x365 -> x319, local copies, waits for them, and re-layouts: 59.8 us -> 55.8 us
  transfers between devices with their start and end apart: 88 -> 88, of which waited for: 39 -> 36; matrix products, arithmetic and copies ran while one was open for 12% -> 13% of each run, Pallas kernels for 18% -> 17%
where the time goes in v6:
time: 552 us; the launch traced here: 542 us
  waiting for transfers between devices  171 us (31%)
  Pallas kernels  117 us (21%)
  starting transfers between devices  101 us (18%)
  local copies, waits for them, and re-layouts  91.3 us (17%)
  other arithmetic  38.7 us (7%)
  between operations  23.7 us (4%)
    pallas_call x25, Pallas kernels, run(): pl.pallas_call(inner, in_specs=in_specs, out_specs=[pl.BlockSpec(memory_s...  117 us
    ppermute x33, waiting for transfers between devices, ctx_shift(): return lax.ppermute(value, ('section', 'ctx'), pairs)  79.4 us
    unnamed x319, local copies, waits for them, and re-layouts  55.8 us
    ppermute x33, starting transfers between devices, ctx_shift(): return lax.ppermute(value, ('section', 'ctx'), pairs)  49.3 us
    ppermute x36, starting transfers between devices, z_shift(): return lax.ppermute(value, 'wsh', [(i, (i + steps) % 4) for i in range(4)])  46.6 us
    ppermute x36, waiting for transfers between devices, z_shift(): return lax.ppermute(value, 'wsh', [(i, (i + steps) % 4) for i in range(4)])  39.4 us
    all_gather x2, waiting for transfers between devices, whole(): full = lax.all_gather(part, 'wsh', axis=0, tiled=True)  30.8 us
    ppermute x1, waiting for transfers between devices, shards(): grad_down = lax.ppermute(down, ('ctx', 'wsh'), moves)[None]  13.1 us
  transfers between devices with their start and end apart: 88, of which 36 were waited for; matrix products, arithmetic and copies ran while one was open for 13% of the time, Pallas kernels for 17%

profile of v6, /device:TPU:16, one launch (start us, length us, event | category | flops | bytes accessed | tf_op | source)
XLA Modules:
  0.0 542.5 jit_solution(8867344204590788471)
XLA Ops:
  16.0 4.1 collective-permute-start.2
  23.5 30.8 %all-gather.7.cloned.1.call-done.refs_3_.refs_6_.refs_8_.refs_10_ = bf16[960,1376]{1,0:T(8,128)(2,1)} async-done(((bf16[240,1376]{1,0:T(8,128)(2,1)}), bf16[960,1376]{1,0:T(8,128)(2,1)}) %all-gather.7.cloned.1.call-update) | async-done | bytes 2641936 | tf_op jit(solution)/shard_map/all_gather | solution.py:715
  110.6 10.6 %shard_map.205 = (bf16[128,960]{1,0:T(8,128)(2,1)S(1)}, f32[2,5,192,128]{3,2,1,0:T(8,128)S(1)}, bf16[2048,640]{1,0:T(8,128)(2,1)S(1)}, f32[128,960]{1,0:T(8,128)S(1)}, bf16[128,960]{1,0:T(8,128)(2,1)S(1)}) custom-call(s32[84]{0:T(128)S(1)} %concatenate.76.refs_0_, bf16[128,1024]{1,0:T(8,128)(2,1)S(1)} %copy-done.107, ...), custom_call_target="tpu_custom_call" | custom-call | flops 13200000000 | bytes 43200000 | tf_op jit(solution)/shard_map/pallas_call | solution.py:51
  140.7 8.8 %collective-permute-done.18.refs_1_.refs_2_ = bf16[128,960]{1,0:T(8,128)(2,1)S(1)} collective-permute-done((bf16[128,960]{1,0:T(8,128)(2,1)S(1)}, bf16[128,960]{1,0:T(8,128)(2,1)S(1)}, u32[]{:S(2)}, u32[]{:S(2)}) %collective-permute-start.18) | collective-permute-done | bytes 245792 | tf_op jit(solution)/shard_map/ppermute | solution.py:583
  163.6 5.2 collective-permute-done.23.refs_5_
  179.5 4.2 collective-permute-done.25
  189.0 6.4 %collective-permute-done.28.refs_3_ = bf16[512,640]{1,0:T(8,128)(2,1)S(1)} collective-permute-done((bf16[512,640]{1,0:T(8,128)(2,1)S(1)}, bf16[512,640]{1,0:T(8,128)(2,1)S(1)}, u32[]{:S(2)}, u32[]{:S(2)}) %collective-permute-start.28) | collective-permute-done | bytes 655392 | tf_op jit(solution)/shard_map/ppermute | solution.py:593
  195.4 8.0 %collective-permute-done.29.refs_4_ = bf16[512,640]{1,0:T(8,128)(2,1)S(1)} collective-permute-done((bf16[512,640]{1,0:T(8,128)(2,1)S(1)}, bf16[512,640]{1,0:T(8,128)(2,1)S(1)}, u32[]{:S(2)}, u32[]{:S(2)}) %collective-permute-start.29) | collective-permute-done | bytes 655392 | tf_op jit(solution)/shard_map/ppermute | solution.py:593
  207.3 11.4 %shard_map.213 = (bf16[128,960]{1,0:T(8,128)(2,1)S(1)}, f32[2,5,192,128]{3,2,1,0:T(8,128)S(1)}, bf16[2048,640]{1,0:T(8,128)(2,1)S(1)}, f32[128,960]{1,0:T(8,128)S(1)}, bf16[128,960]{1,0:T(8,128)(2,1)}) custom-call(s32[84]{0:T(128)S(1)} %concatenate.76.refs_0_, bf16[128,1024]{1,0:T(8,128)(2,1)S(1)} %copy-done.97, ...), custom_call_target="tpu_custom_call" | custom-call | flops 13200000000 | bytes 43200000 | tf_op jit(solution)/shard_map/pallas_call | solution.py:51
  249.4 5.7 %shard_map.218 = (bf16[16,96,640]{2,1,0:T(8,128)(2,1)S(1)}, bf16[16,96,640]{2,1,0:T(8,128)(2,1)S(1)}) custom-call(s32[84]{0:T(128)S(1)} %concatenate.76.refs_0_, bf16[128,960]{1,0:T(8,128)(2,1)} %get-tuple-element.126.refs_1_, bf16[128,960]{1,0:T(8,128)(2,1)} %collective-permute-done.31.refs_1_.refs_2_, ...), custom_call_target="tpu_custom_call" | custom-call | flops 7150000128 | bytes 23400000 | tf_op jit(solution)/shard_map/pallas_call | solution.py:51
  259.0 15.7 %shard_map.219 = (f32[128,960]{1,0:T(8,128)S(1)}, bf16[128,960]{1,0:T(8,128)(2,1)S(1)}, f32[1,960]{1,0:T(1,128)S(1)}, bf16[128,960]{1,0:T(8,128)(2,1)S(1)}, bf16...) custom-call(s32[84]{0:T(128)S(1)} %concatenate.76.refs_0_, ...), custom_call_target="tpu_custom_call" | custom-call | flops 22000001024 | bytes 72000000 | tf_op jit(solution)/shard_map/pallas_call | solution.py:51
  285.7 6.4 %collective-permute-done.43 = bf16[512,640]{1,0:T(8,128)(2,1)S(1)} collective-permute-done((bf16[512,640]{1,0:T(8,128)(2,1)}, bf16[512,640]{1,0:T(8,128)(2,1)S(1)}, u32[]{:S(2)}, u32[]{:S(2)}) %collective-permute-start.43) | collective-permute-done | bytes 655392 | tf_op jit(solution)/shard_map/ppermute | solution.py:593
  295.1 6.9 %collective-permute-done.41 = bf16[512,640]{1,0:T(8,128)(2,1)S(1)} collective-permute-done((bf16[512,640]{1,0:T(8,128)(2,1)}, bf16[512,640]{1,0:T(8,128)(2,1)S(1)}, u32[]{:S(2)}, u32[]{:S(2)}) %collective-permute-start.41) | collective-permute-done | bytes 655392 | tf_op jit(solution)/shard_map/ppermute | solution.py:593
  308.8 5.3 all-gather.13.cloned.1.call-done
  338.1 8.4 %collective-permute-done.47.refs_1_.refs_14_ = bf16[128,960]{1,0:T(8,128)(2,1)S(1)} collective-permute-done((bf16[128,960]{1,0:T(8,128)(2,1)S(1)}, bf16[128,960]{1,0:T(8,128)(2,1)S(1)}, u32[]{:S(2)}, u32[]{:S(2)}) %collective-permute-start.47) | collective-permute-done | bytes 245792 | tf_op jit(solution)/shard_map/ppermute | solution.py:583
  355.2 6.3 %shard_map.225 = (bf16[16,96,640]{2,1,0:T(8,128)(2,1)S(1)}, bf16[16,96,640]{2,1,0:T(8,128)(2,1)}) custom-call(s32[84]{0:T(128)S(1)} %concatenate.76.refs_0_, bf16[128,960]{1,0:T(8,128)(2,1)S(1)} %copy-done.34, bf16[128,960]{1,0:T(8,128)(2,1)S(1)} %copy-done.36, bf16[128,960]{1,0:T(8,128)(2,1)S(1)} %copy-done.38, bf16[128,960]{1,0:T(8,128)(2,1)S(1)} %copy-done.40, ...), custom_call_target="tpu_custom_call" | custom-call | flops 7150000128 | bytes 23400000 | tf_op jit(solution)/shard_map/pallas_call | solution.py:51
  363.3 17.2 %shard_map.226 = (f32[128,960]{1,0:T(8,128)S(1)}, bf16[128,960]{1,0:T(8,128)(2,1)S(1)}, f32[1,960]{1,0:T(1,128)S(1)}, bf16[128,960]{1,0:T(8,128)(2,1)S(1)}, bf16...) custom-call(s32[84]{0:T(128)S(1)} %concatenate.76.refs_0_, ...), custom_call_target="tpu_custom_call" | custom-call | flops 22000001024 | bytes 72000000 | tf_op jit(solution)/shard_map/pallas_call | solution.py:51
  395.9 4.5 collective-permute-done.53
  435.6 10.0 %collective-permute-done.58.refs_4_ = bf16[128,640]{1,0:T(8,128)(2,1)S(1)} collective-permute-done((bf16[128,640]{1,0:T(8,128)(2,1)S(1)}, bf16[128,640]{1,0:T(8,128)(2,1)S(1)}, u32[]{:S(2)}, u32[]{:S(2)}) %collective-permute-start.58) | collective-permute-done | bytes 163872 | tf_op jit(solution)/shard_map/ppermute | solution.py:593
  454.1 6.5 %collective-permute-done.65.refs_2_ = bf16[128,640]{1,0:T(8,128)(2,1)S(1)} collective-permute-done((bf16[128,640]{1,0:T(8,128)(2,1)S(1)}, bf16[128,640]{1,0:T(8,128)(2,1)S(1)}, u32[]{:S(2)}, u32[]{:S(2)}) %collective-permute-start.65) | collective-permute-done | bytes 163872 | tf_op jit(solution)/shard_map/ppermute | solution.py:583
  461.2 4.1 shard_map.229
  481.0 4.1 collective-permute-done.73
  492.3 7.8 %collective-permute-done.78 = bf16[96,2048]{1,0:T(8,128)(2,1)S(1)} collective-permute-done((bf16[96,2048]{1,0:T(8,128)(2,1)S(1)}, bf16[96,2048]{1,0:T(8,128)(2,1)S(1)}, u32[]{:S(2)}, u32[]{:S(2)}) %collective-permute-start.78) | collective-permute-done | bytes 393248 | tf_op jit(solution)/shard_map/ppermute | solution.py:593
  521.7 13.1 %collective-permute-done.83 = f32[40,960]{1,0:T(8,128)S(1)} collective-permute-done((f32[40,960]{1,0:T(8,128)S(1)}, f32[40,960]{1,0:T(8,128)S(1)}, u32[]{:S(2)}, u32[]{:S(2)}) %collective-permute-start.83) | collective-permute-done | bytes 153632 | tf_op jit(solution)/shard_map/ppermute | solution.py:850
  (633 shorter events, 307.2 us)
Async XLA Ops:
  7.2 47.2 %all-gather.7.cloned.1.call-start = ((), (), s32[]{:S(2)}) async-start(), calls=%async_computation | async-start | bytes 3379200 | tf_op jit(solution)/shard_map/all_gather | solution.py:715
  15.9 116.6 %all-gather.9.cloned.1.call-start = ((), (), s32[]{:S(2)}) async-start(), calls=%async_computation.1 | async-start | bytes 3379200 | tf_op jit(solution)/shard_map/all_gather | solution.py:715
  16.0 43.6 %collective-permute-start.2 = (bf16[2,240]{1,0:T(2,128)(2,1)S(1)}, bf16[2,240]{1,0:T(2,128)(2,1)S(1)}, u32[]{:S(2)}, u32[]{:S(2)}) collective-permute-start(bf16[2,240]{1,0:T(2,128)(2,1)S(1)} %pad_maximum_fusion.13), channel_id=1, source_target_pairs={{0,3},{1,0},{2,1},{3,2},{4,7},{5,4},{6,5},{7,6},{8,11},{9,8},{10,9... | collective-permute-start | bytes 2888 | tf_op jit(solution)/shard_map/ppermute | solution.py:583
  20.1 39.5 %collective-permute-start.1 = (bf16[2,240]{1,0:T(2,128)(2,1)S(1)}, bf16[2,240]{1,0:T(2,128)(2,1)S(1)}, u32[]{:S(2)}, u32[]{:S(2)}) collective-permute-start(bf16[2,240]{1,0:T(2,128)(2,1)S(1)} %pad_maximum_fusion.13), channel_id=1, source_target_pairs={{0,2},{1,3},{2,0},{3,1},{4,6},{5,7},{6,4},{7,5},{8,10},{9,11},{10,... | collective-permute-start | bytes 2888 | tf_op jit(solution)/shard_map/ppermute | solution.py:583
  20.1 39.5 %collective-permute-start = (bf16[2,240]{1,0:T(2,128)(2,1)S(1)}, bf16[2,240]{1,0:T(2,128)(2,1)S(1)}, u32[]{:S(2)}, u32[]{:S(2)}) collective-permute-start(bf16[2,240]{1,0:T(2,128)(2,1)S(1)} %pad_maximum_fusion.13), channel_id=1, source_target_pairs={{0,1},{1,2},{2,3},{3,0},{4,5},{5,6},{6,7},{7,4},{8,9},{9,10},{10,1... | collective-permute-start | bytes 2888 | tf_op jit(solution)/shard_map/ppermute | solution.py:583
  22.6 42.3 %collective-permute-start.13 = (bf16[240,2560]{1,0:T(8,128)(2,1)}, bf16[240,2560]{1,0:T(8,128)(2,1)}, u32[]{:S(2)}, u32[]{:S(2)}) collective-permute-start(bf16[240,2560]{1,0:T(8,128)(2,1)} %bitcast_select_fusion.1), channel_id=1, source_target_pairs={{0,64},{64,0},{1,65},{65,1},{2,66},{66,2},{3,67},{67,3},{4,68},{68... | collective-permute-start | bytes 3686408 | tf_op jit(solution)/shard_map/ppermute | solution.py:605
  64.8 166.1 %all-gather.11.cloned.1.call-start = ((), (), s32[]{:S(2)}) async-start(), calls=%async_computation.2 | async-start | bytes 3932160 | tf_op jit(solution)/shard_map/all_gather | solution.py:729
  78.9 21.4 %collective-permute-start.12 = (bf16[640,960]{0,1:T(8,128)(2,1)}, bf16[640,960]{0,1:T(8,128)(2,1)}, u32[]{:S(2)}, u32[]{:S(2)}) collective-permute-start(bf16[640,960]{0,1:T(8,128)(2,1)} %copy.93), channel_id=1, source_target_pairs={{0,64},{64,0},{1,65},{65,1},{2,66},{66,2},{3,67},{67,3},{4,68},{68... | collective-permute-start | bytes 3686408 | tf_op jit(solution)/shard_map/ppermute | solution.py:605
  94.2 32.2 %collective-permute-start.16 = (bf16[240,1280]{1,0:T(8,128)(2,1)}, bf16[240,1280]{1,0:T(8,128)(2,1)}, u32[]{:S(2)}, u32[]{:S(2)}) collective-permute-start(bf16[240,1280]{1,0:T(8,128)(2,1)} %get-tuple-element.115), channel_id=1, source_target_pairs={{0,3},{1,0},{2,1},{3,2},{4,7},{5,4},{6,5},{7,6},{8,11},{9,8},{10,9... | collective-permute-start | bytes 1843208 | tf_op jit(solution)/shard_map/ppermute | solution.py:583
  98.6 30.2 %collective-permute-start.14 = (bf16[240,1280]{1,0:T(8,128)(2,1)}, bf16[240,1280]{1,0:T(8,128)(2,1)}, u32[]{:S(2)}, u32[]{:S(2)}) collective-permute-start(bf16[240,1280]{1,0:T(8,128)(2,1)} %get-tuple-element.114), channel_id=1, source_target_pairs={{0,1},{1,2},{2,3},{3,0},{4,5},{5,6},{6,7},{7,4},{8,9},{9,10},{10,1... | collective-permute-start | bytes 1843208 | tf_op jit(solution)/shard_map/ppermute | solution.py:583
  100.4 28.5 %collective-permute-start.15 = (bf16[240,1280]{1,0:T(8,128)(2,1)}, bf16[240,1280]{1,0:T(8,128)(2,1)}, u32[]{:S(2)}, u32[]{:S(2)}) collective-permute-start(bf16[240,1280]{1,0:T(8,128)(2,1)} %shard_map.207), channel_id=1, source_target_pairs={{0,2},{1,3},{2,0},{3,1},{4,6},{5,7},{6,4},{7,5},{8,10},{9,11},{10,... | collective-permute-start | bytes 1843208 | tf_op jit(solution)/shard_map/ppermute | solution.py:583
  132.6 29.9 %collective-permute-start.24 = (bf16[960,1376]{1,0:T(8,128)(2,1)}, bf16[960,1376]{1,0:T(8,128)(2,1)}, u32[]{:S(2)}, u32[]{:S(2)}) collective-permute-start(bf16[960,1376]{1,0:T(8,128)(2,1)} %all-gather.9.cloned.1.call-done.refs_7_.refs_6_.refs_8_.refs_10_), channel_id=1, source_target_pairs={{0,64},{64,0},{1,65},{65,1},{2,66},{66,2},{3,67},{67,3},{4,68},{68... | collective-permute-start | bytes 7925768 | tf_op jit(solution)/shard_map/ppermute | solution.py:605
  175.1 139.0 %all-gather.13.cloned.1.call-start = ((), (), s32[]{:S(2)}) async-start(), calls=%async_computation.3 | async-start | bytes 2621440 | tf_op jit(solution)/shard_map/all_gather | solution.py:796
  222.7 21.5 %collective-permute-start.35 = (bf16[128,960]{1,0:T(8,128)(2,1)}, bf16[128,960]{1,0:T(8,128)(2,1)}, u32[]{:S(2)}, u32[]{:S(2)}) collective-permute-start(bf16[128,960]{1,0:T(8,128)(2,1)} %get-tuple-element.126.refs_1_), channel_id=1, source_target_pairs={{0,3},{1,0},{2,1},{3,2},{4,7},{5,4},{6,5},{7,6},{8,11},{9,8},{10,9... | collective-permute-start | bytes 737288 | tf_op jit(solution)/shard_map/ppermute | solution.py:583
  332.1 51.6 %collective-permute-start.61 = (bf16[16,96,640]{2,1,0:T(8,128)(2,1)S(1)}, bf16[16,96,640]{2,1,0:T(8,128)(2,1)S(1)}, u32[]{:S(2)}, u32[]{:S(2)}) collective-permute-start(bf16[16,96,640]{2,1,0:T(8,128)(2,1)S(1)} %copy-done.63), channel_id=1, source_target_pairs={{0,64},{64,0},{1,65},{65,1},{2,66},{66,2},{3,67},{67,3},{4,68},{68... | collective-permute-start | bytes 5898248 | tf_op jit(solution)/shard_map/ppermute | solution.py:605
  362.7 42.9 %collective-permute-start.60 = (bf16[16,96,640]{2,1,0:T(8,128)(2,1)}, bf16[16,96,640]{2,1,0:T(8,128)(2,1)}, u32[]{:S(2)}, u32[]{:S(2)}) collective-permute-start(bf16[16,96,640]{2,1,0:T(8,128)(2,1)} %get-tuple-element.185), channel_id=1, source_target_pairs={{0,64},{64,0},{1,65},{65,1},{2,66},{66,2},{3,67},{67,3},{4,68},{68... | collective-permute-start | bytes 5898248 | tf_op jit(solution)/shard_map/ppermute | solution.py:605
  383.8 30.6 %collective-permute-start.36 = (bf16[128,960]{1,0:T(8,128)(2,1)}, bf16[128,960]{1,0:T(8,128)(2,1)}, u32[]{:S(2)}, u32[]{:S(2)}) collective-permute-start(bf16[128,960]{1,0:T(8,128)(2,1)} %get-tuple-element.131), channel_id=1, source_target_pairs={{0,1},{1,2},{2,3},{3,0},{4,5},{5,6},{6,7},{7,4},{8,9},{9,10},{10,1... | collective-permute-start | bytes 737288 | tf_op jit(solution)/shard_map/ppermute | solution.py:583
  391.4 26.1 %collective-permute-start.34 = (bf16[128,960]{1,0:T(8,128)(2,1)}, bf16[128,960]{1,0:T(8,128)(2,1)}, u32[]{:S(2)}, u32[]{:S(2)}) collective-permute-start(bf16[128,960]{1,0:T(8,128)(2,1)} %copy-done.68), channel_id=1, source_target_pairs={{0,2},{1,3},{2,0},{3,1},{4,6},{5,7},{6,4},{7,5},{8,10},{9,11},{10,... | collective-permute-start | bytes 737288 | tf_op jit(solution)/shard_map/ppermute | solution.py:583
  395.2 23.8 %collective-permute-start.32 = (bf16[128,960]{1,0:T(8,128)(2,1)}, bf16[128,960]{1,0:T(8,128)(2,1)}, u32[]{:S(2)}, u32[]{:S(2)}) collective-permute-start(bf16[128,960]{1,0:T(8,128)(2,1)} %copy-done.67), channel_id=1, source_target_pairs={{0,3},{1,0},{2,1},{3,2},{4,7},{5,4},{6,5},{7,6},{8,11},{9,8},{10,9... | collective-permute-start | bytes 737288 | tf_op jit(solution)/shard_map/ppermute | solution.py:583
  419.0 30.1 %collective-permute-start.64 = (bf16[4,192,640]{2,1,0:T(8,128)(2,1)S(1)}, bf16[4,192,640]{2,1,0:T(8,128)(2,1)S(1)}, u32[]{:S(2)}, u32[]{:S(2)}) collective-permute-start(bf16[4,192,640]{2,1,0:T(8,128)(2,1)S(1)} %get-tuple-element.267), channel_id=1, source_target_pairs={{0,48},{4,52},{8,56},{12,60},{16,0},{20,4},{24,8},{28,12},{32,16},... | collective-permute-start | bytes 2949128 | tf_op jit(solution)/shard_map/ppermute | solution.py:593
  419.6 29.6 %collective-permute-start.63 = (bf16[4,192,640]{2,1,0:T(8,128)(2,1)S(1)}, bf16[4,192,640]{2,1,0:T(8,128)(2,1)S(1)}, u32[]{:S(2)}, u32[]{:S(2)}) collective-permute-start(bf16[4,192,640]{2,1,0:T(8,128)(2,1)S(1)} %get-tuple-element.268), channel_id=1, source_target_pairs={{0,32},{4,36},{8,40},{12,44},{16,48},{20,52},{24,56},{28,60},{32,0... | collective-permute-start | bytes 2949128 | tf_op jit(solution)/shard_map/ppermute | solution.py:593
  423.7 28.1 %collective-permute-start.62 = (bf16[4,192,640]{2,1,0:T(8,128)(2,1)S(1)}, bf16[4,192,640]{2,1,0:T(8,128)(2,1)S(1)}, u32[]{:S(2)}, u32[]{:S(2)}) collective-permute-start(bf16[4,192,640]{2,1,0:T(8,128)(2,1)S(1)} %get-tuple-element.266), channel_id=1, source_target_pairs={{0,16},{4,20},{8,24},{12,28},{16,32},{20,36},{24,40},{28,44},{32,4... | collective-permute-start | bytes 2949128 | tf_op jit(solution)/shard_map/ppermute | solution.py:593
  435.6 29.7 %collective-permute-start.37 = (f32[128,960]{1,0:T(8,128)}, f32[128,960]{1,0:T(8,128)}, u32[]{:S(2)}, u32[]{:S(2)}) collective-permute-start(f32[128,960]{1,0:T(8,128)} %get-tuple-element.262), channel_id=1, source_target_pairs={{0,64},{64,0},{1,65},{65,1},{2,66},{66,2},{3,67},{67,3},{4,68},{68... | collective-permute-start | bytes 1474568 | tf_op jit(solution)/shard_map/ppermute | solution.py:605
  512.8 22.0 %collective-permute-start.83 = (f32[40,960]{1,0:T(8,128)S(1)}, f32[40,960]{1,0:T(8,128)S(1)}, u32[]{:S(2)}, u32[]{:S(2)}) collective-permute-start(f32[40,960]{1,0:T(8,128)S(1)} %maximum_maximum_fusion), channel_id=1, source_target_pairs={{0,0},{1,16},{2,32},{3,48},{4,1},{5,17},{6,33},{7,49},{8,2},{9,18}... | collective-permute-start | bytes 460808 | tf_op jit(solution)/shard_map/ppermute | solution.py:850
  (218 other events, 1783.3 us)
Sparse Core Ops, SparseCore 0:
  16.0 38.2 all-gather.6
  64.9 37.3 all-gather.8
  175.2 37.5 all-gather.10
  281.4 32.6 all-gather.12

commit v7 on v6

--- a/solution.py
+++ b/solution.py
@@ -313,8 +313,8 @@
 
 
 def attend_back_body(
-    info, p0, p1, p2, p3, grad, resid, gain, own, other, normed, mixed, q_ref, lse, kvs, cosine, sine,
-    d_resid_out, d_low_out, dc_out, dq_out, ahead_out, o0, o1, o2, o3,
+    info, p0, p1, p2, p3, grad, resid, gain, own, other, mixed, q_ref, lse, kvs, cosine, sine,
+    d_resid_out, d_low_out, dc_out, dq_out, o0, o1, o2, o3,
     qd, qd_turned, delta, dq, dkv, placed, dm, mx, halves,
 ):
     d_second = p0[...].astype(F32) + p1[...].astype(F32) + p2[...].astype(F32) + p3[...].astype(F32)
@@ -328,9 +328,6 @@
     halves[0] = d_resid[:, : D // 2].astype(BF)
     halves[1] = d_resid[:, D // 2 :].astype(BF)
     d_mixed = dot(halves[side], own[:, HALF:], NT) + dot(halves[1 - side], other[:, HALF:], NT)
-    ahead_out[:, :D] = normed[...]
-    ahead_out[:, QP : QP + D] = mixed[...]
-    ahead_out[:, D:QP] = jnp.zeros((ROWS, QP - D), BF)
     dm[:, :D] = d_mixed.astype(BF)
     dm[:, D:] = jnp.zeros((ROWS, QP - D), BF)
     mx[:, :D] = mixed[...]
@@ -397,13 +394,12 @@
             number += 1
 
 
-def attend_back(info, parts, grad, resid, gain, wo, normed, mixed, q, lse, kvs, cosine, sine, after=()):
+def attend_back(info, parts, grad, resid, gain, wo, mixed, q, lse, kvs, cosine, sine, after=()):
     outs = [
         ((ROWS, D), F32),
         ((ROWS, D), BF),
         ((1, D), F32),
         ((ROWS, D), BF),
-        ((ROWS, QP + D), BF),
     ] + [((4 * ROWS, 2 * KW), BF)] * 4
     shape = (2, KV_HEADS, GROUP * BLK, 128)
     scratch = [
@@ -418,7 +414,7 @@
         pltpu.VMEM((2, ROWS, D // 2), BF),
     ]
     return call(attend_back_body, outs, 20.0, 28, scratch, smem=1)(
-        info, *parts, grad, resid, gain, *wo, normed, mixed, q, lse, kvs, cosine, sine, after=after
+        info, *parts, grad, resid, gain, *wo, mixed, q, lse, kvs, cosine, sine, after=after
     )
 
 
@@ -785,15 +781,20 @@
             ]
         parts = [back[0][1]] + [z_shift(back[k][1], -k) for k in (1, 2, 3)]
         keep, give = feed_grads(info, s["seconds"], [b[0] for b in back], s["hidden"], lows)
-        d_resid, d_low, dc_two, dq, ahead, *goes_out = attend_back(
-            info, parts, grad, s["resid"], gain_two, gathered[layer], s["normed"], s["mixed"], s["q"],
-            s["lse"], s["kvs"], cosine, sine, after=(token(keep),),
+        mark = token(keep)
+        d_resid, d_low, dc_two, dq, *goes_out = attend_back(
+            info, parts, grad, s["resid"], gain_two, gathered[layer], s["mixed"], s["q"],
+            s["lse"], s["kvs"], cosine, sine, after=(mark,),
         )
         feed_halves[layer] = add(keep, swap(give)).astype(BF)
         row = add(goes_out[0], *[reduce_shift(goes_out[k], k) for k in (1, 2, 3)])
         row = row.astype(BF).reshape(4, ROWS, 2 * KW)
         own_pieces = [row[0]] + [gather_shift(row[k], k) for k in (1, 2, 3)]
-        ahead = lax.all_gather(ahead, "wsh") if layer else first_ahead
+        ahead = first_ahead
+        if layer:
+            gap = jnp.zeros((ROWS, QP - D), BF)
+            ahead = jnp.concatenate([s["normed"], gap, s["mixed"]], axis=1)
+            ahead = lax.all_gather(hold([ahead], mark)[0], "wsh")
         if layer == 0:
             kept[1] = attention_grads(none_of(d_low[0, 0]))
         cut, grad, dc_one = project_back(

time: 552 us -> 556 us (level)
  local copies, waits for them, and re-layouts: 91.3 us -> 102 us
  waiting for transfers between devices: 171 us -> 162 us
    unnamed x319 -> x305, local copies, waits for them, and re-layouts: 55.8 us -> 63.7 us
    ppermute x36, waiting for transfers between devices: 39.4 us -> 33.6 us  [z_shift(): return lax.ppermute(value, 'wsh', [(i, (i + steps) % 4) for i in range(4)])]
  transfers between devices with their start and end apart: 88 -> 88, of which waited for: 36 -> 36; matrix products, arithmetic and copies ran while one was open for 13% -> 13% of each run, Pallas kernels for 17% -> 21%
where the time goes in v7:
time: 556 us; the launch traced here: 546 us
  waiting for transfers between devices  162 us (29%)
  Pallas kernels  119 us (21%)
  local copies, waits for them, and re-layouts  102 us (18%)
  starting transfers between devices  101 us (18%)
  other arithmetic  37.6 us (7%)
  between operations  23.5 us (4%)
    pallas_call x25, Pallas kernels, run(): pl.pallas_call(inner, in_specs=in_specs, out_specs=[pl.BlockSpec(memory_s...  119 us
    ppermute x33, waiting for transfers between devices, ctx_shift(): return lax.ppermute(value, ('section', 'ctx'), pairs)  82 us
    unnamed x305, local copies, waits for them, and re-layouts  63.7 us
    ppermute x33, starting transfers between devices, ctx_shift(): return lax.ppermute(value, ('section', 'ctx'), pairs)  48.5 us
    ppermute x36, starting transfers between devices, z_shift(): return lax.ppermute(value, 'wsh', [(i, (i + steps) % 4) for i in range(4)])  45.6 us
    ppermute x36, waiting for transfers between devices, z_shift(): return lax.ppermute(value, 'wsh', [(i, (i + steps) % 4) for i in range(4)])  33.6 us
    all_gather x2, waiting for transfers between devices, whole(): full = lax.all_gather(part, 'wsh', axis=0, tiled=True)  30.9 us
    ppermute x1, waiting for transfers between devices, shards(): grad_down = lax.ppermute(down, ('ctx', 'wsh'), moves)[None]  13.1 us
  transfers between devices with their start and end apart: 88, of which 36 were waited for; matrix products, arithmetic and copies ran while one was open for 13% of the time, Pallas kernels for 21%

profile of v7, /device:TPU:16, one launch (start us, length us, event | category | flops | bytes accessed | tf_op | source)
XLA Modules:
  0.0 545.7 jit_solution(8555867861044897762)
XLA Ops:
  16.0 4.1 collective-permute-start.2
  23.5 30.9 %all-gather.7.cloned.1.call-done.refs_3_.refs_6_.refs_8_.refs_10_ = bf16[960,1376]{1,0:T(8,128)(2,1)} async-done(((bf16[240,1376]{1,0:T(8,128)(2,1)}), bf16[960,1376]{1,0:T(8,128)(2,1)}) %all-gather.7.cloned.1.call-update) | async-done | bytes 2641936 | tf_op jit(solution)/shard_map/all_gather | solution.py:711
  110.5 10.6 %shard_map.205 = (bf16[128,960]{1,0:T(8,128)(2,1)S(1)}, f32[2,5,192,128]{3,2,1,0:T(8,128)S(1)}, bf16[2048,640]{1,0:T(8,128)(2,1)S(1)}, f32[128,960]{1,0:T(8,128)S(1)}, bf16[128,960]{1,0:T(8,128)(2,1)S(1)}) custom-call(s32[84]{0:T(128)S(1)} %concatenate.79.refs_0_, bf16[128,1024]{1,0:T(8,128)(2,1)S(1)} %copy-done.102, ...), custom_call_target="tpu_custom_call" | custom-call | flops 13200000000 | bytes 43200000 | tf_op jit(solution)/shard_map/pallas_call | solution.py:51
  140.7 8.8 %collective-permute-done.18.refs_1_.refs_2_ = bf16[128,960]{1,0:T(8,128)(2,1)S(1)} collective-permute-done((bf16[128,960]{1,0:T(8,128)(2,1)S(1)}, bf16[128,960]{1,0:T(8,128)(2,1)S(1)}, u32[]{:S(2)}, u32[]{:S(2)}) %collective-permute-start.18) | collective-permute-done | bytes 245792 | tf_op jit(solution)/shard_map/ppermute | solution.py:579
  163.6 5.2 collective-permute-done.23.refs_5_
  179.6 4.2 collective-permute-done.25
  189.1 6.4 %collective-permute-done.28.refs_3_ = bf16[512,640]{1,0:T(8,128)(2,1)S(1)} collective-permute-done((bf16[512,640]{1,0:T(8,128)(2,1)S(1)}, bf16[512,640]{1,0:T(8,128)(2,1)S(1)}, u32[]{:S(2)}, u32[]{:S(2)}) %collective-permute-start.28) | collective-permute-done | bytes 655392 | tf_op jit(solution)/shard_map/ppermute | solution.py:589
  195.5 7.9 %collective-permute-done.29.refs_4_ = bf16[512,640]{1,0:T(8,128)(2,1)S(1)} collective-permute-done((bf16[512,640]{1,0:T(8,128)(2,1)S(1)}, bf16[512,640]{1,0:T(8,128)(2,1)S(1)}, u32[]{:S(2)}, u32[]{:S(2)}) %collective-permute-start.29) | collective-permute-done | bytes 655392 | tf_op jit(solution)/shard_map/ppermute | solution.py:589
  207.4 11.3 %shard_map.213 = (bf16[128,960]{1,0:T(8,128)(2,1)S(1)}, f32[2,5,192,128]{3,2,1,0:T(8,128)S(1)}, bf16[2048,640]{1,0:T(8,128)(2,1)S(1)}, f32[128,960]{1,0:T(8,128)S(1)}, bf16[128,960]{1,0:T(8,128)(2,1)}) custom-call(s32[84]{0:T(128)S(1)} %concatenate.79.refs_0_, bf16[128,1024]{1,0:T(8,128)(2,1)S(1)} %copy-done.92, ...), custom_call_target="tpu_custom_call" | custom-call | flops 13200000000 | bytes 43200000 | tf_op jit(solution)/shard_map/pallas_call | solution.py:51
  257.2 5.6 %shard_map.218 = (bf16[16,96,640]{2,1,0:T(8,128)(2,1)S(1)}, bf16[16,96,640]{2,1,0:T(8,128)(2,1)S(1)}) custom-call(s32[84]{0:T(128)S(1)} %concatenate.79.refs_0_, bf16[128,960]{1,0:T(8,128)(2,1)} %get-tuple-element.125.refs_1_, bf16[128,960]{1,0:T(8,128)(2,1)} %collective-permute-done.31.refs_1_.refs_2_, ...), custom_call_target="tpu_custom_call" | custom-call | flops 7150000128 | bytes 23400000 | tf_op jit(solution)/shard_map/pallas_call | solution.py:51
  277.0 16.1 %shard_map.219 = (f32[128,960]{1,0:T(8,128)S(1)}, bf16[128,960]{1,0:T(8,128)(2,1)S(1)}, f32[1,960]{1,0:T(1,128)S(1)}, bf16[128,960]{1,0:T(8,128)(2,1)S(1)}, bf16...) custom-call(s32[84]{0:T(128)S(1)} %concatenate.79.refs_0_, ...), custom_call_target="tpu_custom_call" | custom-call | flops 22000001024 | bytes 72000000 | tf_op jit(solution)/shard_map/pallas_call | solution.py:51
  297.3 6.5 %collective-permute-done.43 = bf16[512,640]{1,0:T(8,128)(2,1)S(1)} collective-permute-done((bf16[512,640]{1,0:T(8,128)(2,1)S(1)}, bf16[512,640]{1,0:T(8,128)(2,1)S(1)}, u32[]{:S(2)}, u32[]{:S(2)}) %collective-permute-start.43) | collective-permute-done | bytes 655392 | tf_op jit(solution)/shard_map/ppermute | solution.py:589
  306.7 7.7 %collective-permute-done.41 = bf16[512,640]{1,0:T(8,128)(2,1)S(1)} collective-permute-done((bf16[512,640]{1,0:T(8,128)(2,1)S(1)}, bf16[512,640]{1,0:T(8,128)(2,1)S(1)}, u32[]{:S(2)}, u32[]{:S(2)}) %collective-permute-start.41) | collective-permute-done | bytes 655392 | tf_op jit(solution)/shard_map/ppermute | solution.py:589
  346.7 4.3 collective-permute-done.47.refs_1_.refs_14_
  360.3 6.3 %shard_map.226 = (bf16[16,96,640]{2,1,0:T(8,128)(2,1)S(1)}, bf16[16,96,640]{2,1,0:T(8,128)(2,1)}) custom-call(s32[84]{0:T(128)S(1)} %concatenate.79.refs_0_, bf16[128,960]{1,0:T(8,128)(2,1)S(1)} %copy-done.35, bf16[128,960]{1,0:T(8,128)(2,1)S(1)} %copy-done.37, bf16[128,960]{1,0:T(8,128)(2,1)S(1)} %copy-done.39, bf16[128,960]{1,0:T(8,128)(2,1)S(1)} %copy-done.41, ...), custom_call_target="tpu_custom_call" | custom-call | flops 7150000128 | bytes 23400000 | tf_op jit(solution)/shard_map/pallas_call | solution.py:51
  370.2 17.0 %shard_map.227 = (f32[128,960]{1,0:T(8,128)S(1)}, bf16[128,960]{1,0:T(8,128)(2,1)S(1)}, f32[1,960]{1,0:T(1,128)S(1)}, bf16[128,960]{1,0:T(8,128)(2,1)S(1)}, bf16...) custom-call(s32[84]{0:T(128)S(1)} %concatenate.79.refs_0_, ...), custom_call_target="tpu_custom_call" | custom-call | flops 22000001024 | bytes 72000000 | tf_op jit(solution)/shard_map/pallas_call | solution.py:51
  402.4 4.4 collective-permute-done.53
  433.3 9.0 %collective-permute-done.56.refs_2_ = bf16[128,640]{1,0:T(8,128)(2,1)S(1)} collective-permute-done((bf16[128,640]{1,0:T(8,128)(2,1)S(1)}, bf16[128,640]{1,0:T(8,128)(2,1)S(1)}, u32[]{:S(2)}, u32[]{:S(2)}) %collective-permute-start.56) | collective-permute-done | bytes 163872 | tf_op jit(solution)/shard_map/ppermute | solution.py:589
  458.1 6.3 %collective-permute-done.65.refs_2_ = bf16[128,640]{1,0:T(8,128)(2,1)S(1)} collective-permute-done((bf16[128,640]{1,0:T(8,128)(2,1)S(1)}, bf16[128,640]{1,0:T(8,128)(2,1)S(1)}, u32[]{:S(2)}, u32[]{:S(2)}) %collective-permute-start.65) | collective-permute-done | bytes 163872 | tf_op jit(solution)/shard_map/ppermute | solution.py:579
  465.0 4.1 shard_map.230
  485.1 4.1 collective-permute-done.73
  496.6 6.8 %collective-permute-done.78 = bf16[96,2048]{1,0:T(8,128)(2,1)S(1)} collective-permute-done((bf16[96,2048]{1,0:T(8,128)(2,1)S(1)}, bf16[96,2048]{1,0:T(8,128)(2,1)S(1)}, u32[]{:S(2)}, u32[]{:S(2)}) %collective-permute-start.78) | collective-permute-done | bytes 393248 | tf_op jit(solution)/shard_map/ppermute | solution.py:589
  516.0 4.6 collective-permute-start.83
  524.9 13.1 %collective-permute-done.83 = f32[40,960]{1,0:T(8,128)S(1)} collective-permute-done((f32[40,960]{1,0:T(8,128)S(1)}, f32[40,960]{1,0:T(8,128)S(1)}, u32[]{:S(2)}, u32[]{:S(2)}) %collective-permute-start.83) | collective-permute-done | bytes 153632 | tf_op jit(solution)/shard_map/ppermute | solution.py:851
  (622 shorter events, 316.9 us)
Async XLA Ops:
  7.2 47.2 %all-gather.7.cloned.1.call-start = ((), (), s32[]{:S(2)}) async-start(), calls=%async_computation | async-start | bytes 3379200 | tf_op jit(solution)/shard_map/all_gather | solution.py:711
  15.9 116.7 %all-gather.9.cloned.1.call-start = ((), (), s32[]{:S(2)}) async-start(), calls=%async_computation.1 | async-start | bytes 3379200 | tf_op jit(solution)/shard_map/all_gather | solution.py:711
  16.0 43.6 %collective-permute-start.2 = (bf16[2,240]{1,0:T(2,128)(2,1)S(1)}, bf16[2,240]{1,0:T(2,128)(2,1)S(1)}, u32[]{:S(2)}, u32[]{:S(2)}) collective-permute-start(bf16[2,240]{1,0:T(2,128)(2,1)S(1)} %pad_maximum_fusion.13), channel_id=1, source_target_pairs={{0,3},{1,0},{2,1},{3,2},{4,7},{5,4},{6,5},{7,6},{8,11},{9,8},{10,9... | collective-permute-start | bytes 2888 | tf_op jit(solution)/shard_map/ppermute | solution.py:579
  20.1 39.5 %collective-permute-start.1 = (bf16[2,240]{1,0:T(2,128)(2,1)S(1)}, bf16[2,240]{1,0:T(2,128)(2,1)S(1)}, u32[]{:S(2)}, u32[]{:S(2)}) collective-permute-start(bf16[2,240]{1,0:T(2,128)(2,1)S(1)} %pad_maximum_fusion.13), channel_id=1, source_target_pairs={{0,2},{1,3},{2,0},{3,1},{4,6},{5,7},{6,4},{7,5},{8,10},{9,11},{10,... | collective-permute-start | bytes 2888 | tf_op jit(solution)/shard_map/ppermute | solution.py:579
  20.1 39.5 %collective-permute-start = (bf16[2,240]{1,0:T(2,128)(2,1)S(1)}, bf16[2,240]{1,0:T(2,128)(2,1)S(1)}, u32[]{:S(2)}, u32[]{:S(2)}) collective-permute-start(bf16[2,240]{1,0:T(2,128)(2,1)S(1)} %pad_maximum_fusion.13), channel_id=1, source_target_pairs={{0,1},{1,2},{2,3},{3,0},{4,5},{5,6},{6,7},{7,4},{8,9},{9,10},{10,1... | collective-permute-start | bytes 2888 | tf_op jit(solution)/shard_map/ppermute | solution.py:579
  22.6 42.3 %collective-permute-start.13 = (bf16[240,2560]{1,0:T(8,128)(2,1)}, bf16[240,2560]{1,0:T(8,128)(2,1)}, u32[]{:S(2)}, u32[]{:S(2)}) collective-permute-start(bf16[240,2560]{1,0:T(8,128)(2,1)} %bitcast_select_fusion.1), channel_id=1, source_target_pairs={{0,64},{64,0},{1,65},{65,1},{2,66},{66,2},{3,67},{67,3},{4,68},{68... | collective-permute-start | bytes 3686408 | tf_op jit(solution)/shard_map/ppermute | solution.py:601
  64.8 172.2 %all-gather.11.cloned.1.call-start = ((), (), s32[]{:S(2)}) async-start(), calls=%async_computation.2 | async-start | bytes 3932160 | tf_op jit(solution)/shard_map/all_gather | solution.py:725
  94.2 32.1 %collective-permute-start.16 = (bf16[240,1280]{1,0:T(8,128)(2,1)}, bf16[240,1280]{1,0:T(8,128)(2,1)}, u32[]{:S(2)}, u32[]{:S(2)}) collective-permute-start(bf16[240,1280]{1,0:T(8,128)(2,1)} %get-tuple-element.114), channel_id=1, source_target_pairs={{0,3},{1,0},{2,1},{3,2},{4,7},{5,4},{6,5},{7,6},{8,11},{9,8},{10,9... | collective-permute-start | bytes 1843208 | tf_op jit(solution)/shard_map/ppermute | solution.py:579
  98.6 30.2 %collective-permute-start.14 = (bf16[240,1280]{1,0:T(8,128)(2,1)}, bf16[240,1280]{1,0:T(8,128)(2,1)}, u32[]{:S(2)}, u32[]{:S(2)}) collective-permute-start(bf16[240,1280]{1,0:T(8,128)(2,1)} %get-tuple-element.113), channel_id=1, source_target_pairs={{0,1},{1,2},{2,3},{3,0},{4,5},{5,6},{6,7},{7,4},{8,9},{9,10},{10,1... | collective-permute-start | bytes 1843208 | tf_op jit(solution)/shard_map/ppermute | solution.py:579
  100.4 28.5 %collective-permute-start.15 = (bf16[240,1280]{1,0:T(8,128)(2,1)}, bf16[240,1280]{1,0:T(8,128)(2,1)}, u32[]{:S(2)}, u32[]{:S(2)}) collective-permute-start(bf16[240,1280]{1,0:T(8,128)(2,1)} %shard_map.207), channel_id=1, source_target_pairs={{0,2},{1,3},{2,0},{3,1},{4,6},{5,7},{6,4},{7,5},{8,10},{9,11},{10,... | collective-permute-start | bytes 1843208 | tf_op jit(solution)/shard_map/ppermute | solution.py:579
  132.6 30.0 %collective-permute-start.24 = (bf16[960,1376]{1,0:T(8,128)(2,1)}, bf16[960,1376]{1,0:T(8,128)(2,1)}, u32[]{:S(2)}, u32[]{:S(2)}) collective-permute-start(bf16[960,1376]{1,0:T(8,128)(2,1)} %all-gather.9.cloned.1.call-done.refs_7_.refs_6_.refs_8_.refs_10_), channel_id=1, source_target_pairs={{0,64},{64,0},{1,65},{65,1},{2,66},{66,2},{3,67},{67,3},{4,68},{68... | collective-permute-start | bytes 7925768 | tf_op jit(solution)/shard_map/ppermute | solution.py:601
  175.2 146.0 %all-gather.13.cloned.1.call-start = ((), (), s32[]{:S(2)}) async-start(), calls=%async_computation.3 | async-start | bytes 2621440 | tf_op jit(solution)/shard_map/all_gather | solution.py:797
  222.7 29.0 %collective-permute-start.35 = (bf16[128,960]{1,0:T(8,128)(2,1)}, bf16[128,960]{1,0:T(8,128)(2,1)}, u32[]{:S(2)}, u32[]{:S(2)}) collective-permute-start(bf16[128,960]{1,0:T(8,128)(2,1)} %get-tuple-element.125.refs_1_), channel_id=1, source_target_pairs={{0,3},{1,0},{2,1},{3,2},{4,7},{5,4},{6,5},{7,6},{8,11},{9,8},{10,9... | collective-permute-start | bytes 737288 | tf_op jit(solution)/shard_map/ppermute | solution.py:579
  223.3 22.8 %collective-permute-start.33 = (bf16[128,960]{1,0:T(8,128)(2,1)}, bf16[128,960]{1,0:T(8,128)(2,1)}, u32[]{:S(2)}, u32[]{:S(2)}) collective-permute-start(bf16[128,960]{1,0:T(8,128)(2,1)} %get-tuple-element.125.refs_1_), channel_id=1, source_target_pairs={{0,2},{1,3},{2,0},{3,1},{4,6},{5,7},{6,4},{7,5},{8,10},{9,11},{10,... | collective-permute-start | bytes 737288 | tf_op jit(solution)/shard_map/ppermute | solution.py:579
  243.4 23.2 %collective-permute-start.38 = (bf16[128,960]{1,0:T(8,128)(2,1)}, bf16[128,960]{1,0:T(8,128)(2,1)}, u32[]{:S(2)}, u32[]{:S(2)}) collective-permute-start(bf16[128,960]{1,0:T(8,128)(2,1)} %get-tuple-element.132), channel_id=1, source_target_pairs={{0,3},{1,0},{2,1},{3,2},{4,7},{5,4},{6,5},{7,6},{8,11},{9,8},{10,9... | collective-permute-start | bytes 737288 | tf_op jit(solution)/shard_map/ppermute | solution.py:579
  341.8 50.1 %collective-permute-start.61 = (bf16[16,96,640]{2,1,0:T(8,128)(2,1)S(1)}, bf16[16,96,640]{2,1,0:T(8,128)(2,1)S(1)}, u32[]{:S(2)}, u32[]{:S(2)}) collective-permute-start(bf16[16,96,640]{2,1,0:T(8,128)(2,1)S(1)} %copy-done.64), channel_id=1, source_target_pairs={{0,64},{64,0},{1,65},{65,1},{2,66},{66,2},{3,67},{67,3},{4,68},{68... | collective-permute-start | bytes 5898248 | tf_op jit(solution)/shard_map/ppermute | solution.py:601
  367.8 43.8 %collective-permute-start.60 = (bf16[16,96,640]{2,1,0:T(8,128)(2,1)}, bf16[16,96,640]{2,1,0:T(8,128)(2,1)}, u32[]{:S(2)}, u32[]{:S(2)}) collective-permute-start(bf16[16,96,640]{2,1,0:T(8,128)(2,1)} %get-tuple-element.183), channel_id=1, source_target_pairs={{0,64},{64,0},{1,65},{65,1},{2,66},{66,2},{3,67},{67,3},{4,68},{68... | collective-permute-start | bytes 5898248 | tf_op jit(solution)/shard_map/ppermute | solution.py:601
  391.9 27.9 %collective-permute-start.36 = (bf16[128,960]{1,0:T(8,128)(2,1)}, bf16[128,960]{1,0:T(8,128)(2,1)}, u32[]{:S(2)}, u32[]{:S(2)}) collective-permute-start(bf16[128,960]{1,0:T(8,128)(2,1)} %get-tuple-element.130), channel_id=1, source_target_pairs={{0,1},{1,2},{2,3},{3,0},{4,5},{5,6},{6,7},{7,4},{8,9},{9,10},{10,1... | collective-permute-start | bytes 737288 | tf_op jit(solution)/shard_map/ppermute | solution.py:579
  398.3 24.1 %collective-permute-start.34 = (bf16[128,960]{1,0:T(8,128)(2,1)}, bf16[128,960]{1,0:T(8,128)(2,1)}, u32[]{:S(2)}, u32[]{:S(2)}) collective-permute-start(bf16[128,960]{1,0:T(8,128)(2,1)} %copy-done.66), channel_id=1, source_target_pairs={{0,2},{1,3},{2,0},{3,1},{4,6},{5,7},{6,4},{7,5},{8,10},{9,11},{10,... | collective-permute-start | bytes 737288 | tf_op jit(solution)/shard_map/ppermute | solution.py:579
  400.5 22.5 %collective-permute-start.32 = (bf16[128,960]{1,0:T(8,128)(2,1)}, bf16[128,960]{1,0:T(8,128)(2,1)}, u32[]{:S(2)}, u32[]{:S(2)}) collective-permute-start(bf16[128,960]{1,0:T(8,128)(2,1)} %copy-done.65), channel_id=1, source_target_pairs={{0,3},{1,0},{2,1},{3,2},{4,7},{5,4},{6,5},{7,6},{8,11},{9,8},{10,9... | collective-permute-start | bytes 737288 | tf_op jit(solution)/shard_map/ppermute | solution.py:579
  423.0 30.0 %collective-permute-start.64 = (bf16[4,192,640]{2,1,0:T(8,128)(2,1)S(1)}, bf16[4,192,640]{2,1,0:T(8,128)(2,1)S(1)}, u32[]{:S(2)}, u32[]{:S(2)}) collective-permute-start(bf16[4,192,640]{2,1,0:T(8,128)(2,1)S(1)} %get-tuple-element.265), channel_id=1, source_target_pairs={{0,48},{4,52},{8,56},{12,60},{16,0},{20,4},{24,8},{28,12},{32,16},... | collective-permute-start | bytes 2949128 | tf_op jit(solution)/shard_map/ppermute | solution.py:589
  423.6 29.5 %collective-permute-start.63 = (bf16[4,192,640]{2,1,0:T(8,128)(2,1)S(1)}, bf16[4,192,640]{2,1,0:T(8,128)(2,1)S(1)}, u32[]{:S(2)}, u32[]{:S(2)}) collective-permute-start(bf16[4,192,640]{2,1,0:T(8,128)(2,1)S(1)} %get-tuple-element.266), channel_id=1, source_target_pairs={{0,32},{4,36},{8,40},{12,44},{16,48},{20,52},{24,56},{28,60},{32,0... | collective-permute-start | bytes 2949128 | tf_op jit(solution)/shard_map/ppermute | solution.py:589
  426.7 28.3 %collective-permute-start.62 = (bf16[4,192,640]{2,1,0:T(8,128)(2,1)S(1)}, bf16[4,192,640]{2,1,0:T(8,128)(2,1)S(1)}, u32[]{:S(2)}, u32[]{:S(2)}) collective-permute-start(bf16[4,192,640]{2,1,0:T(8,128)(2,1)S(1)} %get-tuple-element.264), channel_id=1, source_target_pairs={{0,16},{4,20},{8,24},{12,28},{16,32},{20,36},{24,40},{28,44},{32,4... | collective-permute-start | bytes 2949128 | tf_op jit(solution)/shard_map/ppermute | solution.py:589
  446.5 22.6 %collective-permute-start.37 = (f32[128,960]{1,0:T(8,128)}, f32[128,960]{1,0:T(8,128)}, u32[]{:S(2)}, u32[]{:S(2)}) collective-permute-start(f32[128,960]{1,0:T(8,128)} %get-tuple-element.260), channel_id=1, source_target_pairs={{0,64},{64,0},{1,65},{65,1},{2,66},{66,2},{3,67},{67,3},{4,68},{68... | collective-permute-start | bytes 1474568 | tf_op jit(solution)/shard_map/ppermute | solution.py:601
  (211 other events, 1661.5 us)
Sparse Core Ops, SparseCore 0:
  16.0 38.2 all-gather.6
  64.9 37.3 all-gather.8
  175.3 37.5 all-gather.10
  266.8 31.4 all-gather.12
